TPU v7x, 32 devices: a whole 2x2x4 slice. The times are simulated.
32 devices in a mesh: dp: 16 (over z, y, x), tensor: 2 (over core).
Axes of the slice: x: 2, y: 2, z: 4, core: 2. Of those that a mesh axis runs over, the one named last changes fastest.
Arguments:
- tokens: bfloat16 [2048, 2048], P('dp'), may hold values from -6 to 6
- cotangent: bfloat16 [2048, 2048], P('dp'), may hold values from -6 to 6
- expert_ids: int32 [2048, 4], P('dp'), may hold values from 0 to 15, all different within a row; in each aligned block of 128 rows (0 to 127, 128 to 255, ...) at most 40 rows name the same one
- route_weight: float32 [2048, 4], P('dp'), may hold values from 0.05 to 1
- forget_mask: int32 [2048], P('dp'), may hold values from 0 to 1, as said below
- lengths: int32 [2], replicated, may hold values from 256 to 1024, as said below
- gate_weight: bfloat16 [16, 1024, 2048], P('dp', 'tensor'), may hold values from -0.125 to 0.125
- up_weight: bfloat16 [16, 1024, 2048], P('dp', 'tensor'), may hold values from -0.125 to 0.125
- down_weight: bfloat16 [16, 1024, 2048], P('dp', 'tensor'), may hold values from -0.1875 to 0.1875
Outputs:
- mixed_out: bfloat16 [2048, 2048], P('dp', 'tensor')
- grad_gate: bfloat16 [16, 1024, 2048], P('dp', 'tensor')
- grad_up: bfloat16 [16, 1024, 2048], P('dp', 'tensor')
- grad_down: bfloat16 [16, 1024, 2048], P('dp', 'tensor')
Inputs may be any that keep to these rules, and one draw needn't show every extreme that they name: `expert_ids`: among the rows of one index of dp (aligned blocks of 128 tokens), no expert is named more than 40 times. `forget_mask`: the first token slot of every sequence is 0 and the second is 1. `lengths`: at least one sequence uses all 1024 slots.
All inputs are finite; a program needn't handle non-finite values.
Results may differ from a plain program's by a relative error of at most 0.019.
Values may be sent and summed in bfloat16 or wider, within the bound.
No kernel may reach another device: no remote copies, remote signals or barrier semaphores. Data moves between devices by JAX's collectives and lax.ppermute only.
A program may use at most 128 MiB of HBM per device.

v0:
```python
import jax
import jax.numpy as jnp
from jax import lax
from jax.sharding import PartitionSpec as P


def body(
    tokens,
    cotangent,
    expert_ids,
    route_weight,
    forget_mask,
    lengths,
    gate_weight,
    up_weight,
    down_weight,
):
    tok_rows = tokens.shape[0]
    features = tokens.shape[1]
    top_count = expert_ids.shape[1]
    owners = lax.axis_size("dp")
    capacity = 5 * tok_rows * top_count // (4 * owners)
    seq_count = lengths.shape[0]
    seq_len = tok_rows * owners // seq_count
    token_index = lax.axis_index("dp") * tok_rows + jnp.arange(tok_rows, dtype=jnp.int32)
    seq_id = token_index // seq_len
    seq_pos = token_index - seq_id * seq_len
    in_seq = seq_id[:, None] == jnp.arange(seq_count, dtype=jnp.int32)[None, :]
    limits = jnp.sum(jnp.where(in_seq, lengths[None, :], 0), axis=1)
    is_valid = (seq_pos < limits).astype(jnp.int32)
    forget = is_valid * forget_mask
    retain = is_valid - forget
    n_forget, n_retain = lax.psum((jnp.sum(forget), jnp.sum(retain)), "dp")
    coefficient = float(top_count * tok_rows) * (
        retain.astype(jnp.float32) / n_retain.astype(jnp.float32)
        - forget.astype(jnp.float32) / n_forget.astype(jnp.float32)
    )
    shares = route_weight / jnp.sum(route_weight, axis=1, keepdims=True)
    share_flat = shares.reshape(-1)
    assigned = tok_rows * top_count
    flat_ids = expert_ids.reshape(-1)
    one_hot = (flat_ids[:, None] == jnp.arange(owners, dtype=jnp.int32)[None, :]).astype(jnp.int32)
    before = jnp.cumsum(one_hot, axis=0) - one_hot
    slot_id = jnp.sum(before * one_hot, axis=1)
    target = flat_ids * capacity + slot_id
    slots_all = owners * capacity
    source = (
        jnp.full((slots_all,), assigned, jnp.int32)
        .at[target]
        .set(jnp.arange(assigned, dtype=jnp.int32))
    )
    is_live = source < assigned
    source_row = jnp.minimum(source, assigned - 1)
    source_tok = source_row // top_count
    send_rows = jnp.where(
        is_live[:, None], tokens[source_tok], jnp.zeros((), tokens.dtype)
    ).reshape(owners, capacity, features)
    slot_weight = jnp.where(is_live, coefficient[source_tok] * share_flat[source_row], 0.0)
    send_cotan = (
        (slot_weight[:, None] * cotangent[source_tok].astype(jnp.float32))
        .astype(jnp.bfloat16)
        .reshape(owners, capacity, features)
    )
    recv_rows, recv_cotan = (
        lax.all_to_all(send_rows, "dp", split_axis=0, concat_axis=0, tiled=True),
        lax.all_to_all(send_cotan, "dp", split_axis=0, concat_axis=0, tiled=True),
    )
    rows_in = recv_rows.reshape(slots_all, features)
    contract_last = (((1,), (1,)), ((), ()))
    contract_first = (((0,), (0,)), ((), ()))
    gate_pre = lax.dot_general(
        gate_weight[0], rows_in, contract_last, preferred_element_type=jnp.float32
    )
    up_pre = lax.dot_general(
        up_weight[0], rows_in, contract_last, preferred_element_type=jnp.float32
    )
    sigmoid_gate = jax.nn.sigmoid(gate_pre)
    hidden = (gate_pre * sigmoid_gate * up_pre).astype(jnp.bfloat16)
    partial_out = lax.dot_general(
        hidden, down_weight[0], contract_first, preferred_element_type=jnp.float32
    )
    returned = lax.all_to_all(
        partial_out.astype(jnp.bfloat16).reshape(owners, capacity, features),
        "dp",
        split_axis=0,
        concat_axis=0,
        tiled=True,
    )
    picked = returned.reshape(slots_all, features)[target].astype(jnp.float32) * share_flat[:, None]
    token_terms = jnp.sum(picked.reshape(tok_rows, top_count, features), axis=1)
    mixed_out = lax.psum_scatter(
        token_terms.astype(jnp.bfloat16), "tensor", scatter_dimension=1, tiled=True
    )
    routed = recv_cotan.reshape(slots_all, features)
    grad_down = jnp.dot(hidden, routed, preferred_element_type=jnp.float32)
    dhidden = lax.dot_general(
        down_weight[0], routed, contract_last, preferred_element_type=jnp.float32
    )
    dgate = (dhidden * up_pre * sigmoid_gate * (1.0 + gate_pre * (1.0 - sigmoid_gate))).astype(
        jnp.bfloat16
    )
    dup = (dhidden * gate_pre * sigmoid_gate).astype(jnp.bfloat16)
    grad_gate = jnp.dot(dgate, rows_in, preferred_element_type=jnp.float32)
    grad_up = jnp.dot(dup, rows_in, preferred_element_type=jnp.float32)
    return (
        mixed_out,
        grad_gate.astype(jnp.bfloat16)[None],
        grad_up.astype(jnp.bfloat16)[None],
        grad_down.astype(jnp.bfloat16)[None],
    )


def solution(mesh):
    in_specs = (
        P("dp", None),
        P("dp", None),
        P("dp", None),
        P("dp", None),
        P("dp"),
        P(),
        P("dp", "tensor", None),
        P("dp", "tensor", None),
        P("dp", "tensor", None),
    )
    out_specs = (
        P("dp", "tensor"),
        P("dp", "tensor", None),
        P("dp", "tensor", None),
        P("dp", "tensor", None),
    )
    return jax.shard_map(body, mesh=mesh, in_specs=in_specs, out_specs=out_specs, check_vma=False)
```

profile of v0, /device:TPU:12, one launch (start us, length us, event | category | flops | bytes accessed | tf_op | source)
XLA Modules:
  0.0 279.1 jit_solution(17082358962301851433)
XLA Ops:
  7.2 0.0 copy-start
  7.2 0.8 broadcast_multiply_fusion
  8.0 0.8 copy.21
  8.8 0.1 eq.42
  8.9 0.1 eq.38
  9.0 0.7 fusion.30
  9.8 1.3 fusion.32
  11.1 13.2 %all-reduce = (s32[]{:T(128)}, s32[]{:T(128)}) all-reduce(s32[]{:T(128)} %get-tuple-element.5, s32[]{:T(128)} %get-tuple-element.4), channel_id=1, replica_groups=mesh['dp'=16,'tensor'=2] {'dp'}, use_global_device_ids=true, to_apply=%region_11.12 | all-reduce | flops 2 | bytes 16 | tf_op jit(solution)/shard_map/psum | solution.py:33
  25.6 0.7 reduce_sum.58
  26.3 0.7 broadcast_divide_fusion
  27.0 0.1 copy.24
  27.1 0.1 reshape.122
  27.2 0.1 copy.20
  27.3 0.1 mul.84
  27.5 1.2 reduce-window.6
  28.6 0.2 slice_reduce_fusion
  28.9 0.1 fusion.24
  29.0 2.4 scatter_custom_fusion
  31.5 0.0 copy-start.3
  31.5 4.3 %gather_fusion.3 = f32[640]{0:T(1024)S(1)} fusion(f32[512]{0:T(512)S(1)} %reshape.122, s32[1024]{0:T(1024)S(1)} %get-tuple-element.15), kind=kCustom, calls=%fused_computation.3 | custom fusion | bytes 7680 | tf_op jit(solution)/shard_map/gather | solution.py:58
  35.8 0.0 copy-done.3
  35.8 0.0 copy-start.1
  35.9 4.1 %gather_fusion.2 = f32[640]{0:T(1024)S(1)} fusion(f32[128]{0:T(128)S(1)} %fusion.31, s32[1024]{0:T(1024)S(1)} %get-tuple-element.16), kind=kCustom, calls=%fused_computation.2 | custom fusion | bytes 7680 | tf_op jit(solution)/shard_map/gather | solution.py:58
  40.0 0.1 broadcast_in_dim.56
  40.1 0.0 copy-done.1
  40.1 4.1 %gather_fusion = bf16[640,2048]{1,0:T(8,128)(2,1)} fusion(bf16[128,2048]{1,0:T(8,128)(2,1)S(1)} %copy-done.1, s32[1024]{0:T(1024)S(1)} %get-tuple-element.16), kind=kCustom, calls=%fused_computation | custom fusion | bytes 5245440 | tf_op jit(solution)/shard_map/gather | solution.py:56
  44.2 3.5 %broadcast_select_fusion = bf16[16,40,2048]{2,1,0:T(8,128)(2,1)} fusion(bf16[16,40,2048]{2,1,0:T(8,128)(2,1)} %bitcast.69, pred[16,40]{1,0:T(8,128)(4,1)S(1)} %broadcast_in_dim.56), kind=kLoop, calls=%fused_computation.16 | loop fusion | flops 1310720 | bytes 5243520 | tf_op jit(solution)/shard_map/jit(_where)/select_n | solution.py:55
  47.7 0.0 copy-start.2
  47.7 6.9 %all-to-all-start = ((bf16[16,40,2048]{2,1,0:T(8,128)(2,1)}), bf16[16,40,2048]{2,1,0:T(8,128)(2,1)}, u32[]{:S(2)}, u32[]{:S(2)}) async-start(bf16[16,40,2048]{2,1,0:T(8,128)(2,1)} %broadcast_select_fusion), calls=%async_computation | async-start | bytes 5242880 | tf_op jit(solution)/shard_map/all_to_all | solution.py:65
  54.6 0.1 mul.96
  54.7 0.0 copy-done.2
  54.7 4.1 %gather_fusion.4 = bf16[640,2048]{1,0:T(8,128)(2,1)} fusion(bf16[128,2048]{1,0:T(8,128)(2,1)S(1)} %copy-done.2, s32[1024]{0:T(1024)S(1)} %get-tuple-element.16), kind=kCustom, calls=%fused_computation.4 | custom fusion | bytes 5245440 | tf_op jit(solution)/shard_map/gather | solution.py:60
  58.7 3.8 %fusion = bf16[16,40,2048]{2,1,0:T(8,128)(2,1)} fusion(bf16[16,40,2048]{2,1,0:T(8,128)(2,1)} %bitcast.68, f32[16,40]{1,0:T(8,128)S(1)} %mul.96), kind=kLoop, calls=%fused_computation.7 | loop fusion | flops 3932160 | bytes 5245440 | tf_op jit(solution)/shard_map/convert_element_type | solution.py:61
  62.5 48.2 %all-to-all-done = bf16[16,40,2048]{2,1,0:T(8,128)(2,1)} async-done(((bf16[16,40,2048]{2,1,0:T(8,128)(2,1)}), bf16[16,40,2048]{2,1,0:T(8,128)(2,1)}, u32[]{:S(2)}, u32[]{:S(2)}) %all-to-all-start) | async-done | bytes 2621472 | tf_op jit(solution)/shard_map/all_to_all | solution.py:65
  110.7 5.2 %all-to-all-start.2 = ((bf16[16,40,2048]{2,1,0:T(8,128)(2,1)}), bf16[16,40,2048]{2,1,0:T(8,128)(2,1)}, u32[]{:S(2)}, u32[]{:S(2)}) async-start(bf16[16,40,2048]{2,1,0:T(8,128)(2,1)} %fusion), calls=%async_computation.3 | async-start | bytes 5242880 | tf_op jit(solution)/shard_map/all_to_all | solution.py:66
  115.9 0.0 copy-start.4
  115.9 4.1 %fusion.11 = f32[512,640]{0,1:T(8,128)S(1)} fusion(bf16[640,2048]{1,0:T(8,128)(2,1)} %bitcast.4, bf16[1,512,2048]{2,1,0:T(8,128)(2,1)} %param.15), kind=kOutput, calls=%fused_computation.24 | convolution fusion | flops 1342177280 | bytes 6029312 | tf_op jit(solution)/shard_map/dot_general | solution.py:71
  120.0 0.0 copy-done.4
  120.0 0.0 copy-start.5
  120.0 4.9 %multiply_convert_fusion.2 = (bf16[512,640]{0,1:T(8,128)(2,1)S(1)}, f32[512,640]{0,1:T(8,128)}) fusion(f32[512,640]{0,1:T(8,128)S(1)} %fusion.11, bf16[640,2048]{1,0:T(8,128)(2,1)} %bitcast.4, bf16[1,512,2048]{2,1,0:T(8,128)(2,1)S(1)} %copy-done.4), kind=kOutput, calls=%fused_computation.29 | convolution fusion | flops 1344143360 | bytes 7995392 | tf_op jit(solution)/shard_map/dot_general | solution.py:74
  124.9 0.0 copy-done.5
  124.9 0.0 copy-done
  124.9 3.0 %convolution_convert_fusion = bf16[640,2048]{1,0:T(8,128)(2,1)} fusion(bf16[512,640]{0,1:T(8,128)(2,1)S(1)} %get-tuple-element.13, bf16[1,512,2048]{2,1,0:T(8,128)(2,1)S(1)} %copy-done), kind=kOutput, calls=%fused_computation.9 | convolution fusion | flops 1343488000 | bytes 5373952 | tf_op jit(solution)/shard_map/dot_general | solution.py:79
  128.0 46.1 %all-to-all-done.2 = bf16[16,40,2048]{2,1,0:T(8,128)(2,1)} async-done(((bf16[16,40,2048]{2,1,0:T(8,128)(2,1)}), bf16[16,40,2048]{2,1,0:T(8,128)(2,1)}, u32[]{:S(2)}, u32[]{:S(2)}) %all-to-all-start.2) | async-done | bytes 2621472 | tf_op jit(solution)/shard_map/all_to_all | solution.py:66
  174.1 4.8 %all-to-all-start.1 = ((bf16[16,40,2048]{2,1,0:T(8,128)(2,1)}), bf16[16,40,2048]{2,1,0:T(8,128)(2,1)}, u32[]{:S(2)}, u32[]{:S(2)}) async-start(bf16[16,40,2048]{2,1,0:T(8,128)(2,1)} %bitcast.70), calls=%async_computation.1 | async-start | bytes 5242880 | tf_op jit(solution)/shard_map/all_to_all | solution.py:82
  178.9 0.0 reduce-scatter.2.cloned.1.call-start
  178.9 4.4 %fusion.17 = f32[512,640]{0,1:T(8,128)} fusion(bf16[640,2048]{1,0:T(8,128)(2,1)} %bitcast.13, bf16[1,512,2048]{2,1,0:T(8,128)(2,1)S(1)} %copy-done), kind=kOutput, calls=%fused_computation.26 | convolution fusion | flops 1342177280 | bytes 6029312 | tf_op jit(solution)/shard_map/dot_general | solution.py:96
  183.3 54.3 %all-to-all-done.1 = bf16[16,40,2048]{2,1,0:T(8,128)(2,1)} async-done(((bf16[16,40,2048]{2,1,0:T(8,128)(2,1)}), bf16[16,40,2048]{2,1,0:T(8,128)(2,1)}, u32[]{:S(2)}, u32[]{:S(2)}) %all-to-all-start.1) | async-done | bytes 2621472 | tf_op jit(solution)/shard_map/all_to_all | solution.py:82
  237.6 7.5 %gather_fusion.1 = bf16[512,2048]{1,0:T(8,128)(2,1)} fusion(bf16[640,2048]{1,0:T(8,128)(2,1)} %bitcast.11, s32[1024]{0:T(1024)S(1)} %pad_clamp_fusion.1), kind=kCustom, calls=%fused_computation.1 | custom fusion | bytes 4196352 | tf_op jit(solution)/shard_map/gather | solution.py:89
  245.1 4.8 %reshape.124 = f32[128,4,2048]{2,1,0:T(4,128)} reshape(bf16[512,2048]{1,0:T(8,128)(2,1)} %gather_fusion.1) | data formatting | bytes 6291456 | tf_op jit(solution)/shard_map/convert_element_type | solution.py:89
  249.9 6.2 %multiply_reduce_fusion = bf16[128,2048]{1,0:T(8,128)(2,1)} fusion(f32[128,4,2048]{2,1,0:T(4,128)} %reshape.124, f32[128,4]{1,0:T(8,128)S(1)} %copy.24), kind=kLoop, calls=%fused_computation.8 | loop fusion | flops 1835008 | bytes 4720640 | tf_op jit(solution)/shard_map/reduce_sum | solution.py:90
  256.1 0.0 reduce-scatter.2.cloned.1.call-update
  256.1 5.7 %fusion.2 = bf16[1,512,2048]{2,1,0:T(8,128)(2,1)} fusion(bf16[640,2048]{1,0:T(8,128)(2,1)} %bitcast.4, f32[512,640]{0,1:T(8,128)} %fusion.17, f32[512,640]{0,1:T(8,128)} %copy-done.5), kind=kOutput, calls=%fused_computation.14 | convolution fusion | flops 1345191936 | bytes 7340032 | tf_op jit(solution)/shard_map/dot_general | solution.py:104
  261.9 0.0 copy-start.6
  261.9 0.0 copy-start.7
  261.9 0.0 copy-start.8
  261.9 5.1 %fusion.3 = bf16[1,512,2048]{2,1,0:T(8,128)(2,1)} fusion(bf16[512,640]{0,1:T(8,128)(2,1)S(1)} %get-tuple-element.13, bf16[640,2048]{1,0:T(8,128)(2,1)} %bitcast.13), kind=kOutput, calls=%fused_computation.15 | convolution fusion | flops 1343225856 | bytes 5373952 | tf_op jit(solution)/shard_map/dot_general | solution.py:95
  267.0 0.0 copy-done.6
  267.0 0.0 copy-done.7
  267.0 0.0 copy-done.8
  267.0 5.2 %fusion.1 = bf16[1,512,2048]{2,1,0:T(8,128)(2,1)} fusion(bf16[640,2048]{1,0:T(8,128)(2,1)} %bitcast.4, f32[512,640]{0,1:T(8,128)S(1)} %copy-done.6, f32[512,640]{0,1:T(8,128)S(1)} %copy-done.8, f32[512,640]{0,1:T(8,128)S(1)} %copy-done.7), kind=kOutput, calls=%fused_computation.13 | convolution fusion | flops 1346502656 | bytes 8650752 | tf_op jit(solution)/shard_map/dot_general | solution.py:103
  272.2 0.0 reduce-scatter.2.cloned.1.call-done
  (11 shorter events, 0.1 us)
Async XLA Ops:
  7.2 117.8 %copy-start = (bf16[1,512,2048]{2,1,0:T(8,128)(2,1)S(1)}, bf16[1,512,2048]{2,1,0:T(8,128)(2,1)}, u32[]{:S(2)}) copy-start(bf16[1,512,2048]{2,1,0:T(8,128)(2,1)} %param.17) | copy-start | bytes 6291460
  31.5 4.3 %copy-start.3 = (s32[128]{0:T(128)S(1)}, s32[128]{0:T(128)}, u32[]{:S(2)}) copy-start(s32[128]{0:T(128)} %param.13) | copy-start | bytes 1540
  35.8 4.3 %copy-start.1 = (bf16[128,2048]{1,0:T(8,128)(2,1)S(1)}, bf16[128,2048]{1,0:T(8,128)(2,1)}, u32[]{:S(2)}) copy-start(bf16[128,2048]{1,0:T(8,128)(2,1)} %param.9) | copy-start | bytes 1572868
  47.7 7.0 %copy-start.2 = (bf16[128,2048]{1,0:T(8,128)(2,1)S(1)}, bf16[128,2048]{1,0:T(8,128)(2,1)}, u32[]{:S(2)}) copy-start(bf16[128,2048]{1,0:T(8,128)(2,1)} %param.10) | copy-start | bytes 1572868
  47.7 63.0 %all-to-all-start = ((bf16[16,40,2048]{2,1,0:T(8,128)(2,1)}), bf16[16,40,2048]{2,1,0:T(8,128)(2,1)}, u32[]{:S(2)}, u32[]{:S(2)}) async-start(bf16[16,40,2048]{2,1,0:T(8,128)(2,1)} %broadcast_select_fusion), calls=%async_computation | async-start | bytes 5242880 | tf_op jit(solution)/shard_map/all_to_all | solution.py:65
  110.7 63.4 %all-to-all-start.2 = ((bf16[16,40,2048]{2,1,0:T(8,128)(2,1)}), bf16[16,40,2048]{2,1,0:T(8,128)(2,1)}, u32[]{:S(2)}, u32[]{:S(2)}) async-start(bf16[16,40,2048]{2,1,0:T(8,128)(2,1)} %fusion), calls=%async_computation.3 | async-start | bytes 5242880 | tf_op jit(solution)/shard_map/all_to_all | solution.py:66
  115.9 4.1 %copy-start.4 = (bf16[1,512,2048]{2,1,0:T(8,128)(2,1)S(1)}, bf16[1,512,2048]{2,1,0:T(8,128)(2,1)}, u32[]{:S(2)}) copy-start(bf16[1,512,2048]{2,1,0:T(8,128)(2,1)} %param.16) | copy-start | bytes 6291460
  120.0 4.9 %copy-start.5 = (f32[512,640]{0,1:T(8,128)}, f32[512,640]{0,1:T(8,128)S(1)}, u32[]{:S(2)}) copy-start(f32[512,640]{0,1:T(8,128)S(1)} %fusion.11) | copy-start | bytes 3932164
  174.1 63.5 %all-to-all-start.1 = ((bf16[16,40,2048]{2,1,0:T(8,128)(2,1)}), bf16[16,40,2048]{2,1,0:T(8,128)(2,1)}, u32[]{:S(2)}, u32[]{:S(2)}) async-start(bf16[16,40,2048]{2,1,0:T(8,128)(2,1)} %bitcast.70), calls=%async_computation.1 | async-start | bytes 5242880 | tf_op jit(solution)/shard_map/all_to_all | solution.py:82
  178.9 93.4 %reduce-scatter.2.cloned.1.call-start = ((), (), s32[]{:S(2)}) async-start(), calls=%async_computation.4 | async-start | bytes 786432 | tf_op jit(solution)/shard_map/reduce_scatter | solution.py:91
  261.9 5.1 %copy-start.6 = (f32[512,640]{0,1:T(8,128)S(1)}, f32[512,640]{0,1:T(8,128)}, u32[]{:S(2)}) copy-start(f32[512,640]{0,1:T(8,128)} %copy-done.5) | copy-start | bytes 3932164
  261.9 5.1 %copy-start.7 = (f32[512,640]{0,1:T(8,128)S(1)}, f32[512,640]{0,1:T(8,128)}, u32[]{:S(2)}) copy-start(f32[512,640]{0,1:T(8,128)} %get-tuple-element.14) | copy-start | bytes 3932164
  261.9 5.1 %copy-start.8 = (f32[512,640]{0,1:T(8,128)S(1)}, f32[512,640]{0,1:T(8,128)}, u32[]{:S(2)}) copy-start(f32[512,640]{0,1:T(8,128)} %fusion.17) | copy-start | bytes 3932164
Sparse Core Ops, SparseCore 0:
  256.2 6.9 reduce-scatter.1
where the time goes:
time: 280 us; the launch traced here: 279 us
  waiting for transfers between devices  149 us (53%)
  local copies, waits for them, and re-layouts  33.2 us (12%)
  matrix products  32.4 us (12%)
  other arithmetic  19.1 us (7%)
  starting transfers between devices  16.9 us (6%)
  between operations  15.5 us (6%)
  blocking collectives  13.2 us (5%)
    all_to_all x1, waiting for transfers between devices, body(): lax.all_to_all(partial_out.astype(jnp.bfloat16).reshape(owners, capacity,...  54.3 us
    all_to_all x1, waiting for transfers between devices, body(): lax.all_to_all(send_rows, 'dp', split_axis=0, concat_axis=0, tiled=True)  48.2 us
    all_to_all x1, waiting for transfers between devices, body(): lax.all_to_all(send_cotan, 'dp', split_axis=0, concat_axis=0, tiled=True)  46.1 us
    psum x1, blocking collectives, body(): n_forget, n_retain = lax.psum((jnp.sum(forget), jnp.sum(retain)), 'dp')  13.2 us
    gather x1, local copies, waits for them, and re-layouts, body(): returned.reshape(slots_all, features)[target].astype(jnp.float32)  7.48 us
    all_to_all x1, starting transfers between devices, body(): lax.all_to_all(send_rows, 'dp', split_axis=0, concat_axis=0, tiled=True)  6.87 us
    reduce_sum x1, other arithmetic, body(): token_terms = jnp.sum(picked.reshape(tok_rows, top_count, features), axis=1)  6.22 us
    dot_general x1, matrix products, body(): grad_up = jnp.dot(dup, rows_in, preferred_element_type=jnp.float32)  5.75 us
  transfers between devices with their start and end apart: 4, of which 3 were waited for; matrix products, arithmetic and copies ran while one was open for 14% of the time, Pallas kernels for 0%

commit v1 on v0

v1 whole, which is shorter than its diff:
```python
import jax
import jax.numpy as jnp
from jax import lax
from jax.sharding import PartitionSpec as P

F32 = jnp.float32
BF16 = jnp.bfloat16
META = 128


def dot(a, b, dims):
    return lax.dot_general(a, b, (dims, ((), ())), preferred_element_type=F32)


def body(
    tokens,
    cotangent,
    expert_ids,
    route_weight,
    forget_mask,
    lengths,
    gate_weight,
    up_weight,
    down_weight,
):
    tok_rows, features = tokens.shape
    top_count = expert_ids.shape[1]
    owners = lax.axis_size("dp")
    parts = lax.axis_size("tensor")
    half = owners // 2
    width = features // parts
    capacity = 5 * tok_rows * top_count // (4 * owners)
    slots = half * capacity
    me = lax.axis_index("dp")
    core = lax.axis_index("tensor")
    mates = [(i, (i + half) % owners) for i in range(owners)]
    halves = [list(range(half)), list(range(half, owners))]

    def to_mate(value):
        return lax.ppermute(value, "dp", mates)

    def exchange(value):
        return lax.all_to_all(
            value, "dp", split_axis=0, concat_axis=0, axis_index_groups=halves, tiled=True
        )

    def whole_rows(mine):
        if parts != 2:
            return lax.all_gather(mine, "tensor", axis=1, tiled=True)
        other = lax.ppermute(mine, "tensor", [(0, 1), (1, 0)])
        return jnp.where(
            core == 0,
            jnp.concatenate([mine, other], axis=1),
            jnp.concatenate([other, mine], axis=1),
        )

    def sum_rows(partial):
        if parts != 2:
            return lax.psum_scatter(partial, "tensor", scatter_dimension=1, tiled=True)
        low, high = partial[:, :width], partial[:, width:]
        other = lax.ppermute(jnp.where(core == 0, high, low), "tensor", [(0, 1), (1, 0)])
        mine = jnp.where(core == 0, low, high)
        return (mine.astype(F32) + other.astype(F32)).astype(BF16)

    def my_features(value):
        return lax.dynamic_slice_in_dim(value, core * width, width, axis=1)

    seq_count = lengths.shape[0]
    seq_len = tok_rows * owners // seq_count
    token_index = me * tok_rows + jnp.arange(tok_rows, dtype=jnp.int32)
    seq_id = token_index // seq_len
    seq_pos = token_index - seq_id * seq_len
    in_seq = seq_id[:, None] == jnp.arange(seq_count, dtype=jnp.int32)[None, :]
    limits = jnp.sum(jnp.where(in_seq, lengths[None, :], 0), axis=1)
    is_valid = (seq_pos < limits).astype(jnp.int32)
    forget = is_valid * forget_mask
    retain = is_valid - forget
    shares = route_weight / jnp.sum(route_weight, axis=1, keepdims=True)
    about = jnp.concatenate(
        [
            expert_ids.astype(F32).T,
            shares.T,
            retain.astype(F32)[None, :],
            forget.astype(F32)[None, :],
        ],
        axis=0,
    )
    about_mate = to_mate(about)
    tok_mine = my_features(tokens)
    tok_mate = to_mate(tok_mine)

    first = (me // half) * half
    expert = (first + jnp.arange(half, dtype=jnp.int32)).astype(F32)
    place = jnp.arange(tok_rows, dtype=jnp.int32)
    earlier = (place[:, None] < place[None, :]).astype(BF16)

    def slot_tables(info):
        hit = info[None, :top_count, :] == expert[:, None, None]
        named = jnp.any(hit, axis=1)
        weight = jnp.sum(jnp.where(hit, info[None, top_count : 2 * top_count, :], 0.0), axis=1)
        rank = dot(named.astype(BF16), earlier, ((1,), (0,)))
        rank = jnp.where(named, rank, -1.0)
        at_slot = rank[:, None, :] == jnp.arange(capacity, dtype=jnp.int32).astype(F32)[None, :, None]
        pick = at_slot.astype(BF16).reshape(slots, tok_rows)
        spread = jnp.where(at_slot, weight[:, None, :], 0.0).astype(BF16).reshape(slots, tok_rows)
        return pick, spread

    def split3(value):
        high = lax.reduce_precision(value, 8, 7)
        rest = value - high
        middle = lax.reduce_precision(rest, 8, 7)
        return [high, middle, rest - middle]

    def columns(info):
        share = info[top_count : 2 * top_count]
        rows = jnp.concatenate(
            [info[:top_count]] + split3(share) + [info[2 * top_count : 2 * top_count + 2]], axis=0
        )
        rows = jnp.pad(rows, ((0, META - rows.shape[0]), (0, 0)))
        return rows.T.astype(BF16)

    pick_own, spread_own = slot_tables(about)
    send_own = dot(pick_own, tok_mine, ((1,), (0,))).astype(BF16)
    recv_own = exchange(send_own.reshape(half, capacity, width)).reshape(slots, width)
    pick_mate, spread_mate = slot_tables(about_mate)
    send_mate = dot(pick_mate, tok_mate, ((1,), (0,))).astype(BF16)
    recv_mate = exchange(send_mate.reshape(half, capacity, width)).reshape(slots, width)

    cot_mine = my_features(cotangent)
    cot_mate = to_mate(cot_mine)
    count_at = 4 * top_count + 2
    counts = jnp.sum(about[2 * top_count :] + about_mate[2 * top_count :], axis=1)
    count_row = jnp.zeros((META,), F32).at[count_at].set(counts[0]).at[count_at + 1].set(counts[1])

    def cot_rows(pick, cot, info):
        rows = dot(pick, cot, ((1,), (0,))).astype(BF16)
        facts = (dot(pick, columns(info), ((1,), (0,))) + count_row[None, :]).astype(BF16)
        return jnp.concatenate([rows, facts], axis=1).reshape(half, capacity, width + META)

    send_cot = jnp.concatenate(
        [cot_rows(pick_own, cot_mine, about), cot_rows(pick_mate, cot_mate, about_mate)], axis=1
    )
    recv_cot = exchange(send_cot)

    gate_w, up_w, down_w = gate_weight[0], up_weight[0], down_weight[0]

    def forward(rows):
        gate_pre = dot(rows, gate_w, ((1,), (1,)))
        up_pre = dot(rows, up_w, ((1,), (1,)))
        sigmoid_gate = jax.nn.sigmoid(gate_pre)
        hidden = (gate_pre * sigmoid_gate * up_pre).astype(BF16)
        partial = dot(hidden, down_w, ((1,), (0,))).astype(BF16)
        return gate_pre, up_pre, hidden, sum_rows(partial)

    rows_own = whole_rows(recv_own)
    gate_own, up_own, hidden_own, out_own = forward(rows_own)
    rows_mate = whole_rows(recv_mate)
    gate_mate, up_mate, hidden_mate, out_mate = forward(rows_mate)

    back_mate = exchange(out_mate.reshape(half, capacity, width)).reshape(slots, width)
    mix_mate = dot(spread_mate, back_mate, ((0,), (0,))).astype(BF16)
    mix_far = to_mate(mix_mate)
    back_own = exchange(out_own.reshape(half, capacity, width)).reshape(slots, width)
    mixed = dot(spread_own, back_own, ((0,), (0,))) + mix_far.astype(F32)

    facts = recv_cot[:, :, width:].astype(F32)
    totals = jnp.sum(facts[:, 0, count_at : count_at + 2], axis=0)
    mine = facts[:, :, :top_count] == me.astype(F32)
    share = sum(facts[:, :, (1 + i) * top_count : (2 + i) * top_count] for i in range(3))
    share = jnp.sum(jnp.where(mine, share, 0.0), axis=2)
    flag_at = 4 * top_count
    coefficient = float(top_count * tok_rows) * (
        facts[:, :, flag_at] / totals[0] - facts[:, :, flag_at + 1] / totals[1]
    )
    slot_weight = coefficient * share
    routed = (slot_weight[:, :, None] * recv_cot[:, :, :width].astype(F32)).astype(BF16)
    routed = jnp.concatenate(
        [
            routed[:, :capacity].reshape(slots, width),
            routed[:, capacity:].reshape(slots, width),
        ],
        axis=0,
    )
    routed = whole_rows(routed)

    def joined(a, b):
        return jnp.concatenate([a, b], axis=0)

    hidden = joined(hidden_own, hidden_mate)
    rows_in = joined(rows_own, rows_mate)
    gate_pre = joined(gate_own, gate_mate)
    up_pre = joined(up_own, up_mate)
    sigmoid_gate = jax.nn.sigmoid(gate_pre)
    grad_down = dot(hidden, routed, ((0,), (0,)))
    dhidden = dot(routed, down_w, ((1,), (1,)))
    dgate = (dhidden * up_pre * sigmoid_gate * (1.0 + gate_pre * (1.0 - sigmoid_gate))).astype(BF16)
    dup = (dhidden * gate_pre * sigmoid_gate).astype(BF16)
    grad_gate = dot(dgate, rows_in, ((0,), (0,)))
    grad_up = dot(dup, rows_in, ((0,), (0,)))
    return (
        mixed.astype(BF16),
        grad_gate.astype(BF16)[None],
        grad_up.astype(BF16)[None],
        grad_down.astype(BF16)[None],
    )


def solution(mesh):
    in_specs = (
        P("dp", None),
        P("dp", None),
        P("dp", None),
        P("dp", None),
        P("dp"),
        P(),
        P("dp", "tensor", None),
        P("dp", "tensor", None),
        P("dp", "tensor", None),
    )
    out_specs = (
        P("dp", "tensor"),
        P("dp", "tensor", None),
        P("dp", "tensor", None),
        P("dp", "tensor", None),
    )
    return jax.shard_map(body, mesh=mesh, in_specs=in_specs, out_specs=out_specs, check_vma=False)
```

time: 280 us -> 142 us (0.51)
  the two profiles are of different devices: /device:TPU:12 before, /device:TPU:0 now
where the time goes in v1:
time: 142 us; the launch traced here: 141 us
  matrix products  43.5 us (31%)
  waiting for transfers between devices  40 us (28%)
  starting transfers between devices  30 us (21%)
  other arithmetic  18.8 us (13%)
  local copies, waits for them, and re-layouts  8.11 us (6%)
    dot_general x20, matrix products, dot(): return lax.dot_general(a, b, (dims, ((), ())), preferred_element_type=F32)  43.5 us
    all_to_all x5, starting transfers between devices, exchange(): lax.all_to_all(value, 'dp', split_axis=0, concat_axis=0, axis_index_group...  22.3 us
    all_to_all x5, waiting for transfers between devices, exchange(): lax.all_to_all(value, 'dp', split_axis=0, concat_axis=0, axis_index_group...  20.1 us
    ppermute x4, waiting for transfers between devices, to_mate(): return lax.ppermute(value, 'dp', mates)  19.7 us
    ppermute x4, starting transfers between devices, to_mate(): return lax.ppermute(value, 'dp', mates)  7.03 us
    convert_element_type x2, other arithmetic, sum_rows(): return (mine.astype(F32) + other.astype(F32)).astype(BF16)  4.94 us
    dynamic_slice x2, local copies, waits for them, and re-layouts, my_features(): return lax.dynamic_slice_in_dim(value, core * width, width, axis=1)  3.34 us
  transfers between devices with their start and end apart: 14, of which 8 were waited for; matrix products, arithmetic and copies ran while one was open for 28% of the time, Pallas kernels for 0%

profile of v1, /device:TPU:0, one launch (start us, length us, event | category | flops | bytes accessed | tf_op | source)
XLA Modules:
  0.0 141.4 jit_solution(4642167773284724070)
XLA Ops:
  0.7 0.8 reduce_sum.65
  1.5 0.7 fusion.47
  2.2 0.7 fusion.51
  2.9 0.7 fusion.49
  3.6 0.7 fusion.64
  4.3 4.1 %collective-permute-start.2 = (f32[10,128]{1,0:T(8,128)S(1)}, f32[10,128]{1,0:T(8,128)S(1)}, u32[]{:S(2)}, u32[]{:S(2)}) collective-permute-start(f32[10,128]{1,0:T(8,128)S(1)} %pad_maximum_fusion.8), channel_id=1, source_target_pairs={{0,16},{2,18},{4,20},{6,22},{8,24},{10,26},{12,28},{14,30},{16,0},... | collective-permute-start | bytes 15368 | tf_op jit(solution)/shard_map/ppermute | solution.py:40
  8.4 1.7 %constant_dynamic-slice_fusion = bf16[128,1024]{1,0:T(8,128)(2,1)} fusion(bf16[128,2048]{1,0:T(8,128)(2,1)} %param.14, s32[]{:T(128)S(6)} %select_n.93), kind=kLoop, calls=%fused_computation.124 | loop fusion | bytes 524292 | tf_op jit(solution)/shard_map/dynamic_slice | solution.py:66
  10.1 1.7 %constant_dynamic-slice_fusion.1 = bf16[128,1024]{1,0:T(8,128)(2,1)} fusion(bf16[128,2048]{1,0:T(8,128)(2,1)} %param.13, s32[]{:T(128)S(6)} %select_n.93), kind=kLoop, calls=%fused_computation.125 | loop fusion | bytes 524292 | tf_op jit(solution)/shard_map/dynamic_slice | solution.py:66
  11.8 2.9 %collective-permute-start.3 = (bf16[128,1024]{1,0:T(8,128)(2,1)}, bf16[128,1024]{1,0:T(8,128)(2,1)}, u32[]{:S(2)}, u32[]{:S(2)}) collective-permute-start(bf16[128,1024]{1,0:T(8,128)(2,1)} %constant_dynamic-slice_fusion.1), channel_id=1, source_target_pairs={{0,16},{2,18},{4,20},{6,22},{8,24},{10,26},{12,28},{14,30},{16,0},... | collective-permute-start | bytes 786440 | tf_op jit(solution)/shard_map/ppermute | solution.py:40
  14.9 0.1 convolution_select_fusion
  15.0 0.1 convolution_select_fusion.1
  15.1 0.1 bitcast_compare_fusion
  15.3 2.1 %convolution_convert_fusion.8 = bf16[320,1024]{1,0:T(8,128)(2,1)} fusion(pred[320,128]{1,0:T(32,128)(4,1)S(1)} %get-tuple-element.50, bf16[128,1024]{1,0:T(8,128)(2,1)} %constant_dynamic-slice_fusion.1), kind=kOutput, calls=%fused_computation.27 | convolution fusion | flops 84213760 | bytes 958464 | tf_op jit(solution)/shard_map/dot_general | solution.py:12
  17.4 4.7 %all-to-all-start = ((bf16[8,40,1024]{2,1,0:T(8,128)(2,1)}), bf16[8,40,1024]{2,1,0:T(8,128)(2,1)S(1)}, u32[]{:S(2)}, u32[]{:S(2)}) async-start(bf16[8,40,1024]{2,1,0:T(8,128)(2,1)} %bitcast.3), calls=%async_computation | async-start | bytes 1310720 | tf_op jit(solution)/shard_map/all_to_all | solution.py:43
  22.2 0.1 fusion.50
  22.3 0.1 scatter.6
  22.5 0.1 constant_dynamic-update-slice_fusion
  22.7 0.8 fusion.22
  23.5 1.3 convolution_convert_fusion.6
  24.7 11.3 %collective-permute-done.3 = bf16[128,1024]{1,0:T(8,128)(2,1)} collective-permute-done((bf16[128,1024]{1,0:T(8,128)(2,1)}, bf16[128,1024]{1,0:T(8,128)(2,1)}, u32[]{:S(2)}, u32[]{:S(2)}) %collective-permute-start.3) | collective-permute-done | bytes 262176 | tf_op jit(solution)/shard_map/ppermute | solution.py:40
  36.0 2.1 %convolution_convert_fusion.7 = bf16[320,1024]{1,0:T(8,128)(2,1)} fusion(pred[320,128]{1,0:T(32,128)(4,1)S(1)} %get-tuple-element.49, bf16[128,1024]{1,0:T(8,128)(2,1)} %collective-permute-done.3), kind=kOutput, calls=%fused_computation.26 | convolution fusion | flops 84213760 | bytes 958464 | tf_op jit(solution)/shard_map/dot_general | solution.py:12
  38.1 3.6 %all-to-all-done = bf16[8,40,1024]{2,1,0:T(8,128)(2,1)S(1)} async-done(((bf16[8,40,1024]{2,1,0:T(8,128)(2,1)}), bf16[8,40,1024]{2,1,0:T(8,128)(2,1)S(1)}, u32[]{:S(2)}, u32[]{:S(2)}) %all-to-all-start) | async-done | bytes 655392 | tf_op jit(solution)/shard_map/all_to_all | solution.py:43
  41.7 4.2 %all-to-all-start.2 = ((bf16[8,40,1024]{2,1,0:T(8,128)(2,1)}), bf16[8,40,1024]{2,1,0:T(8,128)(2,1)}, u32[]{:S(2)}, u32[]{:S(2)}) async-start(bf16[8,40,1024]{2,1,0:T(8,128)(2,1)} %bitcast.13), calls=%async_computation.2 | async-start | bytes 1310720 | tf_op jit(solution)/shard_map/all_to_all | solution.py:43
  45.9 0.1 fusion.21
  46.2 1.3 convolution_convert_fusion.5
  47.6 1.2 pad_maximum_fusion.3
  48.8 5.5 %all-to-all-done.2 = bf16[8,40,1024]{2,1,0:T(8,128)(2,1)} async-done(((bf16[8,40,1024]{2,1,0:T(8,128)(2,1)}), bf16[8,40,1024]{2,1,0:T(8,128)(2,1)}, u32[]{:S(2)}, u32[]{:S(2)}) %all-to-all-start.2) | async-done | bytes 655392 | tf_op jit(solution)/shard_map/all_to_all | solution.py:43
  54.3 4.3 %all-to-all-start.4 = ((bf16[8,80,1152]{2,1,0:T(8,128)(2,1)}), bf16[8,80,1152]{2,1,0:T(8,128)(2,1)}, u32[]{:S(2)}, u32[]{:S(2)}) async-start(bf16[8,80,1152]{2,1,0:T(8,128)(2,1)} %pad_maximum_fusion.3), calls=%async_computation.4 | async-start | bytes 2949120 | tf_op jit(solution)/shard_map/all_to_all | solution.py:43
  58.7 0.5 maximum_select_fusion.1
  59.2 1.0 copy-done.7
  60.2 0.9 fusion.13
  61.1 0.2 copy-done.2
  61.3 1.0 copy-done.8
  62.3 1.7 %multiply_convert_fusion.4 = (bf16[320,512]{1,0:T(8,128)(2,1)S(1)}, f32[320,512]{1,0:T(8,128)}) fusion(f32[320,512]{1,0:T(8,128)S(1)} %fusion.13, bf16[320,2048]{1,0:T(8,128)(2,1)S(1)} %maximum_select_fusion.1, bf16[1,512,2048]{2,1,0:T(8,128)(2,1)S(1)} %copy-done.8), kind=kOutput, calls=%fused_computation.59 | convolution fusion | flops 672071680 | bytes 5046272 | tf_op jit(solution)/shard_map/dot_general | solution.py:12
  64.0 1.9 %maximum_select_fusion.2 = bf16[320,2048]{1,0:T(8,128)(2,1)S(1)} fusion(bf16[320,1024]{1,0:T(8,128)(2,1)S(1)} %collective-permute-done.4, bf16[320,1024]{1,0:T(8,128)(2,1)} %bitcast.14, pred[]{:T(512)S(6)} %eq.106), kind=kLoop, calls=%fused_computation.29 | loop fusion | flops 5898240 | bytes 2621441 | tf_op jit(solution)/shard_map/jit(_where)/select_n | solution.py:51
  65.9 0.9 fusion.11
  66.8 0.2 copy-done.4
  67.0 1.7 %multiply_convert_fusion.3 = (bf16[320,512]{1,0:T(8,128)(2,1)S(1)}, f32[320,512]{1,0:T(8,128)}) fusion(f32[320,512]{1,0:T(8,128)S(1)} %fusion.11, bf16[320,2048]{1,0:T(8,128)(2,1)S(1)} %maximum_select_fusion.2, bf16[1,512,2048]{2,1,0:T(8,128)(2,1)S(1)} %copy-done.8), kind=kOutput, calls=%fused_computation.58 | convolution fusion | flops 672071680 | bytes 5046272 | tf_op jit(solution)/shard_map/dot_general | solution.py:12
  68.7 0.9 convolution_convert_fusion.3
  69.6 1.0 broadcast_select_fusion
  70.7 0.9 convolution_convert_fusion.4
  71.5 0.9 broadcast_select_fusion.1
  72.5 0.5 collective-permute-start.1
  73.0 0.1 collective-permute-done.5
  73.1 2.7 %add_convert_fusion = bf16[320,1024]{1,0:T(8,128)(2,1)} fusion(bf16[320,1024]{1,0:T(8,128)(2,1)} %collective-permute-done.5, pred[]{:T(512)S(6)} %eq.106, bf16[320,2048]{1,0:T(8,128)(2,1)} %copy-done.1), kind=kLoop, calls=%fused_computation.38 | loop fusion | flops 1638400 | bytes 2621441 | tf_op jit(solution)/shard_map/convert_element_type | solution.py:63
  75.8 0.3 all-to-all-done.4
  76.1 4.7 %all-to-all-start.3 = ((bf16[8,40,1024]{2,1,0:T(8,128)(2,1)}), bf16[8,40,1024]{2,1,0:T(8,128)(2,1)}, u32[]{:S(2)}, u32[]{:S(2)}) async-start(bf16[8,40,1024]{2,1,0:T(8,128)(2,1)} %bitcast.102), calls=%async_computation.3 | async-start | bytes 1310720 | tf_op jit(solution)/shard_map/all_to_all | solution.py:43
  80.8 2.3 %add_convert_fusion.1 = bf16[320,1024]{1,0:T(8,128)(2,1)} fusion(bf16[320,1024]{1,0:T(8,128)(2,1)} %collective-permute-done.1, pred[]{:T(512)S(6)} %eq.106, bf16[320,2048]{1,0:T(8,128)(2,1)S(1)} %convolution_convert_fusion.4), kind=kLoop, calls=%fused_computation.39 | loop fusion | flops 1638400 | bytes 2621441 | tf_op jit(solution)/shard_map/convert_element_type | solution.py:63
  83.0 0.9 slice.120
  84.0 0.2 copy.21
  84.3 0.6 fusion.66
  84.9 1.3 fusion.46
  86.2 1.6 %multiply_convert_fusion = bf16[8,80,1024]{2,1,0:T(8,128)(2,1)S(1)} fusion(bf16[8,80,1152]{2,1,0:T(8,128)(2,1)} %all-to-all-done.4, f32[8,80]{1,0:T(8,128)S(1)} %fusion.46), kind=kLoop, calls=%fused_computation.10 | loop fusion | flops 1966080 | bytes 2624000 | tf_op jit(solution)/shard_map/convert_element_type | solution.py:176
  87.9 3.5 %all-to-all-done.3 = bf16[8,40,1024]{2,1,0:T(8,128)(2,1)} async-done(((bf16[8,40,1024]{2,1,0:T(8,128)(2,1)}), bf16[8,40,1024]{2,1,0:T(8,128)(2,1)}, u32[]{:S(2)}, u32[]{:S(2)}) %all-to-all-start.3) | async-done | bytes 655392 | tf_op jit(solution)/shard_map/all_to_all | solution.py:43
  91.5 4.4 %all-to-all-start.1 = ((bf16[8,40,1024]{2,1,0:T(8,128)(2,1)}), bf16[8,40,1024]{2,1,0:T(8,128)(2,1)}, u32[]{:S(2)}, u32[]{:S(2)}) async-start(bf16[8,40,1024]{2,1,0:T(8,128)(2,1)} %bitcast.101), calls=%async_computation.1 | async-start | bytes 1310720 | tf_op jit(solution)/shard_map/all_to_all | solution.py:43
  95.9 1.2 pad_maximum_fusion.4
  97.1 2.2 %fusion.20 = bf16[128,1024]{1,0:T(8,128)(2,1)} fusion(bf16[8,40,1024]{2,1,0:T(8,128)(2,1)} %all-to-all-done.3, bf16[8,128]{1,0:T(8,128)(2,1)S(1)} %get-tuple-element.29, f32[8,128]{1,0:T(8,128)S(1)} %convolution_select_fusion, f32[40]{0:T(128)S(1)} %iota_convert_fusion), kind=kOutput, calls=%fused_computation.44 | convolution fusion | flops 84099072 | bytes 923808 | tf_op jit(solution)/shard_map/dot_general | solution.py:12
  99.3 7.2 %all-to-all-done.1 = bf16[8,40,1024]{2,1,0:T(8,128)(2,1)} async-done(((bf16[8,40,1024]{2,1,0:T(8,128)(2,1)}), bf16[8,40,1024]{2,1,0:T(8,128)(2,1)}, u32[]{:S(2)}, u32[]{:S(2)}) %all-to-all-start.1) | async-done | bytes 655392 | tf_op jit(solution)/shard_map/all_to_all | solution.py:43
  106.5 8.4 %collective-permute-done.6 = bf16[128,1024]{1,0:T(8,128)(2,1)} collective-permute-done((bf16[128,1024]{1,0:T(8,128)(2,1)}, bf16[128,1024]{1,0:T(8,128)(2,1)}, u32[]{:S(2)}, u32[]{:S(2)}) %collective-permute-start.6) | collective-permute-done | bytes 262176 | tf_op jit(solution)/shard_map/ppermute | solution.py:40
  114.9 2.2 %fusion.19 = bf16[128,1024]{1,0:T(8,128)(2,1)} fusion(bf16[8,40,1024]{2,1,0:T(8,128)(2,1)} %all-to-all-done.1, bf16[128,1024]{1,0:T(8,128)(2,1)} %collective-permute-done.6, bf16[8,128]{1,0:T(8,128)(2,1)S(1)} %get-tuple-element.28, f32[8,128]{1,0:T(8,128)S(1)} %convolution_select_fusion.1, f32[40]{0:T(128)S(1)} %iota_convert_fusion), kind=kOutput, calls=%fused_computation.43 | convolution fusion | flops 84361216 | bytes 1185952 | tf_op jit(solution)/shard_map/dot_general | solution.py:12
  117.2 12.4 %fusion.3 = f32[640,512]{1,0:T(8,128)S(1)} fusion(bf16[1,512,2048]{2,1,0:T(8,128)(2,1)S(1)} %copy-done, bf16[640,1024]{1,0:T(8,128)(2,1)} %collective-permute-done.8, bf16[320,1024]{1,0:T(8,128)(2,1)S(1)} %bitcast.97, bf16[320,1024]{1,0:T(8,128)(2,1)S(1)} %bitcast.94, pred[]{:T(512)S(6)} %eq.106), kind=kOutput, calls=%fused_computation.11 | convolution fusion | flops 1359216640 | bytes 6029313 | tf_op jit(solution)/shard_map/dot_general | solution.py:12
  129.6 3.3 %fusion.1 = bf16[1,512,2048]{2,1,0:T(8,128)(2,1)} fusion(bf16[320,2048]{1,0:T(8,128)(2,1)S(1)} %copy-done.5, bf16[320,2048]{1,0:T(8,128)(2,1)S(1)} %copy-done.3, f32[640,512]{1,0:T(8,128)S(1)} %fusion.3, f32[320,512]{1,0:T(8,128)S(1)} %copy-done.16, f32[320,512]{1,0:T(8,128)S(1)} %copy-done.14), kind=kOutput, calls=%fused_computation.4 | convolution fusion | flops 1350762496 | bytes 7340032 | tf_op jit(solution)/shard_map/dot_general | solution.py:12
  132.9 3.5 %fusion = bf16[1,512,2048]{2,1,0:T(8,128)(2,1)} fusion(bf16[320,2048]{1,0:T(8,128)(2,1)S(1)} %copy-done.5, bf16[320,2048]{1,0:T(8,128)(2,1)S(1)} %copy-done.3, f32[640,512]{1,0:T(8,128)S(1)} %fusion.3, f32[320,512]{1,0:T(8,128)S(1)} %copy-done.18, f32[320,512]{1,0:T(8,128)S(1)} %copy-done.17, f32[320,512]{1,0:T(8,128)S(1)} %copy-done.16, ...), kind=kOutput, calls=%fused_computation.3 | convolution fusion | flops 1352400896 | bytes 8650752 | tf_op jit(solution)/shard_map/dot_general | solution.py:12
  136.4 5.0 %fusion.2 = bf16[1,512,2048]{2,1,0:T(8,128)(2,1)} fusion(bf16[320,512]{1,0:T(8,128)(2,1)S(1)} %copy-done.12, bf16[320,512]{1,0:T(8,128)(2,1)S(1)} %copy-done.10, bf16[640,1024]{1,0:T(8,128)(2,1)} %collective-permute-done.8, bf16[320,1024]{1,0:T(8,128)(2,1)S(1)} %bitcast.98, bf16[320,1024]{1,0:T(8,128)(2,1)S(1)} %bitcast.95, pred[]{:T(512)S(6)} %eq.106), kind=kOutput, calls=%fused_computation.5 | convolution fusion | flops 1361575936 | bytes 5373953 | tf_op jit(solution)/shard_map/dot_general | solution.py:12
  (66 shorter events, 1.1 us)
Async XLA Ops:
  0.6 68.1 %copy-start = (bf16[1,512,2048]{2,1,0:T(8,128)(2,1)S(1)}, bf16[1,512,2048]{2,1,0:T(8,128)(2,1)}, u32[]{:S(2)}) copy-start(bf16[1,512,2048]{2,1,0:T(8,128)(2,1)} %param.21) | copy-start | bytes 6291460
  4.3 10.5 %collective-permute-start.2 = (f32[10,128]{1,0:T(8,128)S(1)}, f32[10,128]{1,0:T(8,128)S(1)}, u32[]{:S(2)}, u32[]{:S(2)}) collective-permute-start(f32[10,128]{1,0:T(8,128)S(1)} %pad_maximum_fusion.8), channel_id=1, source_target_pairs={{0,16},{2,18},{4,20},{6,22},{8,24},{10,26},{12,28},{14,30},{16,0},... | collective-permute-start | bytes 15368 | tf_op jit(solution)/shard_map/ppermute | solution.py:40
  10.1 36.1 %collective-permute-start.7 = (bf16[128,1024]{1,0:T(8,128)(2,1)}, bf16[128,1024]{1,0:T(8,128)(2,1)}, u32[]{:S(2)}, u32[]{:S(2)}) collective-permute-start(bf16[128,1024]{1,0:T(8,128)(2,1)} %constant_dynamic-slice_fusion), channel_id=1, source_target_pairs={{0,16},{2,18},{4,20},{6,22},{8,24},{10,26},{12,28},{14,30},{16,0},... | collective-permute-start | bytes 786440 | tf_op jit(solution)/shard_map/ppermute | solution.py:40
  11.8 24.2 %collective-permute-start.3 = (bf16[128,1024]{1,0:T(8,128)(2,1)}, bf16[128,1024]{1,0:T(8,128)(2,1)}, u32[]{:S(2)}, u32[]{:S(2)}) collective-permute-start(bf16[128,1024]{1,0:T(8,128)(2,1)} %constant_dynamic-slice_fusion.1), channel_id=1, source_target_pairs={{0,16},{2,18},{4,20},{6,22},{8,24},{10,26},{12,28},{14,30},{16,0},... | collective-permute-start | bytes 786440 | tf_op jit(solution)/shard_map/ppermute | solution.py:40
  17.4 24.3 %all-to-all-start = ((bf16[8,40,1024]{2,1,0:T(8,128)(2,1)}), bf16[8,40,1024]{2,1,0:T(8,128)(2,1)S(1)}, u32[]{:S(2)}, u32[]{:S(2)}) async-start(bf16[8,40,1024]{2,1,0:T(8,128)(2,1)} %bitcast.3), calls=%async_computation | async-start | bytes 1310720 | tf_op jit(solution)/shard_map/all_to_all | solution.py:43
  41.7 12.6 %all-to-all-start.2 = ((bf16[8,40,1024]{2,1,0:T(8,128)(2,1)}), bf16[8,40,1024]{2,1,0:T(8,128)(2,1)}, u32[]{:S(2)}, u32[]{:S(2)}) async-start(bf16[8,40,1024]{2,1,0:T(8,128)(2,1)} %bitcast.13), calls=%async_computation.2 | async-start | bytes 1310720 | tf_op jit(solution)/shard_map/all_to_all | solution.py:43
  45.9 1.6 %copy-start.6 = (bf16[320,128]{1,0:T(8,128)(2,1)S(1)}, bf16[320,128]{1,0:T(8,128)(2,1)}, u32[]{:S(2)}) copy-start(bf16[320,128]{1,0:T(8,128)(2,1)} %fusion.22) | copy-start | bytes 245764
  46.1 12.6 %collective-permute-start = (bf16[320,1024]{1,0:T(8,128)(2,1)S(1)}, bf16[320,1024]{1,0:T(8,128)(2,1)S(1)}, u32[]{:S(2)}, u32[]{:S(2)}) collective-permute-start(bf16[320,1024]{1,0:T(8,128)(2,1)S(1)} %bitcast.99), channel_id=1, source_target_pairs={{0,1},{1,0},{2,3},{3,2},{4,5},{5,4},{6,7},{7,6},{8,9},{9,8},{10,11... | collective-permute-start | bytes 1966088 | tf_op jit(solution)/shard_map/ppermute | solution.py:50
  54.3 21.8 %all-to-all-start.4 = ((bf16[8,80,1152]{2,1,0:T(8,128)(2,1)}), bf16[8,80,1152]{2,1,0:T(8,128)(2,1)}, u32[]{:S(2)}, u32[]{:S(2)}) async-start(bf16[8,80,1152]{2,1,0:T(8,128)(2,1)} %pad_maximum_fusion.3), calls=%async_computation.4 | async-start | bytes 2949120 | tf_op jit(solution)/shard_map/all_to_all | solution.py:43
  58.6 1.6 %copy-start.7 = (bf16[1,512,2048]{2,1,0:T(8,128)(2,1)S(1)}, bf16[1,512,2048]{2,1,0:T(8,128)(2,1)}, u32[]{:S(2)}) copy-start(bf16[1,512,2048]{2,1,0:T(8,128)(2,1)} %param.19) | copy-start | bytes 6291460
  58.6 5.4 %collective-permute-start.4 = (bf16[320,1024]{1,0:T(8,128)(2,1)}, bf16[320,1024]{1,0:T(8,128)(2,1)S(1)}, u32[]{:S(2)}, u32[]{:S(2)}) collective-permute-start(bf16[320,1024]{1,0:T(8,128)(2,1)} %bitcast.14), channel_id=1, source_target_pairs={{0,1},{1,0},{2,3},{3,2},{4,5},{5,4},{6,7},{7,6},{8,9},{9,8},{10,11... | collective-permute-start | bytes 1966088 | tf_op jit(solution)/shard_map/ppermute | solution.py:50
  60.2 1.1 copy-start.2
  60.2 2.1 %copy-start.8 = (bf16[1,512,2048]{2,1,0:T(8,128)(2,1)S(1)}, bf16[1,512,2048]{2,1,0:T(8,128)(2,1)}, u32[]{:S(2)}) copy-start(bf16[1,512,2048]{2,1,0:T(8,128)(2,1)} %param.20) | copy-start | bytes 6291460
  62.3 1.7 %copy-start.13 = (f32[320,512]{1,0:T(8,128)}, f32[320,512]{1,0:T(8,128)S(1)}, u32[]{:S(2)}) copy-start(f32[320,512]{1,0:T(8,128)S(1)} %fusion.13) | copy-start | bytes 1966084
  64.0 6.6 %copy-start.9 = (bf16[320,512]{1,0:T(8,128)(2,1)}, bf16[320,512]{1,0:T(8,128)(2,1)S(1)}, u32[]{:S(2)}) copy-start(bf16[320,512]{1,0:T(8,128)(2,1)S(1)} %get-tuple-element.55) | copy-start | bytes 983044
  65.9 1.1 copy-start.4
  67.0 1.7 %copy-start.15 = (f32[320,512]{1,0:T(8,128)}, f32[320,512]{1,0:T(8,128)S(1)}, u32[]{:S(2)}) copy-start(f32[320,512]{1,0:T(8,128)S(1)} %fusion.11) | copy-start | bytes 1966084
  68.7 0.9 copy-start.11
  69.6 2.0 %copy-start.1 = (bf16[320,2048]{1,0:T(8,128)(2,1)}, bf16[320,2048]{1,0:T(8,128)(2,1)S(1)}, u32[]{:S(2)}) copy-start(bf16[320,2048]{1,0:T(8,128)(2,1)S(1)} %convolution_convert_fusion.3) | copy-start | bytes 3932164
  70.6 2.4 %collective-permute-start.5 = (bf16[320,1024]{1,0:T(8,128)(2,1)}, bf16[320,1024]{1,0:T(8,128)(2,1)}, u32[]{:S(2)}, u32[]{:S(2)}) collective-permute-start(bf16[320,1024]{1,0:T(8,128)(2,1)} %broadcast_select_fusion), channel_id=1, source_target_pairs={{0,1},{1,0},{2,3},{3,2},{4,5},{5,4},{6,7},{7,6},{8,9},{9,8},{10,11... | collective-permute-start | bytes 1966088 | tf_op jit(solution)/shard_map/ppermute | solution.py:61
  72.5 8.3 %collective-permute-start.1 = (bf16[320,1024]{1,0:T(8,128)(2,1)}, bf16[320,1024]{1,0:T(8,128)(2,1)}, u32[]{:S(2)}, u32[]{:S(2)}) collective-permute-start(bf16[320,1024]{1,0:T(8,128)(2,1)} %broadcast_select_fusion.1), channel_id=1, source_target_pairs={{0,1},{1,0},{2,3},{3,2},{4,5},{5,4},{6,7},{7,6},{8,9},{9,8},{10,11... | collective-permute-start | bytes 1966088 | tf_op jit(solution)/shard_map/ppermute | solution.py:61
  76.1 15.4 %all-to-all-start.3 = ((bf16[8,40,1024]{2,1,0:T(8,128)(2,1)}), bf16[8,40,1024]{2,1,0:T(8,128)(2,1)}, u32[]{:S(2)}, u32[]{:S(2)}) async-start(bf16[8,40,1024]{2,1,0:T(8,128)(2,1)} %bitcast.102), calls=%async_computation.3 | async-start | bytes 1310720 | tf_op jit(solution)/shard_map/all_to_all | solution.py:43
  91.5 15.0 %all-to-all-start.1 = ((bf16[8,40,1024]{2,1,0:T(8,128)(2,1)}), bf16[8,40,1024]{2,1,0:T(8,128)(2,1)}, u32[]{:S(2)}, u32[]{:S(2)}) async-start(bf16[8,40,1024]{2,1,0:T(8,128)(2,1)} %bitcast.101), calls=%async_computation.1 | async-start | bytes 1310720 | tf_op jit(solution)/shard_map/all_to_all | solution.py:43
  97.0 20.1 %collective-permute-start.8 = (bf16[640,1024]{1,0:T(8,128)(2,1)}, bf16[640,1024]{1,0:T(8,128)(2,1)}, u32[]{:S(2)}, u32[]{:S(2)}) collective-permute-start(bf16[640,1024]{1,0:T(8,128)(2,1)} %pad_maximum_fusion.4), channel_id=1, source_target_pairs={{0,1},{1,0},{2,3},{3,2},{4,5},{5,4},{6,7},{7,6},{8,9},{9,8},{10,11... | collective-permute-start | bytes 3932168 | tf_op jit(solution)/shard_map/ppermute | solution.py:50
  99.3 15.6 %collective-permute-start.6 = (bf16[128,1024]{1,0:T(8,128)(2,1)}, bf16[128,1024]{1,0:T(8,128)(2,1)}, u32[]{:S(2)}, u32[]{:S(2)}) collective-permute-start(bf16[128,1024]{1,0:T(8,128)(2,1)} %fusion.20), channel_id=1, source_target_pairs={{0,16},{2,18},{4,20},{6,22},{8,24},{10,26},{12,28},{14,30},{16,0},... | collective-permute-start | bytes 786440 | tf_op jit(solution)/shard_map/ppermute | solution.py:40
  117.1 12.4 %copy-start.3 = (bf16[320,2048]{1,0:T(8,128)(2,1)S(1)}, bf16[320,2048]{1,0:T(8,128)(2,1)}, u32[]{:S(2)}) copy-start(bf16[320,2048]{1,0:T(8,128)(2,1)} %copy-done.2) | copy-start | bytes 3932164
  117.1 12.5 %copy-start.5 = (bf16[320,2048]{1,0:T(8,128)(2,1)S(1)}, bf16[320,2048]{1,0:T(8,128)(2,1)}, u32[]{:S(2)}) copy-start(bf16[320,2048]{1,0:T(8,128)(2,1)} %copy-done.4) | copy-start | bytes 3932164
  117.1 12.5 %copy-start.14 = (f32[320,512]{1,0:T(8,128)S(1)}, f32[320,512]{1,0:T(8,128)}, u32[]{:S(2)}) copy-start(f32[320,512]{1,0:T(8,128)} %copy-done.13) | copy-start | bytes 1966084
  117.1 12.5 %copy-start.16 = (f32[320,512]{1,0:T(8,128)S(1)}, f32[320,512]{1,0:T(8,128)}, u32[]{:S(2)}) copy-start(f32[320,512]{1,0:T(8,128)} %copy-done.15) | copy-start | bytes 1966084
  129.6 3.3 %copy-start.17 = (f32[320,512]{1,0:T(8,128)S(1)}, f32[320,512]{1,0:T(8,128)}, u32[]{:S(2)}) copy-start(f32[320,512]{1,0:T(8,128)} %get-tuple-element.56) | copy-start | bytes 1966084
  129.6 3.3 %copy-start.18 = (f32[320,512]{1,0:T(8,128)S(1)}, f32[320,512]{1,0:T(8,128)}, u32[]{:S(2)}) copy-start(f32[320,512]{1,0:T(8,128)} %get-tuple-element.58) | copy-start | bytes 1966084
  132.9 3.5 %copy-start.10 = (bf16[320,512]{1,0:T(8,128)(2,1)S(1)}, bf16[320,512]{1,0:T(8,128)(2,1)}, u32[]{:S(2)}) copy-start(bf16[320,512]{1,0:T(8,128)(2,1)} %copy-done.9) | copy-start | bytes 983044
  132.9 3.5 %copy-start.12 = (bf16[320,512]{1,0:T(8,128)(2,1)S(1)}, bf16[320,512]{1,0:T(8,128)(2,1)}, u32[]{:S(2)}) copy-start(bf16[320,512]{1,0:T(8,128)(2,1)} %copy-done.11) | copy-start | bytes 983044

commit v2 on v0

v2 whole, which is shorter than its diff:
```python
import functools

import jax
import jax.numpy as jnp
from jax import lax
from jax.experimental import pallas as pl
from jax.experimental.pallas import tpu as pltpu
from jax.sharding import PartitionSpec as P

F32 = jnp.float32
BF16 = jnp.bfloat16
LANES = 128
FACTS = 16
VMEM = pl.BlockSpec(memory_space=pltpu.VMEM)
SMEM = pl.BlockSpec(memory_space=pltpu.SMEM)
ANY = pl.BlockSpec(memory_space=pl.ANY)
HBM = pl.BlockSpec(memory_space=pltpu.HBM)


def cost(micros):
    return pl.CostEstimate(
        flops=int(micros * 1e9), bytes_accessed=int(micros * 3e6), transcendentals=0
    )


def in_hbm(value):
    return pltpu.with_memory_space_constraint(value, pltpu.HBM)


def dot(a, b, dims):
    return lax.dot_general(a, b, (dims, ((), ())), preferred_element_type=F32)


def facts_kernel(top, seq_len, place_ref, lengths_ref, ids_ref, weight_ref, forget_ref, out_ref):
    toks = ids_ref.shape[1]
    weight = weight_ref[...]
    out_ref[:top, :] = ids_ref[...].astype(F32)
    out_ref[top : 2 * top, :] = weight / jnp.sum(weight, axis=0, keepdims=True)
    token = place_ref[0] + lax.broadcasted_iota(jnp.int32, (1, toks), 1)
    valid = jnp.zeros((1, toks), jnp.int32)
    for s in range(lengths_ref.shape[0]):
        begin = s * seq_len
        inside = (token >= begin) & (token < begin + lengths_ref[s])
        valid = jnp.where(inside, 1, valid)
    forget = valid * forget_ref[...]
    out_ref[2 * top : 2 * top + 1, :] = (valid - forget).astype(F32)
    out_ref[2 * top + 1 : 2 * top + 2, :] = forget.astype(F32)
    rest = 2 * top + 2
    out_ref[rest:, :] = jnp.zeros((out_ref.shape[0] - rest, toks), F32)


def slot_tables(top, half, capacity, first, info, pick_ref, weighted_ref=None, factor=None):
    toks = info.shape[1]
    expert = (first + lax.broadcasted_iota(jnp.int32, (half, toks), 0)).astype(F32)
    named = jnp.zeros((half, toks), F32)
    weight = jnp.zeros((half, toks), F32)
    for k in range(top):
        hit = info[k : k + 1, :] == expert
        named = jnp.where(hit, 1.0, named)
        weight = jnp.where(hit, info[top + k : top + k + 1, :], weight)
    row = lax.broadcasted_iota(jnp.int32, (toks, toks), 0)
    column = lax.broadcasted_iota(jnp.int32, (toks, toks), 1)
    earlier = jnp.where(row < column, 1.0, 0.0).astype(BF16)
    rank = dot(named.astype(BF16), earlier, ((1,), (0,)))
    rank = jnp.where(named > 0.0, rank, -1.0)
    if factor is not None:
        weight = factor * weight
    slot = lax.broadcasted_iota(jnp.int32, (capacity, toks), 0).astype(F32)
    for e in range(half):
        at = rank[e : e + 1, :] == slot
        rows = slice(e * capacity, (e + 1) * capacity)
        pick_ref[rows, :] = jnp.where(at, 1.0, 0.0)
        if weighted_ref is not None:
            weighted_ref[rows, :] = jnp.where(at, weight[e : e + 1, :], 0.0)


def gather_kernel(top, half, capacity, counted, first_ref, info_ref, x_ref, out_ref, pick_ref):
    info = info_ref[...]
    width = x_ref.shape[1]
    slot_tables(top, half, capacity, first_ref[0], info, pick_ref)
    out_ref[:, :width] = dot(pick_ref[...].astype(BF16), x_ref[...], ((1,), (0,))).astype(BF16)
    if counted:
        count = jnp.sum(info[2 * top : 2 * top + 2, :], axis=1, keepdims=True)
        lane = lax.broadcasted_iota(jnp.int32, (out_ref.shape[0], LANES), 1)
        both = jnp.where(lane == 0, count[0:1, :], jnp.where(lane == 1, count[1:2, :], 0.0))
        out_ref[:, width:] = both.astype(BF16)


def scaled_kernel(
    top, half, capacity, scale, first_ref, total_ref, info_ref, info2_ref, x_ref, x2_ref, out_ref, pick_ref, weight_ref
):
    width = x_ref.shape[1]
    total = total_ref[...]
    retain_all, forget_all = total[:, 0:1], total[:, 1:2]
    for i, (own, x) in enumerate(((info_ref, x_ref), (info2_ref, x2_ref))):
        info = own[...]
        factor = scale * (
            info[2 * top : 2 * top + 1, :] / retain_all - info[2 * top + 1 : 2 * top + 2, :] / forget_all
        )
        slot_tables(top, half, capacity, first_ref[0], info, pick_ref, weight_ref, factor)
        rows = dot(pick_ref[...].astype(BF16), x[...], ((1,), (0,)))
        slot_weight = jnp.sum(weight_ref[...], axis=1, keepdims=True)
        out_ref[:, i * width : (i + 1) * width] = (slot_weight * rows).astype(BF16)


def mix_kernel(top, half, capacity, first_ref, info_ref, back_ref, *rest):
    far_refs, (out_ref, pick_ref, weight_ref) = rest[:-3], rest[-3:]
    slot_tables(top, half, capacity, first_ref[0], info_ref[...], pick_ref, weight_ref)
    weight = weight_ref[...]
    high = weight.astype(BF16)
    low = (weight - high.astype(F32)).astype(BF16)
    back = back_ref[...]
    total = dot(high, back, ((0,), (0,))) + dot(low, back, ((0,), (0,)))
    for far in far_refs:
        total = total + far[...].astype(F32)
    out_ref[...] = total.astype(BF16)


def halve_kernel(core_ref, x_ref, out_ref):
    width = out_ref.shape[1]
    out_ref[...] = x_ref[:, pl.ds(pl.multiple_of(core_ref[0] * width, LANES), width)]


def add_kernel(a_ref, b_ref, out_ref):
    out_ref[...] = (a_ref[...].astype(F32) + b_ref[...].astype(F32)).astype(BF16)


def spans_of(at_ref, pieces, width):
    return [pl.ds(pl.multiple_of(at_ref[i], LANES), width) for i in range(pieces)]


def copier(sems):
    started = []

    def copy(src, dst):
        started.append(pltpu.make_async_copy(src, dst, sems.at[len(started)]))
        started[-1].start()
        return started[-1]

    return copy


def block(ref, j, step):
    return ref.at[pl.ds(j * step, step)]


def forward_kernel(pieces, step, at_ref, *refs):
    n = pieces
    xs_in, weights_in, refs = refs[: 2 * n], refs[2 * n : 2 * n + 3], refs[2 * n + 3 :]
    outs, refs = refs[: 3 + 2 * n], refs[3 + 2 * n :]
    xs, (gate_w, up_w, down_w), refs = refs[: 2 * n], refs[2 * n : 2 * n + 3], refs[2 * n + 3 :]
    held, sems = refs[:-1], refs[-1]
    keep_gate, keep_up, hidden_ref = held[:3]
    copy = copier(sems)
    slots, width = held[3].shape
    spans = spans_of(at_ref, n, width)
    blocks = gate_w.shape[0] // step
    x_copies = [copy(src.at[:, pl.ds(0, width)], dst) for src, dst in zip(xs_in, xs)]
    gate_copies, up_copies, down_copies = [], [], []
    for j in range(blocks):
        gate_copies.append(copy(block(weights_in[0], j, step), block(gate_w, j, step)))
        up_copies.append(copy(block(weights_in[1], j, step), block(up_w, j, step)))
    down_copy = copy(weights_in[2], down_w)
    for started in x_copies:
        started.wait()
    for j in range(blocks):
        gate_copies[j].wait()
        up_copies[j].wait()
        units = slice(j * step, (j + 1) * step)
        for part in (1, 0):
            rows = slice(part * slots, (part + 1) * slots)
            mine = xs[part * n : (part + 1) * n]
            gate = sum(dot(x[...], gate_w[units, span], ((1,), (1,))) for x, span in zip(mine, spans))
            up = sum(dot(x[...], up_w[units, span], ((1,), (1,))) for x, span in zip(mine, spans))
            s = jax.nn.sigmoid(gate)
            silu = gate * s
            keep_gate[rows, units] = (up * s * (1.0 + gate * (1.0 - s))).astype(BF16)
            keep_up[rows, units] = silu.astype(BF16)
            hidden_ref[rows, units] = (silu * up).astype(BF16)
    out_copies = [copy(src, dst) for src, dst in zip(held[:3], outs[:3])]
    down_copy.wait()
    for k, part in enumerate((1, 0)):
        hidden = hidden_ref[part * slots : (part + 1) * slots, :]
        for i in reversed(range(n)):
            spot = 3 + k * n + i
            held[spot][...] = dot(hidden, down_w[:, spans[i]], ((1,), (0,))).astype(BF16)
            out_copies.append(copy(held[spot], outs[spot]))
    for started in out_copies:
        started.wait()


def backward_kernel(pieces, step, at_ref, *refs):
    n = pieces
    xs_in, (weight_in, gate_in, up_in), refs = refs[:n], refs[n : n + 3], refs[n + 3 :]
    outs, xs, refs = refs[:2], refs[2 : 2 + n], refs[2 + n :]
    down_w, keep_gate, keep_up, dgate_ref, dup_ref, sems = refs
    copy = copier(sems)
    slots, width = xs[0].shape[0], xs[0].shape[1] // 2
    spans = spans_of(at_ref, n, width)
    blocks = down_w.shape[0] // step
    copies = [copy(src, dst) for src, dst in zip(xs_in, xs)]
    w_copies = [copy(block(weight_in, j, step), block(down_w, j, step)) for j in range(blocks)]
    copies += [copy(gate_in, keep_gate), copy(up_in, keep_up)]
    for started in copies:
        started.wait()
    for j in range(blocks):
        w_copies[j].wait()
        units = slice(j * step, (j + 1) * step)
        for part in range(2):
            rows = slice(part * slots, (part + 1) * slots)
            lanes = slice(part * width, (part + 1) * width)
            dhidden = sum(dot(x[:, lanes], down_w[units, span], ((1,), (1,))) for x, span in zip(xs, spans))
            dgate_ref[rows, units] = (dhidden * keep_gate[rows, units].astype(F32)).astype(BF16)
            dup_ref[rows, units] = (dhidden * keep_up[rows, units].astype(F32)).astype(BF16)
    for started in [copy(dgate_ref, outs[0]), copy(dup_ref, outs[1])]:
        started.wait()


def grads_kernel(joined, pieces, count, width, step, at_ref, *refs):
    n = pieces
    number = n if joined else 2 * n
    lefts_in, xs_in, refs = refs[:count], refs[count : count + number], refs[count + number :]
    outs, refs = refs[:count], refs[count:]
    lefts, xs, (turned, buffer, sems, out_sems) = refs[:count], refs[count : count + number], refs[count + number :]
    copy = copier(sems)
    slots = xs[0].shape[0]
    left_copies = [copy(src, dst) for src, dst in zip(lefts_in, lefts)]
    lanes = xs[0].shape[1]
    x_copies = [copy(src.at[:, pl.ds(0, lanes)], dst) for src, dst in zip(xs_in, xs)]
    copies, number = [None, None], 0
    for m in range(count):
        left_copies[m].wait()
        turned[...] = lefts[m][...].T
        if m == 0:
            for started in x_copies:
                started.wait()
        for i in range(n):
            for begin in range(0, width, step):
                total = 0.0
                for part in range(2):
                    rows = slice(part * slots, (part + 1) * slots)
                    if joined:
                        right = xs[i][:, part * width + begin : part * width + begin + step]
                    else:
                        right = xs[part * n + i][:, begin : begin + step]
                    total = total + dot(turned[:, rows], right, ((1,), (0,)))
                spot = number % 2
                if copies[spot] is not None:
                    copies[spot].wait()
                buffer[spot] = total.astype(BF16)
                target = pl.ds(pl.multiple_of(at_ref[i] + begin, LANES), step)
                copies[spot] = pltpu.make_async_copy(buffer.at[spot], outs[m].at[:, target], out_sems.at[spot])
                copies[spot].start()
                number += 1
    for started in copies:
        if started is not None:
            started.wait()


def body(
    tokens,
    cotangent,
    expert_ids,
    route_weight,
    forget_mask,
    lengths,
    gate_weight,
    up_weight,
    down_weight,
):
    tok_rows, features = tokens.shape
    top = expert_ids.shape[1]
    owners = lax.axis_size("dp")
    parts = lax.axis_size("tensor")
    half = owners // 2
    width = features // parts
    capacity = 5 * tok_rows * top // (4 * owners)
    slots = half * capacity
    seq_len = tok_rows * owners // lengths.shape[0]
    me = lax.axis_index("dp")
    core = lax.axis_index("tensor")
    mates = [(i, (i + half) % owners) for i in range(owners)]
    halves = [list(range(half)), list(range(half, owners))]
    first = ((me // half) * half).astype(jnp.int32).reshape(1)
    place = (me * tok_rows).astype(jnp.int32).reshape(1)
    table = pltpu.VMEM((slots, tok_rows), F32)
    limit = pltpu.CompilerParams(vmem_limit_bytes=8 * 2**20)

    def to_mate(value):
        return lax.ppermute(value, "dp", mates)

    def exchange(value):
        value = value.reshape(half, value.shape[0] // half, value.shape[1])
        return lax.all_to_all(
            value, "dp", split_axis=0, concat_axis=0, axis_index_groups=halves, tiled=True
        )

    def swapped(value):
        return lax.ppermute(value, "tensor", [(0, 1), (1, 0)])

    def my_features(value):
        return pl.pallas_call(
            halve_kernel,
            out_shape=jax.ShapeDtypeStruct((tok_rows, width), BF16),
            in_specs=[SMEM, VMEM],
            out_specs=VMEM,
            compiler_params=limit,
            cost_estimate=cost(1),
        )(core.astype(jnp.int32).reshape(1), value)

    def after(value, *others):
        return lax.optimization_barrier((value, *others))[0]

    def mixed_rows(info, back, *far):
        return pl.pallas_call(
            functools.partial(mix_kernel, top, half, capacity),
            out_shape=jax.ShapeDtypeStruct((tok_rows, width), BF16),
            in_specs=[SMEM, VMEM, VMEM] + [VMEM] * len(far),
            out_specs=VMEM,
            scratch_shapes=[table, table],
            compiler_params=limit,
            cost_estimate=cost(1),
        )(first, info, back, *far)

    tok_mine = my_features(tokens)
    tok_mate = to_mate(tok_mine)
    expert_ids = after(expert_ids, tok_mine)
    about = pl.pallas_call(
        functools.partial(facts_kernel, top, seq_len),
        out_shape=jax.ShapeDtypeStruct((FACTS, tok_rows), F32),
        in_specs=[SMEM, SMEM, VMEM, VMEM, VMEM],
        out_specs=VMEM,
        compiler_params=limit,
        cost_estimate=cost(1),
    )(place, lengths, expert_ids.T, route_weight.T, forget_mask.reshape(1, tok_rows))
    about_mate = to_mate(about)

    def gathered(info, x, counted, micros):
        return pl.pallas_call(
            functools.partial(gather_kernel, top, half, capacity, counted),
            out_shape=jax.ShapeDtypeStruct((slots, width + (LANES if counted else 0)), BF16),
            in_specs=[SMEM, VMEM, VMEM],
            out_specs=VMEM,
            scratch_shapes=[table],
            compiler_params=limit,
            cost_estimate=cost(micros),
        )(first, info, x)

    recv_own = exchange(gathered(about, tok_mine, True, 1))
    count = jnp.sum(recv_own[:, :1, width:].astype(F32), axis=0)
    total = count + to_mate(count)
    recv_own = recv_own.reshape(slots, width + LANES)
    recv_mate = exchange(gathered(about_mate, tok_mate, False, 1)).reshape(slots, width)

    cot_mine = my_features(after(cotangent, about))
    cot_mate = to_mate(cot_mine)
    send_cot = pl.pallas_call(
        functools.partial(scaled_kernel, top, half, capacity, float(top * tok_rows)),
        out_shape=jax.ShapeDtypeStruct((slots, 2 * width), BF16),
        in_specs=[SMEM] + [VMEM] * 5,
        out_specs=VMEM,
        scratch_shapes=[table, table],
        compiler_params=limit,
        cost_estimate=cost(1),
    )(first, total, about, about_mate, cot_mine, cot_mate)
    recv_cot = exchange(after(send_cot, recv_mate)).reshape(slots, 2 * width)

    gate_w, up_w, down_w = gate_weight[0], up_weight[0], down_weight[0]

    units = gate_w.shape[0]
    pieces = 2 if parts == 2 else 1
    span = features // pieces
    step = min(units, 256)
    blocks = units // step
    if parts == 2:
        at = jnp.stack([core, 1 - core]).astype(jnp.int32) * width
    else:
        at = jnp.zeros((1,), jnp.int32)
    shape = jax.ShapeDtypeStruct
    weight_buffer = pltpu.VMEM((units, features), BF16)
    roomy = pltpu.CompilerParams(vmem_limit_bytes=20 * 2**20)

    def pair(value):
        if parts == 2:
            return [value, swapped(value)]
        return [lax.all_gather(value[:, :width], "tensor", axis=1, tiled=True)]

    def double_pair(value):
        if parts == 2:
            return [value, swapped(value)]
        return [jnp.concatenate([pair(value[:, :width])[0], pair(value[:, width:])[0]], axis=1)]

    def summed(outs):
        if parts != 2:
            return lax.psum_scatter(outs[0], "tensor", scatter_dimension=1, tiled=True)
        return pl.pallas_call(
            add_kernel,
            out_shape=shape((slots, width), BF16),
            in_specs=[VMEM] * 2,
            out_specs=VMEM,
            compiler_params=limit,
            cost_estimate=cost(1),
        )(outs[0], swapped(outs[1]))

    toks = [in_hbm(x) for x in pair(recv_own) + pair(after(recv_mate, cot_mate))]
    weights = [in_hbm(w) for w in (gate_w, up_w, down_w)]
    kept = [((2 * slots, units), BF16)] * 3 + [((slots, span), BF16)] * (2 * pieces)
    held = [pltpu.VMEM(*k) for k in kept]
    x_buffers = [pltpu.VMEM((slots, span), BF16) for x in toks]
    keep_gate, keep_up, hidden, *outs = pl.pallas_call(
        functools.partial(forward_kernel, pieces, step),
        out_shape=[pltpu.HBM(*k) for k in kept],
        in_specs=[SMEM] + [HBM] * (2 * pieces + 3),
        out_specs=[HBM] * len(kept),
        scratch_shapes=x_buffers
        + [weight_buffer] * 3
        + held
        + [pltpu.SemaphoreType.DMA((2 * pieces + 2 * blocks + 1 + len(kept),))],
        compiler_params=roomy,
        cost_estimate=cost(7),
    )(at, *toks, *weights)
    out_mate = summed(outs[:pieces])
    back_mate = exchange(out_mate).reshape(slots, width)
    out_own = summed(outs[pieces:])

    cots = [in_hbm(x) for x in double_pair(after(recv_cot, out_mate))]
    c_buffers = [pltpu.VMEM(x.shape, BF16) for x in cots]
    unit_rows = ((2 * slots, units), BF16)
    dgate, dup = pl.pallas_call(
        functools.partial(backward_kernel, pieces, step),
        out_shape=[pltpu.HBM(*unit_rows)] * 2,
        in_specs=[SMEM] + [HBM] * (pieces + 3),
        out_specs=[HBM] * 2,
        scratch_shapes=c_buffers
        + [weight_buffer]
        + [pltpu.VMEM(*unit_rows)] * 4
        + [pltpu.SemaphoreType.DMA((pieces + blocks + 4,))],
        compiler_params=roomy,
        cost_estimate=cost(4),
    )(at, *cots, weights[2], in_hbm(keep_gate), in_hbm(keep_up))

    mix_mate = mixed_rows(about_mate, after(back_mate, dgate))
    mix_far = to_mate(mix_mate)

    def grads(lefts, xs, joined):
        count, lanes = len(lefts), 2 * span if joined else span
        return pl.pallas_call(
            functools.partial(grads_kernel, joined, pieces, count, span, 512),
            out_shape=[pltpu.HBM((units, features), BF16)] * count,
            in_specs=[SMEM] + [HBM] * (len(xs) + count),
            out_specs=[HBM] * count,
            scratch_shapes=[pltpu.VMEM(*unit_rows)] * count
            + [pltpu.VMEM((slots, lanes), BF16) for x in xs]
            + [
                pltpu.VMEM((units, 2 * slots), BF16),
                pltpu.VMEM((2, units, 512), BF16),
                pltpu.SemaphoreType.DMA((count + len(xs),)),
                pltpu.SemaphoreType.DMA((2,)),
            ],
            compiler_params=roomy,
            cost_estimate=cost(4 * count),
        )(at, *[in_hbm(x) for x in lefts], *xs)

    (grad_down,) = grads([hidden], cots, True)
    grad_gate, grad_up = grads([dgate, dup], toks, False)
    back_own = exchange(after(out_own, mix_mate)).reshape(slots, width)
    mixed = mixed_rows(about, back_own, mix_far)
    return (
        mixed,
        grad_gate[None],
        grad_up[None],
        grad_down[None],
    )


def solution(mesh):
    in_specs = (
        P("dp", None),
        P("dp", None),
        P("dp", None),
        P("dp", None),
        P("dp"),
        P(),
        P("dp", "tensor", None),
        P("dp", "tensor", None),
        P("dp", "tensor", None),
    )
    out_specs = (
        P("dp", "tensor"),
        P("dp", "tensor", None),
        P("dp", "tensor", None),
        P("dp", "tensor", None),
    )
    return jax.shard_map(body, mesh=mesh, in_specs=in_specs, out_specs=out_specs, check_vma=False)
```

time: 280 us -> 108 us (0.39)
  the two profiles are of different devices: /device:TPU:12 before, /device:TPU:0 now
where the time goes in v2:
time: 108 us
  Pallas kernels  39.3 us (36%)
  starting transfers between devices  33.9 us (31%)
  waiting for transfers between devices  31.3 us (29%)
  local copies, waits for them, and re-layouts  2.18 us (2%)
    all_to_all x5, starting transfers between devices, exchange(): lax.all_to_all(value, 'dp', split_axis=0, concat_axis=0, axis_index_group...  25.2 us
    ppermute x5, waiting for transfers between devices, to_mate(): return lax.ppermute(value, 'dp', mates)  21.3 us
    pallas_call x2, Pallas kernels, grads(): pl.pallas_call(functools.partial(grads_kernel, joined, pieces, count, spa...  15.5 us
    pallas_call x1, Pallas kernels, body(): pl.pallas_call(functools.partial(forward_kernel, pieces, step), out_shape...  8.63 us
    ppermute x5, starting transfers between devices, to_mate(): return lax.ppermute(value, 'dp', mates)  7.72 us
    ppermute x5, waiting for transfers between devices, swapped(): return lax.ppermute(value, 'tensor', [(0, 1), (1, 0)])  6.88 us
    pallas_call x1, Pallas kernels, body(): pl.pallas_call(functools.partial(backward_kernel, pieces, step), out_shap...  6.13 us
    all_to_all x5, waiting for transfers between devices, exchange(): lax.all_to_all(value, 'dp', split_axis=0, concat_axis=0, axis_index_group...  3.19 us
  transfers between devices with their start and end apart: 15, of which 8 were waited for; matrix products, arithmetic and copies ran while one was open for 0% of the time, Pallas kernels for 33%

profile of v2, /device:TPU:0, one launch (start us, length us, event | category | flops | bytes accessed | tf_op | source)
XLA Modules:
  0.0 107.7 jit_solution(9559934883266737105)
XLA Ops:
  0.6 0.0 copy-start.2
  0.6 0.0 copy-start.4
  0.7 0.0 copy-start.5
  0.7 0.0 copy-start.3
  0.7 0.0 copy-start
  0.7 1.0 copy-done
  1.8 0.0 copy-done.2
  1.8 0.0 copy-done.4
  1.8 0.0 copy-done.5
  1.8 0.0 copy-done.3
  1.8 0.6 shard_map.121.info_ref
  2.4 1.3 %shard_map.122 = bf16[320,1152]{1,0:T(8,128)(2,1)} custom-call(s32[1]{0:T(128)} %bitcast.first_ref, f32[16,128]{1,0:T(8,128)S(1)} %shard_map.121.info_ref, bf16[128,1024]{1,0:T(8,128)(2,1)S(1)} %shard_map.120.x_ref), custom_call_target="tpu_custom_call" | custom-call | flops 1000000000 | bytes 3000000 | tf_op jit(solution)/shard_map/pallas_call | solution.py:339
  3.7 6.2 %all-to-all-start = ((bf16[8,40,1152]{2,1,0:T(8,128)(2,1)}), bf16[8,40,1152]{2,1,0:T(8,128)(2,1)S(1)}, u32[]{:S(2)}, u32[]{:S(2)}) async-start(bf16[8,40,1152]{2,1,0:T(8,128)(2,1)} %bitcast.7), calls=%async_computation | async-start | bytes 1474560 | tf_op jit(solution)/shard_map/all_to_all | solution.py:294
  9.9 0.0 copy-start.1
  9.9 2.7 %collective-permute-start.2 = (bf16[128,1024]{1,0:T(8,128)(2,1)S(1)}, bf16[128,1024]{1,0:T(8,128)(2,1)S(1)}, u32[]{:S(2)}, u32[]{:S(2)}) collective-permute-start(bf16[128,1024]{1,0:T(8,128)(2,1)S(1)} %shard_map.120.x_ref), channel_id=1, source_target_pairs={{0,16},{2,18},{4,20},{6,22},{8,24},{10,26},{12,28},{14,30},{16,0},... | collective-permute-start | bytes 786440 | tf_op jit(solution)/shard_map/ppermute | solution.py:290
  12.5 0.3 collective-permute-start.1
  12.9 10.9 %collective-permute-done.1.info_ref.info2_ref = f32[16,128]{1,0:T(8,128)S(1)} collective-permute-done((f32[16,128]{1,0:T(8,128)S(1)}, f32[16,128]{1,0:T(8,128)S(1)}, u32[]{:S(2)}, u32[]{:S(2)}) %collective-permute-start.1) | collective-permute-done | bytes 8224 | tf_op jit(solution)/shard_map/ppermute | solution.py:290
  23.8 0.0 collective-permute-done.2.x_ref
  23.8 1.3 %shard_map.123 = bf16[320,1024]{1,0:T(8,128)(2,1)} custom-call(s32[1]{0:T(128)} %bitcast.first_ref, f32[16,128]{1,0:T(8,128)S(1)} %collective-permute-done.1.info_ref.info2_ref, bf16[128,1024]{1,0:T(8,128)(2,1)S(1)} %collective-permute-done.2.x_ref), custom_call_target="tpu_custom_call" | custom-call | flops 1000000000 | bytes 3000000 | tf_op jit(solution)/shard_map/pallas_call | solution.py:339
  25.1 1.7 %all-to-all-done = bf16[8,40,1152]{2,1,0:T(8,128)(2,1)S(1)} async-done(((bf16[8,40,1152]{2,1,0:T(8,128)(2,1)}), bf16[8,40,1152]{2,1,0:T(8,128)(2,1)S(1)}, u32[]{:S(2)}, u32[]{:S(2)}) %all-to-all-start) | async-done | bytes 737312 | tf_op jit(solution)/shard_map/all_to_all | solution.py:294
  26.7 0.0 copy-start.9
  26.7 6.2 %all-to-all-start.1 = ((bf16[8,40,1024]{2,1,0:T(8,128)(2,1)}), bf16[8,40,1024]{2,1,0:T(8,128)(2,1)S(1)}, u32[]{:S(2)}, u32[]{:S(2)}) async-start(bf16[8,40,1024]{2,1,0:T(8,128)(2,1)} %bitcast.9), calls=%async_computation.1 | async-start | bytes 1310720 | tf_op jit(solution)/shard_map/all_to_all | solution.py:294
  32.9 0.0 copy-done.1
  33.0 0.1 collective-permute-start.3
  33.0 0.0 copy-done.9
  33.1 3.0 %collective-permute-start.7 = (f32[1,128]{1,0:T(1,128)S(1)}, f32[1,128]{1,0:T(1,128)S(1)}, u32[]{:S(2)}, u32[]{:S(2)}) collective-permute-start(f32[1,128]{1,0:T(1,128)S(1)} %bitcast.39), channel_id=1, source_target_pairs={{0,16},{2,18},{4,20},{6,22},{8,24},{10,26},{12,28},{14,30},{16,0},... | collective-permute-start | bytes 1544 | tf_op jit(solution)/shard_map/ppermute | solution.py:290
  36.0 10.3 %collective-permute-done.7 = f32[1,128]{1,0:T(1,128)S(1)} collective-permute-done((f32[1,128]{1,0:T(1,128)S(1)}, f32[1,128]{1,0:T(1,128)S(1)}, u32[]{:S(2)}, u32[]{:S(2)}) %collective-permute-start.7) | collective-permute-done | bytes 544 | tf_op jit(solution)/shard_map/ppermute | solution.py:290
  46.4 0.0 collective-permute-done.3.x2_ref
  46.4 1.8 %shard_map.128 = bf16[320,2048]{1,0:T(8,128)(2,1)} custom-call(s32[1]{0:T(128)} %bitcast.first_ref, f32[1,128]{1,0:T(1,128)S(1)} %bitcast_add_fusion.total_ref, f32[16,128]{1,0:T(8,128)S(1)} %shard_map.121.info_ref, f32[16,128]{1,0:T(8,128)S(1)} %collective-permute-done.1.info_ref.info2_ref, bf16[128,1024]{1,0:T(8,128)(2,1)S(1)} %shard_map.124.x_ref, ...), custom_call_target="tpu_custom_call" | custom-call | flops 1000000000 | bytes 3000000 | tf_op jit(solution)/shard_map/pallas_call | solution.py:357
  48.2 0.0 copy-start.10
  48.2 0.0 all-to-all-done.1
  48.2 4.0 %all-to-all-start.3 = ((bf16[8,40,2048]{2,1,0:T(8,128)(2,1)}), bf16[8,40,2048]{2,1,0:T(8,128)(2,1)S(1)}, u32[]{:S(2)}, u32[]{:S(2)}) async-start(bf16[8,40,2048]{2,1,0:T(8,128)(2,1)} %bitcast.17), calls=%async_computation.3 | async-start | bytes 2621440 | tf_op jit(solution)/shard_map/all_to_all | solution.py:294
  52.2 0.0 copy-done.10
  52.2 0.1 collective-permute-start
  52.3 0.5 collective-permute-start.4
  52.8 0.1 add_multiply_fusion.at_ref
  52.9 1.8 %collective-permute-done.refs_1_.refs_3_ = bf16[320,1152]{1,0:T(8,128)(2,1)} collective-permute-done((bf16[320,1152]{1,0:T(8,128)(2,1)S(1)}, bf16[320,1152]{1,0:T(8,128)(2,1)}, u32[]{:S(2)}, u32[]{:S(2)}) %collective-permute-start) | collective-permute-done | bytes 737312 | tf_op jit(solution)/shard_map/ppermute | solution.py:299
  54.7 0.9 collective-permute-done.4.refs_3_.refs_5_
  55.6 0.0 copy-done.11
  55.6 8.6 %shard_map.125 = (bf16[640,512]{1,0:T(8,128)(2,1)}, bf16[640,512]{1,0:T(8,128)(2,1)}, bf16[640,512]{1,0:T(8,128)(2,1)}, bf16[320,1024]{1,0:T(8,128)(2,1)}, bf16[...) custom-call(s32[2]{0:T(128)S(1)} %add_multiply_fusion.at_ref, ...), custom_call_target="tpu_custom_call" | custom-call | flops 7000000000 | bytes 21000000 | tf_op jit(solution)/shard_map/pallas_call | solution.py:410
  64.2 0.2 collective-permute-start.6
  64.4 2.2 %collective-permute-done.6.b_ref = bf16[320,1024]{1,0:T(8,128)(2,1)S(1)} collective-permute-done((bf16[320,1024]{1,0:T(8,128)(2,1)}, bf16[320,1024]{1,0:T(8,128)(2,1)S(1)}, u32[]{:S(2)}, u32[]{:S(2)}) %collective-permute-start.6) | collective-permute-done | bytes 655392 | tf_op jit(solution)/shard_map/ppermute | solution.py:299
  66.6 1.1 %copy-done.7 = bf16[320,1024]{1,0:T(8,128)(2,1)S(1)} copy-done((bf16[320,1024]{1,0:T(8,128)(2,1)S(1)}, bf16[320,1024]{1,0:T(8,128)(2,1)}, u32[]{:S(2)}) %copy-start.7) | copy-done | bytes 655384
  67.7 1.1 shard_map.127
  68.8 0.0 all-to-all-done.3
  68.8 0.1 collective-permute-start.8
  68.9 5.0 %all-to-all-start.2 = ((bf16[8,40,1024]{2,1,0:T(8,128)(2,1)}), bf16[8,40,1024]{2,1,0:T(8,128)(2,1)S(1)}, u32[]{:S(2)}, u32[]{:S(2)}) async-start(bf16[8,40,1024]{2,1,0:T(8,128)(2,1)} %bitcast.14), calls=%async_computation.2 | async-start | bytes 1310720 | tf_op jit(solution)/shard_map/all_to_all | solution.py:294
  73.9 0.0 copy-done.12
  74.0 0.1 collective-permute-start.5
  74.1 2.0 %collective-permute-done.5.b_ref = bf16[320,1024]{1,0:T(8,128)(2,1)S(1)} collective-permute-done((bf16[320,1024]{1,0:T(8,128)(2,1)S(1)}, bf16[320,1024]{1,0:T(8,128)(2,1)S(1)}, u32[]{:S(2)}, u32[]{:S(2)}) %collective-permute-start.5) | collective-permute-done | bytes 655392 | tf_op jit(solution)/shard_map/ppermute | solution.py:299
  76.1 0.0 copy-done.6
  76.1 1.0 shard_map.126
  77.1 0.0 copy-done.8
  77.1 0.0 collective-permute-done.8.refs_1_.refs_2_
  77.1 6.1 %shard_map.129 = (bf16[640,512]{1,0:T(8,128)(2,1)}, bf16[640,512]{1,0:T(8,128)(2,1)}) custom-call(s32[2]{0:T(128)S(1)} %add_multiply_fusion.at_ref, bf16[320,2048]{1,0:T(8,128)(2,1)} %bitcast.31, bf16[320,2048]{1,0:T(8,128)(2,1)} %collective-permute-done.8.refs_1_.refs_2_, bf16[512,2048]{1,0:T(8,128)(2,1)} %bitcast.43, ...), custom_call_target="tpu_custom_call" | custom-call | flops 4000000000 | bytes 12000000 | tf_op jit(solution)/shard_map/pallas_call | solution.py:429
  83.3 1.5 %all-to-all-done.2 = bf16[8,40,1024]{2,1,0:T(8,128)(2,1)S(1)} async-done(((bf16[8,40,1024]{2,1,0:T(8,128)(2,1)}), bf16[8,40,1024]{2,1,0:T(8,128)(2,1)S(1)}, u32[]{:S(2)}, u32[]{:S(2)}) %all-to-all-start.2) | async-done | bytes 655392 | tf_op jit(solution)/shard_map/all_to_all | solution.py:294
  84.8 0.6 shard_map.130
  85.4 3.7 %all-to-all-start.4 = ((bf16[8,40,1024]{2,1,0:T(8,128)(2,1)}), bf16[8,40,1024]{2,1,0:T(8,128)(2,1)S(1)}, u32[]{:S(2)}, u32[]{:S(2)}) async-start(bf16[8,40,1024]{2,1,0:T(8,128)(2,1)} %bitcast.19), calls=%async_computation.4 | async-start | bytes 1310720 | tf_op jit(solution)/shard_map/all_to_all | solution.py:294
  89.1 1.7 %collective-permute-start.9 = (bf16[128,1024]{1,0:T(8,128)(2,1)S(1)}, bf16[128,1024]{1,0:T(8,128)(2,1)S(1)}, u32[]{:S(2)}, u32[]{:S(2)}) collective-permute-start(bf16[128,1024]{1,0:T(8,128)(2,1)S(1)} %shard_map.130), channel_id=1, source_target_pairs={{0,16},{2,18},{4,20},{6,22},{8,24},{10,26},{12,28},{14,30},{16,0},... | collective-permute-start | bytes 786440 | tf_op jit(solution)/shard_map/ppermute | solution.py:290
  90.8 9.5 %shard_map.132 = (bf16[512,2048]{1,0:T(8,128)(2,1)}, bf16[512,2048]{1,0:T(8,128)(2,1)}) custom-call(s32[2]{0:T(128)S(1)} %add_multiply_fusion.at_ref, bf16[640,512]{1,0:T(8,128)(2,1)} %get-tuple-element.33.refs_0_, bf16[640,512]{1,0:T(8,128)(2,1)} %get-tuple-element.36.refs_1_, bf16[320,1152]{1,0:T(8,128)(2,1)} %bitcast.34, ...), custom_call_target="tpu_custom_call" | custom-call | flops 8000000000 | bytes 24000000 | tf_op jit(solution)/shard_map/pallas_call | solution.py:447
  100.3 6.0 %shard_map.133 = bf16[512,2048]{1,0:T(8,128)(2,1)} custom-call(s32[2]{0:T(128)S(1)} %add_multiply_fusion.at_ref, bf16[640,512]{1,0:T(8,128)(2,1)} %get-tuple-element.39.refs_0_, bf16[320,2048]{1,0:T(8,128)(2,1)} %bitcast.32, bf16[320,2048]{1,0:T(8,128)(2,1)} %collective-permute-done.8.refs_1_.refs_2_), custom_call_target="tpu_custom_call" | custom-call | flops 4000000000 | bytes 12000000 | tf_op jit(solution)/shard_map/pallas_call | solution.py:447
  106.3 0.0 collective-permute-done.9.rest_0_
  106.4 0.0 all-to-all-done.4
  106.4 1.3 %shard_map.131 = bf16[128,1024]{1,0:T(8,128)(2,1)} custom-call(s32[1]{0:T(128)} %bitcast.first_ref, f32[16,128]{1,0:T(8,128)S(1)} %shard_map.121.info_ref, bf16[320,1024]{1,0:T(8,128)(2,1)S(1)} %bitcast.25, bf16[128,1024]{1,0:T(8,128)(2,1)S(1)} %collective-permute-done.9.rest_0_), custom_call_target="tpu_custom_call" | custom-call | flops 1000000000 | bytes 3000000 | tf_op jit(solution)/shard_map/pallas_call | solution.py:315
  (9 shorter events, 0.1 us)
Async XLA Ops:
  0.6 1.1 %copy-start.2 = (s32[128,4]{0,1:T(4,128)S(1)}, s32[128,4]{0,1:T(4,128)}, u32[]{:S(2)}) copy-start(s32[128,4]{0,1:T(4,128)} %param.11) | copy-start | bytes 6148
  0.6 1.1 %copy-start.4 = (s32[2]{0:T(128)S(1)}, s32[2]{0:T(128)}, u32[]{:S(2)}) copy-start(s32[2]{0:T(128)} %lengths_ref.1) | copy-start | bytes 28
  0.7 1.1 %copy-start.5 = (s32[128]{0:T(128)S(1)}, s32[128]{0:T(128)}, u32[]{:S(2)}) copy-start(s32[128]{0:T(128)} %param.13) | copy-start | bytes 1540
  0.7 1.1 %copy-start.3 = (f32[128,4]{0,1:T(4,128)S(1)}, f32[128,4]{0,1:T(4,128)}, u32[]{:S(2)}) copy-start(f32[128,4]{0,1:T(4,128)} %param.12) | copy-start | bytes 6148
  0.7 1.1 copy-start
  3.7 23.1 %all-to-all-start = ((bf16[8,40,1152]{2,1,0:T(8,128)(2,1)}), bf16[8,40,1152]{2,1,0:T(8,128)(2,1)S(1)}, u32[]{:S(2)}, u32[]{:S(2)}) async-start(bf16[8,40,1152]{2,1,0:T(8,128)(2,1)} %bitcast.7), calls=%async_computation | async-start | bytes 1474560 | tf_op jit(solution)/shard_map/all_to_all | solution.py:294
  9.9 23.0 %copy-start.1 = (bf16[128,2048]{1,0:T(8,128)(2,1)S(1)}, bf16[128,2048]{1,0:T(8,128)(2,1)}, u32[]{:S(2)}) copy-start(bf16[128,2048]{1,0:T(8,128)(2,1)} %x_ref.2) | copy-start | bytes 1572868
  9.9 13.9 %collective-permute-start.2 = (bf16[128,1024]{1,0:T(8,128)(2,1)S(1)}, bf16[128,1024]{1,0:T(8,128)(2,1)S(1)}, u32[]{:S(2)}, u32[]{:S(2)}) collective-permute-start(bf16[128,1024]{1,0:T(8,128)(2,1)S(1)} %shard_map.120.x_ref), channel_id=1, source_target_pairs={{0,16},{2,18},{4,20},{6,22},{8,24},{10,26},{12,28},{14,30},{16,0},... | collective-permute-start | bytes 786440 | tf_op jit(solution)/shard_map/ppermute | solution.py:290
  12.5 11.2 %collective-permute-start.1 = (f32[16,128]{1,0:T(8,128)S(1)}, f32[16,128]{1,0:T(8,128)S(1)}, u32[]{:S(2)}, u32[]{:S(2)}) collective-permute-start(f32[16,128]{1,0:T(8,128)S(1)} %shard_map.121.info_ref), channel_id=1, source_target_pairs={{0,16},{2,18},{4,20},{6,22},{8,24},{10,26},{12,28},{14,30},{16,0},... | collective-permute-start | bytes 24584 | tf_op jit(solution)/shard_map/ppermute | solution.py:290
  26.7 6.3 %copy-start.9 = (bf16[8,40,1152]{2,1,0:T(8,128)(2,1)}, bf16[8,40,1152]{2,1,0:T(8,128)(2,1)S(1)}, u32[]{:S(2)}) copy-start(bf16[8,40,1152]{2,1,0:T(8,128)(2,1)S(1)} %all-to-all-done) | copy-start | bytes 2211844
  26.7 21.5 %all-to-all-start.1 = ((bf16[8,40,1024]{2,1,0:T(8,128)(2,1)}), bf16[8,40,1024]{2,1,0:T(8,128)(2,1)S(1)}, u32[]{:S(2)}, u32[]{:S(2)}) async-start(bf16[8,40,1024]{2,1,0:T(8,128)(2,1)} %bitcast.9), calls=%async_computation.1 | async-start | bytes 1310720 | tf_op jit(solution)/shard_map/all_to_all | solution.py:294
  33.0 13.4 %collective-permute-start.3 = (bf16[128,1024]{1,0:T(8,128)(2,1)S(1)}, bf16[128,1024]{1,0:T(8,128)(2,1)S(1)}, u32[]{:S(2)}, u32[]{:S(2)}) collective-permute-start(bf16[128,1024]{1,0:T(8,128)(2,1)S(1)} %shard_map.124.x_ref), channel_id=1, source_target_pairs={{0,16},{2,18},{4,20},{6,22},{8,24},{10,26},{12,28},{14,30},{16,0},... | collective-permute-start | bytes 786440 | tf_op jit(solution)/shard_map/ppermute | solution.py:290
  33.1 13.3 %collective-permute-start.7 = (f32[1,128]{1,0:T(1,128)S(1)}, f32[1,128]{1,0:T(1,128)S(1)}, u32[]{:S(2)}, u32[]{:S(2)}) collective-permute-start(f32[1,128]{1,0:T(1,128)S(1)} %bitcast.39), channel_id=1, source_target_pairs={{0,16},{2,18},{4,20},{6,22},{8,24},{10,26},{12,28},{14,30},{16,0},... | collective-permute-start | bytes 1544 | tf_op jit(solution)/shard_map/ppermute | solution.py:290
  48.2 4.0 %copy-start.10 = (bf16[8,40,1152]{2,1,0:T(8,128)(2,1)S(1)}, bf16[8,40,1152]{2,1,0:T(8,128)(2,1)}, u32[]{:S(2)}) copy-start(bf16[8,40,1152]{2,1,0:T(8,128)(2,1)} %copy-done.9) | copy-start | bytes 2211844
  48.2 7.4 %copy-start.11 = (bf16[8,40,1024]{2,1,0:T(8,128)(2,1)}, bf16[8,40,1024]{2,1,0:T(8,128)(2,1)S(1)}, u32[]{:S(2)}) copy-start(bf16[8,40,1024]{2,1,0:T(8,128)(2,1)S(1)} %all-to-all-done.1) | copy-start | bytes 1966084
  48.2 20.6 %all-to-all-start.3 = ((bf16[8,40,2048]{2,1,0:T(8,128)(2,1)}), bf16[8,40,2048]{2,1,0:T(8,128)(2,1)S(1)}, u32[]{:S(2)}, u32[]{:S(2)}) async-start(bf16[8,40,2048]{2,1,0:T(8,128)(2,1)} %bitcast.17), calls=%async_computation.3 | async-start | bytes 2621440 | tf_op jit(solution)/shard_map/all_to_all | solution.py:294
  52.2 2.4 %collective-permute-start = (bf16[320,1152]{1,0:T(8,128)(2,1)S(1)}, bf16[320,1152]{1,0:T(8,128)(2,1)}, u32[]{:S(2)}, u32[]{:S(2)}) collective-permute-start(bf16[320,1152]{1,0:T(8,128)(2,1)S(1)} %bitcast.35), channel_id=1, source_target_pairs={{0,1},{1,0},{2,3},{3,2},{4,5},{5,4},{6,7},{7,6},{8,9},{9,8},{10,11... | collective-permute-start | bytes 2211848 | tf_op jit(solution)/shard_map/ppermute | solution.py:299
  52.3 3.3 %collective-permute-start.4 = (bf16[320,1024]{1,0:T(8,128)(2,1)S(1)}, bf16[320,1024]{1,0:T(8,128)(2,1)}, u32[]{:S(2)}, u32[]{:S(2)}) collective-permute-start(bf16[320,1024]{1,0:T(8,128)(2,1)S(1)} %bitcast.36), channel_id=1, source_target_pairs={{0,1},{1,0},{2,3},{3,2},{4,5},{5,4},{6,7},{7,6},{8,9},{9,8},{10,11... | collective-permute-start | bytes 1966088 | tf_op jit(solution)/shard_map/ppermute | solution.py:299
  64.2 2.4 %collective-permute-start.6 = (bf16[320,1024]{1,0:T(8,128)(2,1)}, bf16[320,1024]{1,0:T(8,128)(2,1)S(1)}, u32[]{:S(2)}, u32[]{:S(2)}) collective-permute-start(bf16[320,1024]{1,0:T(8,128)(2,1)} %get-tuple-element.28), channel_id=1, source_target_pairs={{0,1},{1,0},{2,3},{3,2},{4,5},{5,4},{6,7},{7,6},{8,9},{9,8},{10,11... | collective-permute-start | bytes 1966088 | tf_op jit(solution)/shard_map/ppermute | solution.py:299
  66.6 1.1 %copy-start.7 = (bf16[320,1024]{1,0:T(8,128)(2,1)S(1)}, bf16[320,1024]{1,0:T(8,128)(2,1)}, u32[]{:S(2)}) copy-start(bf16[320,1024]{1,0:T(8,128)(2,1)} %get-tuple-element.27.a_ref) | copy-start | bytes 1966084
  67.7 6.3 %copy-start.12 = (bf16[320,1024]{1,0:T(8,128)(2,1)S(1)}, bf16[320,1024]{1,0:T(8,128)(2,1)}, u32[]{:S(2)}) copy-start(bf16[320,1024]{1,0:T(8,128)(2,1)} %get-tuple-element.26) | copy-start | bytes 1966084
  67.7 8.4 %copy-start.6 = (bf16[320,1024]{1,0:T(8,128)(2,1)S(1)}, bf16[320,1024]{1,0:T(8,128)(2,1)}, u32[]{:S(2)}) copy-start(bf16[320,1024]{1,0:T(8,128)(2,1)} %get-tuple-element.25.a_ref) | copy-start | bytes 1966084
  68.8 8.4 %copy-start.8 = (bf16[8,40,2048]{2,1,0:T(8,128)(2,1)}, bf16[8,40,2048]{2,1,0:T(8,128)(2,1)S(1)}, u32[]{:S(2)}) copy-start(bf16[8,40,2048]{2,1,0:T(8,128)(2,1)S(1)} %all-to-all-done.3) | copy-start | bytes 3932164
  68.8 8.4 %collective-permute-start.8 = (bf16[320,2048]{1,0:T(8,128)(2,1)S(1)}, bf16[320,2048]{1,0:T(8,128)(2,1)}, u32[]{:S(2)}, u32[]{:S(2)}) collective-permute-start(bf16[320,2048]{1,0:T(8,128)(2,1)S(1)} %bitcast.30), channel_id=1, source_target_pairs={{0,1},{1,0},{2,3},{3,2},{4,5},{5,4},{6,7},{7,6},{8,9},{9,8},{10,11... | collective-permute-start | bytes 3932168 | tf_op jit(solution)/shard_map/ppermute | solution.py:299
  68.9 15.9 %all-to-all-start.2 = ((bf16[8,40,1024]{2,1,0:T(8,128)(2,1)}), bf16[8,40,1024]{2,1,0:T(8,128)(2,1)S(1)}, u32[]{:S(2)}, u32[]{:S(2)}) async-start(bf16[8,40,1024]{2,1,0:T(8,128)(2,1)} %bitcast.14), calls=%async_computation.2 | async-start | bytes 1310720 | tf_op jit(solution)/shard_map/all_to_all | solution.py:294
  74.0 2.2 %collective-permute-start.5 = (bf16[320,1024]{1,0:T(8,128)(2,1)S(1)}, bf16[320,1024]{1,0:T(8,128)(2,1)S(1)}, u32[]{:S(2)}, u32[]{:S(2)}) collective-permute-start(bf16[320,1024]{1,0:T(8,128)(2,1)S(1)} %copy-done.12), channel_id=1, source_target_pairs={{0,1},{1,0},{2,3},{3,2},{4,5},{5,4},{6,7},{7,6},{8,9},{9,8},{10,11... | collective-permute-start | bytes 1966088 | tf_op jit(solution)/shard_map/ppermute | solution.py:299
  85.4 21.0 %all-to-all-start.4 = ((bf16[8,40,1024]{2,1,0:T(8,128)(2,1)}), bf16[8,40,1024]{2,1,0:T(8,128)(2,1)S(1)}, u32[]{:S(2)}, u32[]{:S(2)}) async-start(bf16[8,40,1024]{2,1,0:T(8,128)(2,1)} %bitcast.19), calls=%async_computation.4 | async-start | bytes 1310720 | tf_op jit(solution)/shard_map/all_to_all | solution.py:294
  89.1 17.2 %collective-permute-start.9 = (bf16[128,1024]{1,0:T(8,128)(2,1)S(1)}, bf16[128,1024]{1,0:T(8,128)(2,1)S(1)}, u32[]{:S(2)}, u32[]{:S(2)}) collective-permute-start(bf16[128,1024]{1,0:T(8,128)(2,1)S(1)} %shard_map.130), channel_id=1, source_target_pairs={{0,16},{2,18},{4,20},{6,22},{8,24},{10,26},{12,28},{14,30},{16,0},... | collective-permute-start | bytes 786440 | tf_op jit(solution)/shard_map/ppermute | solution.py:290

commit v3 on v2

v3 whole, which is shorter than its diff:
```python
import functools

import jax
import jax.numpy as jnp
from jax import lax
from jax.experimental import pallas as pl
from jax.experimental.pallas import tpu as pltpu
from jax.sharding import PartitionSpec as P

F32 = jnp.float32
BF16 = jnp.bfloat16
LANES = 128
FACTS = 16
VMEM = pl.BlockSpec(memory_space=pltpu.VMEM)
SMEM = pl.BlockSpec(memory_space=pltpu.SMEM)
ANY = pl.BlockSpec(memory_space=pl.ANY)
HBM = pl.BlockSpec(memory_space=pltpu.HBM)


def cost(micros):
    return pl.CostEstimate(
        flops=int(micros * 1e9), bytes_accessed=int(micros * 3e6), transcendentals=0
    )


def in_hbm(value):
    return pltpu.with_memory_space_constraint(value, pltpu.HBM)


def dot(a, b, dims):
    return lax.dot_general(a, b, (dims, ((), ())), preferred_element_type=F32)


def facts_kernel(top, seq_len, place_ref, lengths_ref, ids_ref, weight_ref, forget_ref, out_ref):
    toks = ids_ref.shape[1]
    weight = weight_ref[...]
    out_ref[:top, :] = ids_ref[...].astype(F32)
    out_ref[top : 2 * top, :] = weight / jnp.sum(weight, axis=0, keepdims=True)
    token = place_ref[0] + lax.broadcasted_iota(jnp.int32, (1, toks), 1)
    valid = jnp.zeros((1, toks), jnp.int32)
    for s in range(lengths_ref.shape[0]):
        begin = s * seq_len
        inside = (token >= begin) & (token < begin + lengths_ref[s])
        valid = jnp.where(inside, 1, valid)
    forget = valid * forget_ref[...]
    out_ref[2 * top : 2 * top + 1, :] = (valid - forget).astype(F32)
    out_ref[2 * top + 1 : 2 * top + 2, :] = forget.astype(F32)
    rest = 2 * top + 2
    out_ref[rest:, :] = jnp.zeros((out_ref.shape[0] - rest, toks), F32)


def slot_tables(top, half, capacity, first, info, pick_ref, weighted_ref=None, factor=None):
    toks = info.shape[1]
    expert = (first + lax.broadcasted_iota(jnp.int32, (half, toks), 0)).astype(F32)
    named = jnp.zeros((half, toks), F32)
    weight = jnp.zeros((half, toks), F32)
    for k in range(top):
        hit = info[k : k + 1, :] == expert
        named = jnp.where(hit, 1.0, named)
        weight = jnp.where(hit, info[top + k : top + k + 1, :], weight)
    row = lax.broadcasted_iota(jnp.int32, (toks, toks), 0)
    column = lax.broadcasted_iota(jnp.int32, (toks, toks), 1)
    earlier = jnp.where(row < column, 1.0, 0.0).astype(BF16)
    rank = dot(named.astype(BF16), earlier, ((1,), (0,)))
    rank = jnp.where(named > 0.0, rank, -1.0)
    if factor is not None:
        weight = factor * weight
    slot = lax.broadcasted_iota(jnp.int32, (capacity, toks), 0).astype(F32)
    for e in range(half):
        at = rank[e : e + 1, :] == slot
        rows = slice(e * capacity, (e + 1) * capacity)
        pick_ref[rows, :] = jnp.where(at, 1.0, 0.0)
        if weighted_ref is not None:
            weighted_ref[rows, :] = jnp.where(at, weight[e : e + 1, :], 0.0)


def gather_kernel(top, half, capacity, first_ref, info_ref, x_ref, out_ref, pick_ref, weight_ref):
    info = info_ref[...]
    width = x_ref.shape[1]
    slot_tables(top, half, capacity, first_ref[0], info, pick_ref, weight_ref)
    pick = pick_ref[...]
    out_ref[:, :width] = dot(pick.astype(BF16), x_ref[...], ((1,), (0,))).astype(BF16)
    share = jnp.sum(weight_ref[...], axis=1, keepdims=True)
    high = share.astype(BF16).astype(F32)
    middle = (share - high).astype(BF16).astype(F32)
    flags = info[2 * top : 2 * top + 2, :]
    marks = [jnp.sum(pick * flags[i : i + 1, :], axis=1, keepdims=True) for i in range(2)]
    counts = jnp.sum(flags, axis=1, keepdims=True)
    lane = lax.broadcasted_iota(jnp.int32, (out_ref.shape[0], LANES), 1)
    facts = jnp.zeros((out_ref.shape[0], LANES), F32)
    columns = [high, middle, share - high - middle, marks[0], marks[1], counts[0:1, :], counts[1:2, :]]
    for i, column in enumerate(columns):
        facts = jnp.where(lane == i, column, facts)
    out_ref[:, width:] = facts.astype(BF16)


def cot_kernel(top, half, capacity, first_ref, info_ref, info2_ref, x_ref, x2_ref, out_ref, pick_ref):
    width = x_ref.shape[1]
    for i, (facts, x) in enumerate(((info_ref, x_ref), (info2_ref, x2_ref))):
        slot_tables(top, half, capacity, first_ref[0], facts[...], pick_ref)
        rows = dot(pick_ref[...].astype(BF16), x[...], ((1,), (0,)))
        out_ref[:, i * width : (i + 1) * width] = rows.astype(BF16)


def mix_kernel(top, half, capacity, first_ref, info_ref, back_ref, *rest):
    far_refs, (out_ref, pick_ref, weight_ref) = rest[:-3], rest[-3:]
    slot_tables(top, half, capacity, first_ref[0], info_ref[...], pick_ref, weight_ref)
    weight = weight_ref[...]
    high = weight.astype(BF16)
    low = (weight - high.astype(F32)).astype(BF16)
    back = back_ref[...]
    total = dot(high, back, ((0,), (0,))) + dot(low, back, ((0,), (0,)))
    for far in far_refs:
        total = total + far[...].astype(F32)
    out_ref[...] = total.astype(BF16)


def halve_kernel(core_ref, x_ref, out_ref):
    width = out_ref.shape[1]
    out_ref[...] = x_ref[:, pl.ds(pl.multiple_of(core_ref[0] * width, LANES), width)]


def add_kernel(a_ref, b_ref, out_ref):
    out_ref[...] = (a_ref[...].astype(F32) + b_ref[...].astype(F32)).astype(BF16)


def spans_of(at_ref, first, count, width):
    return [pl.ds(pl.multiple_of(at_ref[first + i], LANES), width) for i in range(count)]


def copier(sems):
    started = []

    def copy(src, dst):
        started.append(pltpu.make_async_copy(src, dst, sems.at[len(started)]))
        started[-1].start()
        return started[-1]

    return copy


def block(ref, j, step):
    return ref.at[pl.ds(j * step, step)]


def stacked(copy, srcs, dst, begin=0):
    slots, width = dst.shape[0] // 2, dst.shape[1]
    if len(srcs) == 1:
        views = [srcs[0].at[:, pl.ds(i * width, width)] for i in range(2)]
    else:
        views = [src.at[:, pl.ds(begin, width)] for src in srcs]
    return [copy(view, block(dst, i, slots)) for i, view in enumerate(views)]


def forward_kernel(pieces, out_pieces, step, at_ref, *refs):
    n = pieces
    xs_in, weights_in, refs = refs[: 2 * n], refs[2 * n : 2 * n + 3], refs[2 * n + 3 :]
    outs, refs = refs[: 3 + 2 * out_pieces], refs[3 + 2 * out_pieces :]
    xs, (gate_w, up_w, down_w), refs = refs[:n], refs[n : n + 3], refs[n + 3 :]
    (keep_gate, keep_up, hidden_ref), own, sems = refs[:3], refs[3:-1], refs[-1]
    copy = copier(sems)
    slots, width = own[0].shape
    spans = spans_of(at_ref, 0, n, xs[0].shape[1])
    out_spans = spans_of(at_ref, n, out_pieces, width)
    blocks = gate_w.shape[0] // step
    x_copies = [started for i, dst in enumerate(xs) for started in stacked(copy, xs_in[i::n], dst)]
    gate_copies, up_copies = [], []
    for j in range(blocks):
        gate_copies.append(copy(block(weights_in[0], j, step), block(gate_w, j, step)))
        up_copies.append(copy(block(weights_in[1], j, step), block(up_w, j, step)))
    down_copy = copy(weights_in[2], down_w)
    for started in x_copies:
        started.wait()
    for j in range(blocks):
        gate_copies[j].wait()
        up_copies[j].wait()
        units = slice(j * step, (j + 1) * step)
        gate = sum(dot(x[...], gate_w[units, span], ((1,), (1,))) for x, span in zip(xs, spans))
        up = sum(dot(x[...], up_w[units, span], ((1,), (1,))) for x, span in zip(xs, spans))
        s = jax.nn.sigmoid(gate)
        silu = gate * s
        keep_gate[:, units] = (up * s * (1.0 + gate * (1.0 - s))).astype(BF16)
        keep_up[:, units] = silu.astype(BF16)
        hidden_ref[:, units] = (silu * up).astype(BF16)
    out_copies = [copy(src, dst) for src, dst in zip((keep_gate, keep_up, hidden_ref), outs[:3])]
    down_copy.wait()
    for i in reversed(range(out_pieces)):
        both = dot(hidden_ref[...], down_w[:, out_spans[i]], ((1,), (0,))).astype(BF16)
        own[i][...] = both[:slots]
        out_copies.append(copy(own[i], outs[3 + out_pieces + i]))
        outs[3 + i][...] = both[slots:]
    for started in out_copies:
        started.wait()


def gradients_kernel(pieces, cot_pieces, capacity, scale, step, at_ref, *refs):
    n, m = pieces, cot_pieces
    cots_in, toks_in, refs = refs[:m], refs[m : m + 2 * n], refs[m + 2 * n :]
    rows_in, inputs, refs = refs[:2], refs[2:6], refs[6:]
    outs, cots, toks, refs = refs[:3], refs[3 : 3 + m], refs[3 + m : 3 + m + n], refs[3 + m + n :]
    down_w, keep_gate, keep_up, hidden, dgate, dup, facts_ref, turned, held, sems = refs
    copy = copier(sems)
    spans = spans_of(at_ref, 0, n, toks[0].shape[1])
    spans = spans_of(at_ref, n, m, cots[0].shape[1])
    facts_copies = stacked(copy, rows_in, facts_ref, rows_in[0].shape[1] - LANES)
    hidden_copy = copy(inputs[3], hidden)
    cot_copies = [stacked(copy, [src], dst) for src, dst in zip(cots_in, cots)]
    down_copy = copy(inputs[0], down_w)
    keep_copies = [copy(inputs[1], keep_gate), copy(inputs[2], keep_up)]
    tok_copies = [stacked(copy, toks_in[i::n], dst) for i, dst in enumerate(toks)]
    for started in facts_copies:
        started.wait()
    facts = facts_ref[...].astype(F32)
    total = jnp.zeros((1, LANES), F32)
    for row in range(0, facts.shape[0], capacity):
        total = total + facts[row : row + 1, :]
    coefficient = scale * (facts[:, 3:4] / total[:, 5:6] - facts[:, 4:5] / total[:, 6:7])
    slot_weight = coefficient * (facts[:, 0:1] + facts[:, 1:2] + facts[:, 2:3])
    for i in range(m):
        for started in cot_copies[i]:
            started.wait()
        cots[i][...] = (slot_weight * cots[i][...].astype(F32)).astype(BF16)
    done = [[] for _ in range(max(n, m))]
    written = []

    def outer(left, xs, spans, copies, k):
        turned[...] = left[...].T
        for i, (x, span) in enumerate(zip(xs, spans)):
            for started in copies[i]:
                started.wait()
            width = x.shape[1]
            place = slice(i * width, (i + 1) * width)
            held[k, :, place] = dot(turned[...], x[...], ((1,), (0,))).astype(BF16)
            written.append(copy(held.at[k, :, pl.ds(i * width, width)], outs[k].at[:, span]))

    hidden_copy.wait()
    outer(hidden, cots, spans, done, 2)
    down_copy.wait()
    for started in keep_copies:
        started.wait()
    for begin in range(0, down_w.shape[0], step):
        units = slice(begin, begin + step)
        dhidden = sum(dot(x[...], down_w[units, span], ((1,), (1,))) for x, span in zip(cots, spans))
        dgate[:, units] = (dhidden * keep_gate[:, units].astype(F32)).astype(BF16)
        dup[:, units] = (dhidden * keep_up[:, units].astype(F32)).astype(BF16)
    outer(dgate, toks, spans, tok_copies, 0)
    outer(dup, toks, spans, done, 1)
    for started in written:
        started.wait()


def body(
    tokens,
    cotangent,
    expert_ids,
    route_weight,
    forget_mask,
    lengths,
    gate_weight,
    up_weight,
    down_weight,
):
    tok_rows, features = tokens.shape
    top = expert_ids.shape[1]
    owners = lax.axis_size("dp")
    parts = lax.axis_size("tensor")
    half = owners // 2
    width = features // parts
    capacity = 5 * tok_rows * top // (4 * owners)
    slots = half * capacity
    seq_len = tok_rows * owners // lengths.shape[0]
    me = lax.axis_index("dp")
    core = lax.axis_index("tensor")
    mates = [(i, (i + half) % owners) for i in range(owners)]
    halves = [list(range(half)), list(range(half, owners))]
    first = ((me // half) * half).astype(jnp.int32).reshape(1)
    place = (me * tok_rows).astype(jnp.int32).reshape(1)
    shape = jax.ShapeDtypeStruct
    table = pltpu.VMEM((slots, tok_rows), F32)
    limit = pltpu.CompilerParams(vmem_limit_bytes=8 * 2**20)

    def to_mate(value):
        return lax.ppermute(value, "dp", mates)

    def exchange(value):
        value = value.reshape(half, value.shape[0] // half, value.shape[1])
        return lax.all_to_all(
            value, "dp", split_axis=0, concat_axis=0, axis_index_groups=halves, tiled=True
        )

    def swapped(value):
        return lax.ppermute(value, "tensor", [(0, 1), (1, 0)])

    def my_features(value, micros):
        return pl.pallas_call(
            halve_kernel,
            out_shape=shape((tok_rows, width), BF16),
            in_specs=[SMEM, VMEM],
            out_specs=VMEM,
            compiler_params=limit,
            cost_estimate=cost(micros),
        )(core.astype(jnp.int32).reshape(1), value)

    def after(value, *others):
        return lax.optimization_barrier((value, *others))[0]

    def mixed_rows(info, back, *far):
        return pl.pallas_call(
            functools.partial(mix_kernel, top, half, capacity),
            out_shape=jax.ShapeDtypeStruct((tok_rows, width), BF16),
            in_specs=[SMEM, VMEM, VMEM] + [VMEM] * len(far),
            out_specs=VMEM,
            scratch_shapes=[table, table],
            compiler_params=limit,
            cost_estimate=cost(1),
        )(first, info, back, *far)

    tok_mine = my_features(tokens, 1)
    tok_mate = to_mate(tok_mine)
    expert_ids = after(expert_ids, tok_mine)
    about = pl.pallas_call(
        functools.partial(facts_kernel, top, seq_len),
        out_shape=jax.ShapeDtypeStruct((FACTS, tok_rows), F32),
        in_specs=[SMEM, SMEM, VMEM, VMEM, VMEM],
        out_specs=VMEM,
        compiler_params=limit,
        cost_estimate=cost(1),
    )(place, lengths, expert_ids.T, route_weight.T, forget_mask.reshape(1, tok_rows))
    about_mate = to_mate(about)

    def gathered(info, x, micros):
        return pl.pallas_call(
            functools.partial(gather_kernel, top, half, capacity),
            out_shape=shape((slots, width + LANES), BF16),
            in_specs=[SMEM, VMEM, VMEM],
            out_specs=VMEM,
            scratch_shapes=[table, table],
            compiler_params=limit,
            cost_estimate=cost(micros),
        )(first, info, x)

    recv_own = exchange(gathered(about, tok_mine, 1)).reshape(slots, width + LANES)
    send_mate = gathered(about_mate, tok_mate, 20)
    recv_mate = exchange(after(send_mate, recv_own)).reshape(slots, width + LANES)

    cot_mine = my_features(after(cotangent, about), 1)
    cot_mate = to_mate(after(cot_mine, tok_mate))
    send_cot = pl.pallas_call(
        functools.partial(cot_kernel, top, half, capacity),
        out_shape=shape((slots, 2 * width), BF16),
        in_specs=[SMEM] + [VMEM] * 4,
        out_specs=VMEM,
        scratch_shapes=[table],
        compiler_params=limit,
        cost_estimate=cost(15),
    )(first, about, about_mate, cot_mine, cot_mate)
    recv_own, recv_mate = after(recv_own, send_cot), after(recv_mate, send_cot)
    recv_cot = exchange(after(send_cot, recv_mate)).reshape(slots, 2 * width)

    gate_w, up_w, down_w = gate_weight[0], up_weight[0], down_weight[0]
    weights = [in_hbm(w) for w in (gate_w, up_w, down_w)]
    units = gate_w.shape[0]
    step = min(units, 256)
    blocks = units // step

    def all_features(row):
        return lax.all_gather(row, "tensor", axis=1, tiled=True)

    if parts == 2:
        other_own = swapped(recv_own)
        toks = [recv_own, other_own, recv_mate, swapped(after(recv_mate, other_own))]
        starts = [core * width, (1 - core) * width] * 2
        span = width
    else:
        toks = [all_features(recv_own[:, :width]), all_features(recv_mate[:, :width])]
        starts = [core * 0] * 2
        span = features
    at = jnp.stack(starts).astype(jnp.int32)
    toks = [in_hbm(x) for x in toks]
    n = m = len(toks) // 2
    weight_buffer = pltpu.VMEM((units, features), BF16)
    unit_rows = ((2 * slots, units), BF16)
    tok_buffers = [pltpu.VMEM((2 * slots, span), BF16)] * n
    cot_buffers = [pltpu.VMEM((2 * slots, span), BF16)] * m
    roomy = pltpu.CompilerParams(vmem_limit_bytes=36 * 2**20)

    def summed(outs):
        if parts != 2:
            return lax.psum_scatter(outs[0], "tensor", scatter_dimension=1, tiled=True)
        return pl.pallas_call(
            add_kernel,
            out_shape=shape((slots, width), BF16),
            in_specs=[VMEM] * 2,
            out_specs=VMEM,
            compiler_params=limit,
            cost_estimate=cost(1),
        )(outs[0], swapped(outs[1]))

    piece = (slots, span)
    keep_gate, keep_up, hidden, *outs = pl.pallas_call(
        functools.partial(forward_kernel, n, m, step),
        out_shape=[pltpu.HBM(*unit_rows)] * 3
        + [shape(piece, BF16)] * m
        + [pltpu.HBM(piece, BF16)] * m,
        in_specs=[SMEM] + [HBM] * (2 * n + 3),
        out_specs=[HBM] * 3 + [VMEM] * m + [HBM] * m,
        scratch_shapes=tok_buffers
        + [weight_buffer] * 3
        + [pltpu.VMEM(*unit_rows)] * 3
        + [pltpu.VMEM(piece, BF16)] * m
        + [pltpu.SemaphoreType.DMA((2 * n + 2 * blocks + 4 + m,))],
        compiler_params=roomy,
        cost_estimate=cost(8),
    )(at, *toks, *weights)
    out_mate = summed(outs[:m])
    back_mate = exchange(out_mate).reshape(slots, width)
    out_own = summed(outs[m:])

    recv_cot = after(recv_cot, out_mate)
    if parts == 2:
        cots = [recv_cot, swapped(recv_cot)]
    else:
        both = [all_features(recv_cot[:, :width]), all_features(recv_cot[:, width:])]
        cots = [jnp.concatenate(both, axis=1)]
    mix_mate = mixed_rows(about_mate, back_mate)
    mix_far = to_mate(mix_mate)
    keeps = [in_hbm(x) for x in (keep_gate, keep_up, after(hidden, mix_mate))]
    grad_gate, grad_up, grad_down = pl.pallas_call(
        functools.partial(gradients_kernel, n, m, capacity, float(top * tok_rows), step),
        out_shape=[pltpu.HBM((units, features), BF16)] * 3,
        in_specs=[SMEM] + [HBM] * (2 * n + m + 6),
        out_specs=[HBM] * 3,
        scratch_shapes=cot_buffers
        + tok_buffers
        + [weight_buffer]
        + [pltpu.VMEM(*unit_rows)] * 5
        + [
            pltpu.VMEM((2 * slots, LANES), BF16),
            pltpu.VMEM((units, 2 * slots), BF16),
            pltpu.VMEM((3, units, features), BF16),
            pltpu.SemaphoreType.DMA((4 * n + 3 * m + 6,)),
        ],
        compiler_params=roomy,
        cost_estimate=cost(20),
    )(at, *[in_hbm(x) for x in cots], *toks, in_hbm(recv_own), in_hbm(recv_mate), weights[2], *keeps)
    back_own = exchange(after(out_own, mix_mate)).reshape(slots, width)
    mixed = mixed_rows(about, back_own, mix_far)
    return (
        mixed,
        grad_gate[None],
        grad_up[None],
        grad_down[None],
    )


def solution(mesh):
    in_specs = (
        P("dp", None),
        P("dp", None),
        P("dp", None),
        P("dp", None),
        P("dp"),
        P(),
        P("dp", "tensor", None),
        P("dp", "tensor", None),
        P("dp", "tensor", None),
    )
    out_specs = (
        P("dp", "tensor"),
        P("dp", "tensor", None),
        P("dp", "tensor", None),
        P("dp", "tensor", None),
    )
    return jax.shard_map(body, mesh=mesh, in_specs=in_specs, out_specs=out_specs, check_vma=False)
```

time: 108 us -> 102 us (0.944)
  waiting for transfers between devices: 31.3 us -> 46.3 us
  Pallas kernels: 39.3 us -> 28.7 us
  starting transfers between devices: 33.9 us -> 25.1 us
  local copies, waits for them, and re-layouts: 2.18 us -> 1.09 us
    all_to_all x5, waiting for transfers between devices: 3.19 us -> 35 us  [exchange(): lax.all_to_all(value, 'dp', split_axis=0, concat_axis=0, axis_index_group...]
    ppermute x5 -> x4, waiting for transfers between devices: 21.3 us -> 5.3 us  [to_mate(): return lax.ppermute(value, 'dp', mates)]
    pallas_call x9 -> x7, Pallas kernels: 34.7 us -> 24.1 us  [the longest x1 11 us: body(): pl.pallas_call(functools.partial(gradients_kernel, n, m, capacity, float(...]
    all_to_all x5, starting transfers between devices: 25.2 us -> 19.6 us  [exchange(): lax.all_to_all(value, 'dp', split_axis=0, concat_axis=0, axis_index_group...]
    ppermute x5 -> x4, starting transfers between devices: 7.72 us -> 4.64 us  [to_mate(): return lax.ppermute(value, 'dp', mates)]
    unnamed x26 -> x20, local copies, waits for them, and re-layouts: 2.18 us -> 1.09 us
  transfers between devices with their start and end apart: 15 -> 14, of which waited for: 8 -> 10; matrix products, arithmetic and copies ran while one was open for 0% -> 0% of each run, Pallas kernels for 33% -> 27%
where the time goes in v3:
time: 102 us
  waiting for transfers between devices  46.3 us (45%)
  Pallas kernels  28.7 us (28%)
  starting transfers between devices  25.1 us (25%)
  local copies, waits for them, and re-layouts  1.09 us (1%)
    all_to_all x5, waiting for transfers between devices, exchange(): lax.all_to_all(value, 'dp', split_axis=0, concat_axis=0, axis_index_group...  35 us
    all_to_all x5, starting transfers between devices, exchange(): lax.all_to_all(value, 'dp', split_axis=0, concat_axis=0, axis_index_group...  19.6 us
    pallas_call x1, Pallas kernels, body(): pl.pallas_call(functools.partial(gradients_kernel, n, m, capacity, float(...  11 us
    pallas_call x1, Pallas kernels, body(): pl.pallas_call(functools.partial(forward_kernel, n, m, step), out_shape=[...  8.6 us
    ppermute x5, waiting for transfers between devices, swapped(): return lax.ppermute(value, 'tensor', [(0, 1), (1, 0)])  5.95 us
    ppermute x4, waiting for transfers between devices, to_mate(): return lax.ppermute(value, 'dp', mates)  5.3 us
    ppermute x4, starting transfers between devices, to_mate(): return lax.ppermute(value, 'dp', mates)  4.64 us
    pallas_call x2, Pallas kernels, gathered(): pl.pallas_call(functools.partial(gather_kernel, top, half, capacity), out...  2.65 us
  transfers between devices with their start and end apart: 14, of which 10 were waited for; matrix products, arithmetic and copies ran while one was open for 0% of the time, Pallas kernels for 27%

profile of v3, /device:TPU:0, one launch (start us, length us, event | category | flops | bytes accessed | tf_op | source)
XLA Modules:
  0.0 102.0 jit_solution(4755137130882369864)
XLA Ops:
  0.6 0.0 copy-start.2
  0.6 0.0 copy-start.4
  0.7 0.0 copy-start.5
  0.7 0.0 copy-start.3
  0.7 0.0 copy-start
  0.7 1.1 %copy-done = bf16[128,2048]{1,0:T(8,128)(2,1)S(1)} copy-done((bf16[128,2048]{1,0:T(8,128)(2,1)S(1)}, bf16[128,2048]{1,0:T(8,128)(2,1)}, u32[]{:S(2)}) %copy-start) | copy-done | bytes 524312
  1.8 4.1 %collective-permute-start.1 = (bf16[128,1024]{1,0:T(8,128)(2,1)S(1)}, bf16[128,1024]{1,0:T(8,128)(2,1)S(1)}, u32[]{:S(2)}, u32[]{:S(2)}) collective-permute-start(bf16[128,1024]{1,0:T(8,128)(2,1)S(1)} %shard_map.120.x_ref), channel_id=1, source_target_pairs={{0,16},{2,18},{4,20},{6,22},{8,24},{10,26},{12,28},{14,30},{16,0},... | collective-permute-start | bytes 786440 | tf_op jit(solution)/shard_map/ppermute | solution.py:283
  5.9 0.0 copy-done.2
  5.9 0.0 copy-done.4
  5.9 0.0 copy-done.5
  5.9 0.0 copy-done.3
  5.9 0.6 shard_map.121.info_ref
  6.4 0.1 collective-permute-start
  6.5 0.0 copy-start.1
  6.5 1.3 %shard_map.122 = bf16[320,1152]{1,0:T(8,128)(2,1)} custom-call(s32[1]{0:T(128)} %bitcast.first_ref, f32[16,128]{1,0:T(8,128)S(1)} %shard_map.121.info_ref, bf16[128,1024]{1,0:T(8,128)(2,1)S(1)} %shard_map.120.x_ref), custom_call_target="tpu_custom_call" | custom-call | flops 1000000000 | bytes 3000000 | tf_op jit(solution)/shard_map/pallas_call | solution.py:332
  7.9 5.0 %all-to-all-start = ((bf16[8,40,1152]{2,1,0:T(8,128)(2,1)}), bf16[8,40,1152]{2,1,0:T(8,128)(2,1)}, u32[]{:S(2)}, u32[]{:S(2)}) async-start(bf16[8,40,1152]{2,1,0:T(8,128)(2,1)} %bitcast.8), calls=%async_computation | async-start | bytes 1474560 | tf_op jit(solution)/shard_map/all_to_all | solution.py:287
  12.9 0.0 copy-done.1
  12.9 5.2 %collective-permute-done.1.x_ref = bf16[128,1024]{1,0:T(8,128)(2,1)S(1)} collective-permute-done((bf16[128,1024]{1,0:T(8,128)(2,1)S(1)}, bf16[128,1024]{1,0:T(8,128)(2,1)S(1)}, u32[]{:S(2)}, u32[]{:S(2)}) %collective-permute-start.1) | collective-permute-done | bytes 262176 | tf_op jit(solution)/shard_map/ppermute | solution.py:283
  18.1 0.0 collective-permute-start.2
  18.1 0.1 collective-permute-done.info2_ref.info_ref
  18.2 1.3 %shard_map.125 = bf16[320,1152]{1,0:T(8,128)(2,1)} custom-call(s32[1]{0:T(128)} %bitcast.first_ref, f32[16,128]{1,0:T(8,128)S(1)} %collective-permute-done.info2_ref.info_ref, bf16[128,1024]{1,0:T(8,128)(2,1)S(1)} %collective-permute-done.1.x_ref), custom_call_target="tpu_custom_call" | custom-call | flops 20000000000 | bytes 60000000 | tf_op jit(solution)/shard_map/pallas_call | solution.py:332
  19.6 10.9 %all-to-all-done = bf16[8,40,1152]{2,1,0:T(8,128)(2,1)} async-done(((bf16[8,40,1152]{2,1,0:T(8,128)(2,1)}), bf16[8,40,1152]{2,1,0:T(8,128)(2,1)}, u32[]{:S(2)}, u32[]{:S(2)}) %all-to-all-start) | async-done | bytes 737312 | tf_op jit(solution)/shard_map/all_to_all | solution.py:287
  30.4 3.7 %all-to-all-start.1 = ((bf16[8,40,1152]{2,1,0:T(8,128)(2,1)}), bf16[8,40,1152]{2,1,0:T(8,128)(2,1)S(1)}, u32[]{:S(2)}, u32[]{:S(2)}) async-start(bf16[8,40,1152]{2,1,0:T(8,128)(2,1)} %bitcast.10), calls=%async_computation.1 | async-start | bytes 1474560 | tf_op jit(solution)/shard_map/all_to_all | solution.py:287
  34.1 0.0 collective-permute-done.2.x2_ref
  34.1 1.8 %shard_map.124 = bf16[320,2048]{1,0:T(8,128)(2,1)} custom-call(s32[1]{0:T(128)} %bitcast.first_ref, f32[16,128]{1,0:T(8,128)S(1)} %shard_map.121.info_ref, f32[16,128]{1,0:T(8,128)S(1)} %collective-permute-done.info2_ref.info_ref, bf16[128,1024]{1,0:T(8,128)(2,1)S(1)} %shard_map.123.x_ref, bf16[128,1024]{1,0:T(8,128)(2,1)S(1)} %collective-permute-done.2.x2_ref), custom_call_target="tpu_custom_call" | custom-call | flops 15000000512 | bytes 45000000 | tf_op jit(solution)/shard_map/pallas_call | solution.py:348
  35.9 0.0 collective-permute-start.3
  35.9 9.5 %all-to-all-done.1 = bf16[8,40,1152]{2,1,0:T(8,128)(2,1)S(1)} async-done(((bf16[8,40,1152]{2,1,0:T(8,128)(2,1)}), bf16[8,40,1152]{2,1,0:T(8,128)(2,1)S(1)}, u32[]{:S(2)}, u32[]{:S(2)}) %all-to-all-start.1) | async-done | bytes 737312 | tf_op jit(solution)/shard_map/all_to_all | solution.py:287
  45.5 0.0 copy-start.8
  45.5 3.6 %all-to-all-start.4 = ((bf16[8,40,2048]{2,1,0:T(8,128)(2,1)}), bf16[8,40,2048]{2,1,0:T(8,128)(2,1)S(1)}, u32[]{:S(2)}, u32[]{:S(2)}) async-start(bf16[8,40,2048]{2,1,0:T(8,128)(2,1)} %bitcast.19), calls=%async_computation.4 | async-start | bytes 2621440 | tf_op jit(solution)/shard_map/all_to_all | solution.py:287
  49.1 0.0 collective-permute-done.3.refs_1_.refs_3_
  49.1 0.1 collective-permute-start.4
  49.1 0.1 pad_add_fusion.at_ref
  49.2 2.2 %collective-permute-done.4.refs_3_.refs_5_ = bf16[320,1152]{1,0:T(8,128)(2,1)} collective-permute-done((bf16[320,1152]{1,0:T(8,128)(2,1)S(1)}, bf16[320,1152]{1,0:T(8,128)(2,1)}, u32[]{:S(2)}, u32[]{:S(2)}) %collective-permute-start.4) | collective-permute-done | bytes 737312 | tf_op jit(solution)/shard_map/ppermute | solution.py:292
  51.5 0.0 copy-done.8
  51.5 8.6 %shard_map.126 = (bf16[640,512]{1,0:T(8,128)(2,1)}, bf16[640,512]{1,0:T(8,128)(2,1)}, bf16[640,512]{1,0:T(8,128)(2,1)}, bf16[320,1024]{1,0:T(8,128)(2,1)S(1)}, b...) custom-call(s32[4]{0:T(128)S(1)} %pad_add_fusion.at_ref, ...), custom_call_target="tpu_custom_call" | custom-call | flops 8000000000 | bytes 24000000 | tf_op jit(solution)/shard_map/pallas_call | solution.py:400
  60.1 0.2 collective-permute-start.6
  60.3 2.0 %collective-permute-done.6.b_ref = bf16[320,1024]{1,0:T(8,128)(2,1)S(1)} collective-permute-done((bf16[320,1024]{1,0:T(8,128)(2,1)S(1)}, bf16[320,1024]{1,0:T(8,128)(2,1)S(1)}, u32[]{:S(2)}, u32[]{:S(2)}) %collective-permute-start.6) | collective-permute-done | bytes 655392 | tf_op jit(solution)/shard_map/ppermute | solution.py:292
  62.2 0.0 copy-start.9
  62.2 0.0 copy-start.6
  62.3 1.1 %shard_map.128 = bf16[320,1024]{1,0:T(8,128)(2,1)} custom-call(bf16[320,1024]{1,0:T(8,128)(2,1)S(1)} %get-tuple-element.34.a_ref, bf16[320,1024]{1,0:T(8,128)(2,1)S(1)} %collective-permute-done.6.b_ref), custom_call_target="tpu_custom_call" | custom-call | flops 1000000000 | bytes 3000000 | tf_op jit(solution)/shard_map/pallas_call | solution.py:390
  63.3 3.0 %all-to-all-done.4 = bf16[8,40,2048]{2,1,0:T(8,128)(2,1)S(1)} async-done(((bf16[8,40,2048]{2,1,0:T(8,128)(2,1)}), bf16[8,40,2048]{2,1,0:T(8,128)(2,1)S(1)}, u32[]{:S(2)}, u32[]{:S(2)}) %all-to-all-start.4) | async-done | bytes 1310752 | tf_op jit(solution)/shard_map/all_to_all | solution.py:287
  66.3 0.0 copy-start.7
  66.3 0.0 collective-permute-start.8
  66.3 3.5 %all-to-all-start.2 = ((bf16[8,40,1024]{2,1,0:T(8,128)(2,1)}), bf16[8,40,1024]{2,1,0:T(8,128)(2,1)S(1)}, u32[]{:S(2)}, u32[]{:S(2)}) async-start(bf16[8,40,1024]{2,1,0:T(8,128)(2,1)} %bitcast.15), calls=%async_computation.2 | async-start | bytes 1310720 | tf_op jit(solution)/shard_map/all_to_all | solution.py:287
  69.8 0.0 copy-done.9
  69.8 0.6 collective-permute-start.5
  70.4 1.7 %collective-permute-done.5.b_ref = bf16[320,1024]{1,0:T(8,128)(2,1)S(1)} collective-permute-done((bf16[320,1024]{1,0:T(8,128)(2,1)S(1)}, bf16[320,1024]{1,0:T(8,128)(2,1)S(1)}, u32[]{:S(2)}, u32[]{:S(2)}) %collective-permute-start.5) | collective-permute-done | bytes 655392 | tf_op jit(solution)/shard_map/ppermute | solution.py:292
  72.1 0.0 copy-done.6
  72.1 1.1 %shard_map.127 = bf16[320,1024]{1,0:T(8,128)(2,1)} custom-call(bf16[320,1024]{1,0:T(8,128)(2,1)S(1)} %copy-done.6, bf16[320,1024]{1,0:T(8,128)(2,1)S(1)} %collective-permute-done.5.b_ref), custom_call_target="tpu_custom_call" | custom-call | flops 1000000000 | bytes 3000000 | tf_op jit(solution)/shard_map/pallas_call | solution.py:390
  73.2 0.0 copy-done.7
  73.2 7.8 %all-to-all-done.2 = bf16[8,40,1024]{2,1,0:T(8,128)(2,1)S(1)} async-done(((bf16[8,40,1024]{2,1,0:T(8,128)(2,1)}), bf16[8,40,1024]{2,1,0:T(8,128)(2,1)S(1)}, u32[]{:S(2)}, u32[]{:S(2)}) %all-to-all-start.2) | async-done | bytes 655392 | tf_op jit(solution)/shard_map/all_to_all | solution.py:287
  81.0 0.6 shard_map.129
  81.6 0.4 collective-permute-start.7
  82.1 3.7 %all-to-all-start.3 = ((bf16[8,40,1024]{2,1,0:T(8,128)(2,1)}), bf16[8,40,1024]{2,1,0:T(8,128)(2,1)S(1)}, u32[]{:S(2)}, u32[]{:S(2)}) async-start(bf16[8,40,1024]{2,1,0:T(8,128)(2,1)} %bitcast.17), calls=%async_computation.3 | async-start | bytes 1310720 | tf_op jit(solution)/shard_map/all_to_all | solution.py:287
  85.8 0.0 collective-permute-done.8.refs_1_
  85.8 11.0 %shard_map.131 = (bf16[512,2048]{1,0:T(8,128)(2,1)}, bf16[512,2048]{1,0:T(8,128)(2,1)}, bf16[512,2048]{1,0:T(8,128)(2,1)}) custom-call(s32[4]{0:T(128)S(1)} %pad_add_fusion.at_ref, bf16[320,2048]{1,0:T(8,128)(2,1)} %bitcast.30, bf16[320,2048]{1,0:T(8,128)(2,1)} %collective-permute-done.8.refs_1_, bf16[320,1152]{1,0:T(8,128)(2,1)} %bitcast.9.refs_0_.refs_2_.refs_6_, ...), custom_call_target="tpu_custom_call" | custom-call | flops 20000000000 | bytes 60000000 | tf_op jit(solution)/shard_map/pallas_call | solution.py:428
  96.8 0.0 collective-permute-done.7.rest_0_
  96.8 3.8 %all-to-all-done.3 = bf16[8,40,1024]{2,1,0:T(8,128)(2,1)S(1)} async-done(((bf16[8,40,1024]{2,1,0:T(8,128)(2,1)}), bf16[8,40,1024]{2,1,0:T(8,128)(2,1)S(1)}, u32[]{:S(2)}, u32[]{:S(2)}) %all-to-all-start.3) | async-done | bytes 655392 | tf_op jit(solution)/shard_map/all_to_all | solution.py:287
  100.7 1.3 %shard_map.130 = bf16[128,1024]{1,0:T(8,128)(2,1)} custom-call(s32[1]{0:T(128)} %bitcast.first_ref, f32[16,128]{1,0:T(8,128)S(1)} %shard_map.121.info_ref, bf16[320,1024]{1,0:T(8,128)(2,1)S(1)} %bitcast.24, bf16[128,1024]{1,0:T(8,128)(2,1)S(1)} %collective-permute-done.7.rest_0_), custom_call_target="tpu_custom_call" | custom-call | flops 1000000000 | bytes 3000000 | tf_op jit(solution)/shard_map/pallas_call | solution.py:308
  (2 shorter events, 0.0 us)
Async XLA Ops:
  0.6 5.2 %copy-start.2 = (s32[128,4]{0,1:T(4,128)S(1)}, s32[128,4]{0,1:T(4,128)}, u32[]{:S(2)}) copy-start(s32[128,4]{0,1:T(4,128)} %param.11) | copy-start | bytes 6148
  0.6 5.2 %copy-start.4 = (s32[2]{0:T(128)S(1)}, s32[2]{0:T(128)}, u32[]{:S(2)}) copy-start(s32[2]{0:T(128)} %lengths_ref.1) | copy-start | bytes 28
  0.7 5.2 %copy-start.5 = (s32[128]{0:T(128)S(1)}, s32[128]{0:T(128)}, u32[]{:S(2)}) copy-start(s32[128]{0:T(128)} %param.13) | copy-start | bytes 1540
  0.7 5.2 %copy-start.3 = (f32[128,4]{0,1:T(4,128)S(1)}, f32[128,4]{0,1:T(4,128)}, u32[]{:S(2)}) copy-start(f32[128,4]{0,1:T(4,128)} %param.12) | copy-start | bytes 6148
  0.7 1.1 %copy-start = (bf16[128,2048]{1,0:T(8,128)(2,1)S(1)}, bf16[128,2048]{1,0:T(8,128)(2,1)}, u32[]{:S(2)}) copy-start(bf16[128,2048]{1,0:T(8,128)(2,1)} %x_ref.1) | copy-start | bytes 1572868
  1.8 16.4 %collective-permute-start.1 = (bf16[128,1024]{1,0:T(8,128)(2,1)S(1)}, bf16[128,1024]{1,0:T(8,128)(2,1)S(1)}, u32[]{:S(2)}, u32[]{:S(2)}) collective-permute-start(bf16[128,1024]{1,0:T(8,128)(2,1)S(1)} %shard_map.120.x_ref), channel_id=1, source_target_pairs={{0,16},{2,18},{4,20},{6,22},{8,24},{10,26},{12,28},{14,30},{16,0},... | collective-permute-start | bytes 786440 | tf_op jit(solution)/shard_map/ppermute | solution.py:283
  6.4 11.8 %collective-permute-start = (f32[16,128]{1,0:T(8,128)S(1)}, f32[16,128]{1,0:T(8,128)S(1)}, u32[]{:S(2)}, u32[]{:S(2)}) collective-permute-start(f32[16,128]{1,0:T(8,128)S(1)} %shard_map.121.info_ref), channel_id=1, source_target_pairs={{0,16},{2,18},{4,20},{6,22},{8,24},{10,26},{12,28},{14,30},{16,0},... | collective-permute-start | bytes 24584 | tf_op jit(solution)/shard_map/ppermute | solution.py:283
  6.5 6.4 %copy-start.1 = (bf16[128,2048]{1,0:T(8,128)(2,1)S(1)}, bf16[128,2048]{1,0:T(8,128)(2,1)}, u32[]{:S(2)}) copy-start(bf16[128,2048]{1,0:T(8,128)(2,1)} %x_ref.2) | copy-start | bytes 1572868
  7.9 22.5 %all-to-all-start = ((bf16[8,40,1152]{2,1,0:T(8,128)(2,1)}), bf16[8,40,1152]{2,1,0:T(8,128)(2,1)}, u32[]{:S(2)}, u32[]{:S(2)}) async-start(bf16[8,40,1152]{2,1,0:T(8,128)(2,1)} %bitcast.8), calls=%async_computation | async-start | bytes 1474560 | tf_op jit(solution)/shard_map/all_to_all | solution.py:287
  18.1 16.0 %collective-permute-start.2 = (bf16[128,1024]{1,0:T(8,128)(2,1)S(1)}, bf16[128,1024]{1,0:T(8,128)(2,1)S(1)}, u32[]{:S(2)}, u32[]{:S(2)}) collective-permute-start(bf16[128,1024]{1,0:T(8,128)(2,1)S(1)} %shard_map.123.x_ref), channel_id=1, source_target_pairs={{0,16},{2,18},{4,20},{6,22},{8,24},{10,26},{12,28},{14,30},{16,0},... | collective-permute-start | bytes 786440 | tf_op jit(solution)/shard_map/ppermute | solution.py:283
  30.4 15.1 %all-to-all-start.1 = ((bf16[8,40,1152]{2,1,0:T(8,128)(2,1)}), bf16[8,40,1152]{2,1,0:T(8,128)(2,1)S(1)}, u32[]{:S(2)}, u32[]{:S(2)}) async-start(bf16[8,40,1152]{2,1,0:T(8,128)(2,1)} %bitcast.10), calls=%async_computation.1 | async-start | bytes 1474560 | tf_op jit(solution)/shard_map/all_to_all | solution.py:287
  35.9 13.1 %collective-permute-start.3 = (bf16[320,1152]{1,0:T(8,128)(2,1)}, bf16[320,1152]{1,0:T(8,128)(2,1)}, u32[]{:S(2)}, u32[]{:S(2)}) collective-permute-start(bf16[320,1152]{1,0:T(8,128)(2,1)} %bitcast.9.refs_0_.refs_2_.refs_6_), channel_id=1, source_target_pairs={{0,1},{1,0},{2,3},{3,2},{4,5},{5,4},{6,7},{7,6},{8,9},{9,8},{10,11... | collective-permute-start | bytes 2211848 | tf_op jit(solution)/shard_map/ppermute | solution.py:292
  45.5 6.0 %copy-start.8 = (bf16[8,40,1152]{2,1,0:T(8,128)(2,1)}, bf16[8,40,1152]{2,1,0:T(8,128)(2,1)S(1)}, u32[]{:S(2)}) copy-start(bf16[8,40,1152]{2,1,0:T(8,128)(2,1)S(1)} %all-to-all-done.1) | copy-start | bytes 2211844
  45.5 20.8 %all-to-all-start.4 = ((bf16[8,40,2048]{2,1,0:T(8,128)(2,1)}), bf16[8,40,2048]{2,1,0:T(8,128)(2,1)S(1)}, u32[]{:S(2)}, u32[]{:S(2)}) async-start(bf16[8,40,2048]{2,1,0:T(8,128)(2,1)} %bitcast.19), calls=%async_computation.4 | async-start | bytes 2621440 | tf_op jit(solution)/shard_map/all_to_all | solution.py:287
  49.1 2.4 %collective-permute-start.4 = (bf16[320,1152]{1,0:T(8,128)(2,1)S(1)}, bf16[320,1152]{1,0:T(8,128)(2,1)}, u32[]{:S(2)}, u32[]{:S(2)}) collective-permute-start(bf16[320,1152]{1,0:T(8,128)(2,1)S(1)} %bitcast.31), channel_id=1, source_target_pairs={{0,1},{1,0},{2,3},{3,2},{4,5},{5,4},{6,7},{7,6},{8,9},{9,8},{10,11... | collective-permute-start | bytes 2211848 | tf_op jit(solution)/shard_map/ppermute | solution.py:292
  60.1 2.2 %collective-permute-start.6 = (bf16[320,1024]{1,0:T(8,128)(2,1)S(1)}, bf16[320,1024]{1,0:T(8,128)(2,1)S(1)}, u32[]{:S(2)}, u32[]{:S(2)}) collective-permute-start(bf16[320,1024]{1,0:T(8,128)(2,1)S(1)} %get-tuple-element.35), channel_id=1, source_target_pairs={{0,1},{1,0},{2,3},{3,2},{4,5},{5,4},{6,7},{7,6},{8,9},{9,8},{10,11... | collective-permute-start | bytes 1966088 | tf_op jit(solution)/shard_map/ppermute | solution.py:292
  62.2 7.6 %copy-start.9 = (bf16[320,1024]{1,0:T(8,128)(2,1)S(1)}, bf16[320,1024]{1,0:T(8,128)(2,1)}, u32[]{:S(2)}) copy-start(bf16[320,1024]{1,0:T(8,128)(2,1)} %get-tuple-element.33) | copy-start | bytes 1966084
  62.2 9.9 %copy-start.6 = (bf16[320,1024]{1,0:T(8,128)(2,1)S(1)}, bf16[320,1024]{1,0:T(8,128)(2,1)}, u32[]{:S(2)}) copy-start(bf16[320,1024]{1,0:T(8,128)(2,1)} %get-tuple-element.32.a_ref) | copy-start | bytes 1966084
  66.3 6.9 %copy-start.7 = (bf16[8,40,2048]{2,1,0:T(8,128)(2,1)}, bf16[8,40,2048]{2,1,0:T(8,128)(2,1)S(1)}, u32[]{:S(2)}) copy-start(bf16[8,40,2048]{2,1,0:T(8,128)(2,1)S(1)} %all-to-all-done.4) | copy-start | bytes 3932164
  66.3 19.5 %collective-permute-start.8 = (bf16[320,2048]{1,0:T(8,128)(2,1)S(1)}, bf16[320,2048]{1,0:T(8,128)(2,1)}, u32[]{:S(2)}, u32[]{:S(2)}) collective-permute-start(bf16[320,2048]{1,0:T(8,128)(2,1)S(1)} %bitcast.29), channel_id=1, source_target_pairs={{0,1},{1,0},{2,3},{3,2},{4,5},{5,4},{6,7},{7,6},{8,9},{9,8},{10,11... | collective-permute-start | bytes 3932168 | tf_op jit(solution)/shard_map/ppermute | solution.py:292
  66.3 14.7 %all-to-all-start.2 = ((bf16[8,40,1024]{2,1,0:T(8,128)(2,1)}), bf16[8,40,1024]{2,1,0:T(8,128)(2,1)S(1)}, u32[]{:S(2)}, u32[]{:S(2)}) async-start(bf16[8,40,1024]{2,1,0:T(8,128)(2,1)} %bitcast.15), calls=%async_computation.2 | async-start | bytes 1310720 | tf_op jit(solution)/shard_map/all_to_all | solution.py:287
  69.8 2.3 %collective-permute-start.5 = (bf16[320,1024]{1,0:T(8,128)(2,1)S(1)}, bf16[320,1024]{1,0:T(8,128)(2,1)S(1)}, u32[]{:S(2)}, u32[]{:S(2)}) collective-permute-start(bf16[320,1024]{1,0:T(8,128)(2,1)S(1)} %copy-done.9), channel_id=1, source_target_pairs={{0,1},{1,0},{2,3},{3,2},{4,5},{5,4},{6,7},{7,6},{8,9},{9,8},{10,11... | collective-permute-start | bytes 1966088 | tf_op jit(solution)/shard_map/ppermute | solution.py:292
  81.6 15.2 %collective-permute-start.7 = (bf16[128,1024]{1,0:T(8,128)(2,1)S(1)}, bf16[128,1024]{1,0:T(8,128)(2,1)S(1)}, u32[]{:S(2)}, u32[]{:S(2)}) collective-permute-start(bf16[128,1024]{1,0:T(8,128)(2,1)S(1)} %shard_map.129), channel_id=1, source_target_pairs={{0,16},{2,18},{4,20},{6,22},{8,24},{10,26},{12,28},{14,30},{16,0},... | collective-permute-start | bytes 786440 | tf_op jit(solution)/shard_map/ppermute | solution.py:283
  82.1 18.6 %all-to-all-start.3 = ((bf16[8,40,1024]{2,1,0:T(8,128)(2,1)}), bf16[8,40,1024]{2,1,0:T(8,128)(2,1)S(1)}, u32[]{:S(2)}, u32[]{:S(2)}) async-start(bf16[8,40,1024]{2,1,0:T(8,128)(2,1)} %bitcast.17), calls=%async_computation.3 | async-start | bytes 1310720 | tf_op jit(solution)/shard_map/all_to_all | solution.py:287

commit v4 on v3

--- a/solution.py
+++ b/solution.py
@@ -74,32 +74,31 @@
             weighted_ref[rows, :] = jnp.where(at, weight[e : e + 1, :], 0.0)
 
 
-def gather_kernel(top, half, capacity, first_ref, info_ref, x_ref, out_ref, pick_ref, weight_ref):
-    info = info_ref[...]
+def gather_kernel(top, half, capacity, first_ref, info_ref, x_ref, out_ref, pick_ref):
+    slot_tables(top, half, capacity, first_ref[0], info_ref[...], pick_ref)
+    out_ref[...] = dot(pick_ref[...].astype(BF16), x_ref[...], ((1,), (0,))).astype(BF16)
+
+
+def cot_kernel(top, half, capacity, first_ref, info_ref, info2_ref, x_ref, x2_ref, out_ref, pick_ref, weight_ref):
     width = x_ref.shape[1]
-    slot_tables(top, half, capacity, first_ref[0], info, pick_ref, weight_ref)
-    pick = pick_ref[...]
-    out_ref[:, :width] = dot(pick.astype(BF16), x_ref[...], ((1,), (0,))).astype(BF16)
-    share = jnp.sum(weight_ref[...], axis=1, keepdims=True)
-    high = share.astype(BF16).astype(F32)
-    middle = (share - high).astype(BF16).astype(F32)
-    flags = info[2 * top : 2 * top + 2, :]
-    marks = [jnp.sum(pick * flags[i : i + 1, :], axis=1, keepdims=True) for i in range(2)]
-    counts = jnp.sum(flags, axis=1, keepdims=True)
     lane = lax.broadcasted_iota(jnp.int32, (out_ref.shape[0], LANES), 1)
     facts = jnp.zeros((out_ref.shape[0], LANES), F32)
-    columns = [high, middle, share - high - middle, marks[0], marks[1], counts[0:1, :], counts[1:2, :]]
-    for i, column in enumerate(columns):
-        facts = jnp.where(lane == i, column, facts)
-    out_ref[:, width:] = facts.astype(BF16)
-
-
-def cot_kernel(top, half, capacity, first_ref, info_ref, info2_ref, x_ref, x2_ref, out_ref, pick_ref):
-    width = x_ref.shape[1]
-    for i, (facts, x) in enumerate(((info_ref, x_ref), (info2_ref, x2_ref))):
-        slot_tables(top, half, capacity, first_ref[0], facts[...], pick_ref)
-        rows = dot(pick_ref[...].astype(BF16), x[...], ((1,), (0,)))
+    for i, (info_in, x) in enumerate(((info_ref, x_ref), (info2_ref, x2_ref))):
+        info = info_in[...]
+        slot_tables(top, half, capacity, first_ref[0], info, pick_ref, weight_ref)
+        pick = pick_ref[...]
+        rows = dot(pick.astype(BF16), x[...], ((1,), (0,)))
         out_ref[:, i * width : (i + 1) * width] = rows.astype(BF16)
+        share = jnp.sum(weight_ref[...], axis=1, keepdims=True)
+        high = share.astype(BF16).astype(F32)
+        middle = (share - high).astype(BF16).astype(F32)
+        flags = info[2 * top : 2 * top + 2, :]
+        marks = [jnp.sum(pick * flags[k : k + 1, :], axis=1, keepdims=True) for k in range(2)]
+        counts = jnp.sum(flags, axis=1, keepdims=True)
+        columns = [high, middle, share - high - middle, marks[0], marks[1], counts[0:1, :], counts[1:2, :]]
+        for k, column in enumerate(columns):
+            facts = jnp.where(lane == i * LANES // 2 + k, column, facts)
+    out_ref[:, 2 * width :] = facts.astype(BF16)
 
 
 def mix_kernel(top, half, capacity, first_ref, info_ref, back_ref, *rest):
@@ -115,9 +114,12 @@
     out_ref[...] = total.astype(BF16)
 
 
-def halve_kernel(core_ref, x_ref, out_ref):
+def halve_kernel(core_ref, x_ref, out_ref, sem):
     width = out_ref.shape[1]
-    out_ref[...] = x_ref[:, pl.ds(pl.multiple_of(core_ref[0] * width, LANES), width)]
+    mine = pl.ds(pl.multiple_of(core_ref[0] * width, LANES), width)
+    copy = pltpu.make_async_copy(x_ref.at[:, mine], out_ref, sem)
+    copy.start()
+    copy.wait()
 
 
 def add_kernel(a_ref, b_ref, out_ref):
@@ -196,30 +198,39 @@
 def gradients_kernel(pieces, cot_pieces, capacity, scale, step, at_ref, *refs):
     n, m = pieces, cot_pieces
     cots_in, toks_in, refs = refs[:m], refs[m : m + 2 * n], refs[m + 2 * n :]
-    rows_in, inputs, refs = refs[:2], refs[2:6], refs[6:]
+    facts_in, inputs, refs = refs[0], refs[1:5], refs[5:]
     outs, cots, toks, refs = refs[:3], refs[3 : 3 + m], refs[3 + m : 3 + m + n], refs[3 + m + n :]
     down_w, keep_gate, keep_up, hidden, dgate, dup, facts_ref, turned, held, sems = refs
     copy = copier(sems)
     spans = spans_of(at_ref, 0, n, toks[0].shape[1])
     spans = spans_of(at_ref, n, m, cots[0].shape[1])
-    facts_copies = stacked(copy, rows_in, facts_ref, rows_in[0].shape[1] - LANES)
+    facts_copy = copy(facts_in.at[:, pl.ds(facts_in.shape[1] - LANES, LANES)], facts_ref)
     hidden_copy = copy(inputs[3], hidden)
     cot_copies = [stacked(copy, [src], dst) for src, dst in zip(cots_in, cots)]
     down_copy = copy(inputs[0], down_w)
     keep_copies = [copy(inputs[1], keep_gate), copy(inputs[2], keep_up)]
     tok_copies = [stacked(copy, toks_in[i::n], dst) for i, dst in enumerate(toks)]
-    for started in facts_copies:
-        started.wait()
+    facts_copy.wait()
     facts = facts_ref[...].astype(F32)
+    slots, side = facts.shape[0], LANES // 2
     total = jnp.zeros((1, LANES), F32)
-    for row in range(0, facts.shape[0], capacity):
+    for row in range(0, slots, capacity):
         total = total + facts[row : row + 1, :]
-    coefficient = scale * (facts[:, 3:4] / total[:, 5:6] - facts[:, 4:5] / total[:, 6:7])
-    slot_weight = coefficient * (facts[:, 0:1] + facts[:, 1:2] + facts[:, 2:3])
+    retain_all = total[:, 5:6] + total[:, side + 5 : side + 6]
+    forget_all = total[:, 6:7] + total[:, side + 6 : side + 7]
+
+    def weight_of(begin):
+        share, retain, forget = facts[:, begin : begin + 3], facts[:, begin + 3 : begin + 4], facts[:, begin + 4 : begin + 5]
+        coefficient = scale * (retain / retain_all - forget / forget_all)
+        return coefficient * (share[:, 0:1] + share[:, 1:2] + share[:, 2:3])
+
+    slot_weights = [weight_of(0), weight_of(side)]
     for i in range(m):
         for started in cot_copies[i]:
             started.wait()
-        cots[i][...] = (slot_weight * cots[i][...].astype(F32)).astype(BF16)
+        for part in range(2):
+            rows = slice(part * slots, (part + 1) * slots)
+            cots[i][rows, :] = (slot_weights[part] * cots[i][rows, :].astype(F32)).astype(BF16)
     done = [[] for _ in range(max(n, m))]
     written = []
 
@@ -295,11 +306,12 @@
         return pl.pallas_call(
             halve_kernel,
             out_shape=shape((tok_rows, width), BF16),
-            in_specs=[SMEM, VMEM],
+            in_specs=[SMEM, HBM],
             out_specs=VMEM,
+            scratch_shapes=[pltpu.SemaphoreType.DMA],
             compiler_params=limit,
             cost_estimate=cost(micros),
-        )(core.astype(jnp.int32).reshape(1), value)
+        )(core.astype(jnp.int32).reshape(1), in_hbm(value))
 
     def after(value, *others):
         return lax.optimization_barrier((value, *others))[0]
@@ -331,31 +343,31 @@
     def gathered(info, x, micros):
         return pl.pallas_call(
             functools.partial(gather_kernel, top, half, capacity),
-            out_shape=shape((slots, width + LANES), BF16),
+            out_shape=shape((slots, width), BF16),
             in_specs=[SMEM, VMEM, VMEM],
             out_specs=VMEM,
-            scratch_shapes=[table, table],
+            scratch_shapes=[table],
             compiler_params=limit,
             cost_estimate=cost(micros),
         )(first, info, x)
 
-    recv_own = exchange(gathered(about, tok_mine, 1)).reshape(slots, width + LANES)
+    recv_own = exchange(gathered(about, tok_mine, 1)).reshape(slots, width)
     send_mate = gathered(about_mate, tok_mate, 20)
-    recv_mate = exchange(after(send_mate, recv_own)).reshape(slots, width + LANES)
+    recv_mate = exchange(after(send_mate, recv_own)).reshape(slots, width)
 
     cot_mine = my_features(after(cotangent, about), 1)
     cot_mate = to_mate(after(cot_mine, tok_mate))
     send_cot = pl.pallas_call(
         functools.partial(cot_kernel, top, half, capacity),
-        out_shape=shape((slots, 2 * width), BF16),
+        out_shape=shape((slots, 2 * width + LANES), BF16),
         in_specs=[SMEM] + [VMEM] * 4,
         out_specs=VMEM,
-        scratch_shapes=[table],
+        scratch_shapes=[table, table],
         compiler_params=limit,
         cost_estimate=cost(15),
     )(first, about, about_mate, cot_mine, cot_mate)
     recv_own, recv_mate = after(recv_own, send_cot), after(recv_mate, send_cot)
-    recv_cot = exchange(after(send_cot, recv_mate)).reshape(slots, 2 * width)
+    recv_cot = exchange(after(send_cot, recv_mate)).reshape(slots, 2 * width + LANES)
 
     gate_w, up_w, down_w = gate_weight[0], up_weight[0], down_weight[0]
     weights = [in_hbm(w) for w in (gate_w, up_w, down_w)]
@@ -372,7 +384,7 @@
         starts = [core * width, (1 - core) * width] * 2
         span = width
     else:
-        toks = [all_features(recv_own[:, :width]), all_features(recv_mate[:, :width])]
+        toks = [all_features(recv_own), all_features(recv_mate)]
         starts = [core * 0] * 2
         span = features
     at = jnp.stack(starts).astype(jnp.int32)
@@ -420,7 +432,7 @@
     if parts == 2:
         cots = [recv_cot, swapped(recv_cot)]
     else:
-        both = [all_features(recv_cot[:, :width]), all_features(recv_cot[:, width:])]
+        both = [all_features(recv_cot[:, i * width : (i + 1) * width]) for i in range(2)]
         cots = [jnp.concatenate(both, axis=1)]
     mix_mate = mixed_rows(about_mate, back_mate)
     mix_far = to_mate(mix_mate)
@@ -428,23 +440,23 @@
     grad_gate, grad_up, grad_down = pl.pallas_call(
         functools.partial(gradients_kernel, n, m, capacity, float(top * tok_rows), step),
         out_shape=[pltpu.HBM((units, features), BF16)] * 3,
-        in_specs=[SMEM] + [HBM] * (2 * n + m + 6),
+        in_specs=[SMEM] + [HBM] * (2 * n + m + 5),
         out_specs=[HBM] * 3,
         scratch_shapes=cot_buffers
         + tok_buffers
         + [weight_buffer]
         + [pltpu.VMEM(*unit_rows)] * 5
         + [
-            pltpu.VMEM((2 * slots, LANES), BF16),
+            pltpu.VMEM((slots, LANES), BF16),
             pltpu.VMEM((units, 2 * slots), BF16),
             pltpu.VMEM((3, units, features), BF16),
-            pltpu.SemaphoreType.DMA((4 * n + 3 * m + 6,)),
+            pltpu.SemaphoreType.DMA((4 * n + 3 * m + 5,)),
         ],
         compiler_params=roomy,
         cost_estimate=cost(20),
-    )(at, *[in_hbm(x) for x in cots], *toks, in_hbm(recv_own), in_hbm(recv_mate), weights[2], *keeps)
+    )(at, *[in_hbm(x) for x in cots], *toks, in_hbm(recv_cot), weights[2], *keeps)
     back_own = exchange(after(out_own, mix_mate)).reshape(slots, width)
-    mixed = mixed_rows(about, back_own, mix_far)
+    mixed = mixed_rows(after(about, grad_down), back_own, mix_far)
     return (
         mixed,
         grad_gate[None],

time: 102 us -> 101 us (level)
  waiting for transfers between devices: 46.3 us -> 43.7 us
  Pallas kernels: 28.7 us -> 30.5 us
  local copies, waits for them, and re-layouts: 1.09 us -> 0.04 us
    pallas_call x2, Pallas kernels: 0.04 us -> 1.93 us  [my_features(): pl.pallas_call(halve_kernel, out_shape=shape((tok_rows, width), BF16), in...]
    all_to_all x5, waiting for transfers between devices: 35 us -> 33.5 us  [exchange(): lax.all_to_all(value, 'dp', split_axis=0, concat_axis=0, axis_index_group...]
    unnamed x20, local copies, waits for them, and re-layouts: 1.09 us -> 0.04 us
  transfers between devices with their start and end apart: 14 -> 14, of which waited for: 10 -> 10; matrix products, arithmetic and copies ran while one was open for 0% -> 0% of each run, Pallas kernels for 27% -> 28%
where the time goes in v4:
time: 101 us; the launch traced here: 100 us
  waiting for transfers between devices  43.7 us (43%)
  Pallas kernels  30.5 us (30%)
  starting transfers between devices  25.1 us (25%)
    all_to_all x5, waiting for transfers between devices, exchange(): lax.all_to_all(value, 'dp', split_axis=0, concat_axis=0, axis_index_group...  33.5 us
    all_to_all x5, starting transfers between devices, exchange(): lax.all_to_all(value, 'dp', split_axis=0, concat_axis=0, axis_index_group...  19.4 us
    pallas_call x1, Pallas kernels, body(): pl.pallas_call(functools.partial(gradients_kernel, n, m, capacity, float(...  11 us
    pallas_call x1, Pallas kernels, body(): pl.pallas_call(functools.partial(forward_kernel, n, m, step), out_shape=[...  8.6 us
    ppermute x5, waiting for transfers between devices, swapped(): return lax.ppermute(value, 'tensor', [(0, 1), (1, 0)])  5.83 us
    ppermute x4, starting transfers between devices, to_mate(): return lax.ppermute(value, 'dp', mates)  4.82 us
    ppermute x4, waiting for transfers between devices, to_mate(): return lax.ppermute(value, 'dp', mates)  4.41 us
    pallas_call x2, Pallas kernels, gathered(): pl.pallas_call(functools.partial(gather_kernel, top, half, capacity), out...  2.56 us
  transfers between devices with their start and end apart: 14, of which 10 were waited for; matrix products, arithmetic and copies ran while one was open for 0% of the time, Pallas kernels for 28%

profile of v4, /device:TPU:0, one launch (start us, length us, event | category | flops | bytes accessed | tf_op | source)
XLA Modules:
  0.0 100.2 jit_solution(3814535583066477060)
XLA Ops:
  0.6 0.0 copy-start
  0.6 0.0 copy-start.2
  0.7 0.0 copy-start.3
  0.7 0.0 copy-start.1
  0.7 1.0 shard_map.120.x_ref
  1.7 4.1 %collective-permute-start.1 = (bf16[128,1024]{1,0:T(8,128)(2,1)S(1)}, bf16[128,1024]{1,0:T(8,128)(2,1)S(1)}, u32[]{:S(2)}, u32[]{:S(2)}) collective-permute-start(bf16[128,1024]{1,0:T(8,128)(2,1)S(1)} %shard_map.120.x_ref), channel_id=1, source_target_pairs={{0,16},{2,18},{4,20},{6,22},{8,24},{10,26},{12,28},{14,30},{16,0},... | collective-permute-start | bytes 786440 | tf_op jit(solution)/shard_map/ppermute | solution.py:294
  5.8 0.0 copy-done
  5.8 0.0 copy-done.2
  5.8 0.0 copy-done.3
  5.8 0.0 copy-done.1
  5.8 0.6 shard_map.121.info_ref
  6.3 0.1 collective-permute-start
  6.4 1.3 %shard_map.125 = bf16[320,1024]{1,0:T(8,128)(2,1)} custom-call(s32[1]{0:T(128)} %bitcast.first_ref, f32[16,128]{1,0:T(8,128)S(1)} %shard_map.121.info_ref, bf16[128,1024]{1,0:T(8,128)(2,1)S(1)} %shard_map.120.x_ref), custom_call_target="tpu_custom_call" | custom-call | flops 1000000000 | bytes 3000000 | tf_op jit(solution)/shard_map/pallas_call | solution.py:344
  7.7 5.0 %all-to-all-start = ((bf16[8,40,1024]{2,1,0:T(8,128)(2,1)}), bf16[8,40,1024]{2,1,0:T(8,128)(2,1)S(1)}, u32[]{:S(2)}, u32[]{:S(2)}) async-start(bf16[8,40,1024]{2,1,0:T(8,128)(2,1)} %bitcast.8), calls=%async_computation | async-start | bytes 1310720 | tf_op jit(solution)/shard_map/all_to_all | solution.py:298
  12.8 1.0 shard_map.122.x_ref
  13.7 4.3 %collective-permute-done.1.x_ref = bf16[128,1024]{1,0:T(8,128)(2,1)S(1)} collective-permute-done((bf16[128,1024]{1,0:T(8,128)(2,1)S(1)}, bf16[128,1024]{1,0:T(8,128)(2,1)S(1)}, u32[]{:S(2)}, u32[]{:S(2)}) %collective-permute-start.1) | collective-permute-done | bytes 262176 | tf_op jit(solution)/shard_map/ppermute | solution.py:294
  18.0 0.0 collective-permute-start.2
  18.1 0.1 collective-permute-done.info2_ref.info_ref
  18.1 1.3 %shard_map.124 = bf16[320,1024]{1,0:T(8,128)(2,1)} custom-call(s32[1]{0:T(128)} %bitcast.first_ref, f32[16,128]{1,0:T(8,128)S(1)} %collective-permute-done.info2_ref.info_ref, bf16[128,1024]{1,0:T(8,128)(2,1)S(1)} %collective-permute-done.1.x_ref), custom_call_target="tpu_custom_call" | custom-call | flops 20000000000 | bytes 60000000 | tf_op jit(solution)/shard_map/pallas_call | solution.py:344
  19.4 9.1 %all-to-all-done = bf16[8,40,1024]{2,1,0:T(8,128)(2,1)S(1)} async-done(((bf16[8,40,1024]{2,1,0:T(8,128)(2,1)}), bf16[8,40,1024]{2,1,0:T(8,128)(2,1)S(1)}, u32[]{:S(2)}, u32[]{:S(2)}) %all-to-all-start) | async-done | bytes 655392 | tf_op jit(solution)/shard_map/all_to_all | solution.py:298
  28.5 0.0 copy-start.6
  28.5 3.5 %all-to-all-start.1 = ((bf16[8,40,1024]{2,1,0:T(8,128)(2,1)}), bf16[8,40,1024]{2,1,0:T(8,128)(2,1)S(1)}, u32[]{:S(2)}, u32[]{:S(2)}) async-start(bf16[8,40,1024]{2,1,0:T(8,128)(2,1)} %bitcast.10), calls=%async_computation.1 | async-start | bytes 1310720 | tf_op jit(solution)/shard_map/all_to_all | solution.py:298
  32.1 0.0 collective-permute-done.2.x2_ref
  32.1 1.9 %shard_map.123 = bf16[320,2176]{1,0:T(8,128)(2,1)} custom-call(s32[1]{0:T(128)} %bitcast.first_ref, f32[16,128]{1,0:T(8,128)S(1)} %shard_map.121.info_ref, f32[16,128]{1,0:T(8,128)S(1)} %collective-permute-done.info2_ref.info_ref, bf16[128,1024]{1,0:T(8,128)(2,1)S(1)} %shard_map.122.x_ref, bf16[128,1024]{1,0:T(8,128)(2,1)S(1)} %collective-permute-done.2.x2_ref), custom_call_target="tpu_custom_call" | custom-call | flops 15000000512 | bytes 45000000 | tf_op jit(solution)/shard_map/pallas_call | solution.py:360
  34.0 0.0 copy-done.6
  34.0 0.0 collective-permute-start.3
  34.0 8.7 %all-to-all-done.1 = bf16[8,40,1024]{2,1,0:T(8,128)(2,1)S(1)} async-done(((bf16[8,40,1024]{2,1,0:T(8,128)(2,1)}), bf16[8,40,1024]{2,1,0:T(8,128)(2,1)S(1)}, u32[]{:S(2)}, u32[]{:S(2)}) %all-to-all-start.1) | async-done | bytes 655392 | tf_op jit(solution)/shard_map/all_to_all | solution.py:298
  42.7 0.0 copy-start.7
  42.7 3.6 %all-to-all-start.2 = ((bf16[8,40,2176]{2,1,0:T(8,128)(2,1)}), bf16[8,40,2176]{2,1,0:T(8,128)(2,1)S(1)}, u32[]{:S(2)}, u32[]{:S(2)}) async-start(bf16[8,40,2176]{2,1,0:T(8,128)(2,1)} %bitcast.12), calls=%async_computation.2 | async-start | bytes 2785280 | tf_op jit(solution)/shard_map/all_to_all | solution.py:298
  46.3 0.0 collective-permute-done.3.refs_1_.refs_3_
  46.3 0.0 copy-start.8
  46.3 0.1 collective-permute-start.4
  46.4 0.1 pad_add_fusion.at_ref
  46.4 2.1 %collective-permute-done.4.refs_3_.refs_5_ = bf16[320,1024]{1,0:T(8,128)(2,1)} collective-permute-done((bf16[320,1024]{1,0:T(8,128)(2,1)S(1)}, bf16[320,1024]{1,0:T(8,128)(2,1)}, u32[]{:S(2)}, u32[]{:S(2)}) %collective-permute-start.4) | collective-permute-done | bytes 655392 | tf_op jit(solution)/shard_map/ppermute | solution.py:303
  48.6 0.0 copy-done.7
  48.6 0.0 copy-done.8
  48.6 8.6 %shard_map.126 = (bf16[640,512]{1,0:T(8,128)(2,1)}, bf16[640,512]{1,0:T(8,128)(2,1)}, bf16[640,512]{1,0:T(8,128)(2,1)}, bf16[320,1024]{1,0:T(8,128)(2,1)S(1)}, b...) custom-call(s32[4]{0:T(128)S(1)} %pad_add_fusion.at_ref, ...), custom_call_target="tpu_custom_call" | custom-call | flops 8000000000 | bytes 24000000 | tf_op jit(solution)/shard_map/pallas_call | solution.py:412
  57.2 0.2 collective-permute-start.5
  57.4 2.0 %collective-permute-done.5.b_ref = bf16[320,1024]{1,0:T(8,128)(2,1)S(1)} collective-permute-done((bf16[320,1024]{1,0:T(8,128)(2,1)S(1)}, bf16[320,1024]{1,0:T(8,128)(2,1)S(1)}, u32[]{:S(2)}, u32[]{:S(2)}) %collective-permute-start.5) | collective-permute-done | bytes 655392 | tf_op jit(solution)/shard_map/ppermute | solution.py:303
  59.3 0.0 copy-start.9
  59.3 0.0 copy-start.4
  59.3 1.0 %shard_map.127 = bf16[320,1024]{1,0:T(8,128)(2,1)} custom-call(bf16[320,1024]{1,0:T(8,128)(2,1)S(1)} %get-tuple-element.34.a_ref, bf16[320,1024]{1,0:T(8,128)(2,1)S(1)} %collective-permute-done.5.b_ref), custom_call_target="tpu_custom_call" | custom-call | flops 1000000000 | bytes 3000000 | tf_op jit(solution)/shard_map/pallas_call | solution.py:402
  60.4 4.0 %all-to-all-done.2 = bf16[8,40,2176]{2,1,0:T(8,128)(2,1)S(1)} async-done(((bf16[8,40,2176]{2,1,0:T(8,128)(2,1)}), bf16[8,40,2176]{2,1,0:T(8,128)(2,1)S(1)}, u32[]{:S(2)}, u32[]{:S(2)}) %all-to-all-start.2) | async-done | bytes 1392672 | tf_op jit(solution)/shard_map/all_to_all | solution.py:298
  64.3 0.0 copy-start.5
  64.3 0.0 collective-permute-start.6
  64.3 3.5 %all-to-all-start.3 = ((bf16[8,40,1024]{2,1,0:T(8,128)(2,1)}), bf16[8,40,1024]{2,1,0:T(8,128)(2,1)S(1)}, u32[]{:S(2)}, u32[]{:S(2)}) async-start(bf16[8,40,1024]{2,1,0:T(8,128)(2,1)} %bitcast.17), calls=%async_computation.3 | async-start | bytes 1310720 | tf_op jit(solution)/shard_map/all_to_all | solution.py:298
  67.9 0.0 copy-done.9
  67.9 0.6 collective-permute-start.7
  68.5 1.7 %collective-permute-done.7.b_ref = bf16[320,1024]{1,0:T(8,128)(2,1)S(1)} collective-permute-done((bf16[320,1024]{1,0:T(8,128)(2,1)S(1)}, bf16[320,1024]{1,0:T(8,128)(2,1)S(1)}, u32[]{:S(2)}, u32[]{:S(2)}) %collective-permute-start.7) | collective-permute-done | bytes 655392 | tf_op jit(solution)/shard_map/ppermute | solution.py:303
  70.2 0.0 copy-done.4
  70.2 1.0 %shard_map.130 = bf16[320,1024]{1,0:T(8,128)(2,1)} custom-call(bf16[320,1024]{1,0:T(8,128)(2,1)S(1)} %copy-done.4, bf16[320,1024]{1,0:T(8,128)(2,1)S(1)} %collective-permute-done.7.b_ref), custom_call_target="tpu_custom_call" | custom-call | flops 1000000000 | bytes 3000000 | tf_op jit(solution)/shard_map/pallas_call | solution.py:402
  71.2 0.0 copy-done.5
  71.2 7.8 %all-to-all-done.3 = bf16[8,40,1024]{2,1,0:T(8,128)(2,1)S(1)} async-done(((bf16[8,40,1024]{2,1,0:T(8,128)(2,1)}), bf16[8,40,1024]{2,1,0:T(8,128)(2,1)S(1)}, u32[]{:S(2)}, u32[]{:S(2)}) %all-to-all-start.3) | async-done | bytes 655392 | tf_op jit(solution)/shard_map/all_to_all | solution.py:298
  79.1 0.6 shard_map.128
  79.7 0.6 collective-permute-start.8
  80.3 3.7 %all-to-all-start.4 = ((bf16[8,40,1024]{2,1,0:T(8,128)(2,1)}), bf16[8,40,1024]{2,1,0:T(8,128)(2,1)S(1)}, u32[]{:S(2)}, u32[]{:S(2)}) async-start(bf16[8,40,1024]{2,1,0:T(8,128)(2,1)} %bitcast.19), calls=%async_computation.4 | async-start | bytes 1310720 | tf_op jit(solution)/shard_map/all_to_all | solution.py:298
  84.0 0.0 collective-permute-done.6.refs_1_
  84.1 11.0 %shard_map.129 = (bf16[512,2048]{1,0:T(8,128)(2,1)}, bf16[512,2048]{1,0:T(8,128)(2,1)}, bf16[512,2048]{1,0:T(8,128)(2,1)}) custom-call(s32[4]{0:T(128)S(1)} %pad_add_fusion.at_ref, bf16[320,2176]{1,0:T(8,128)(2,1)} %bitcast.30, bf16[320,2176]{1,0:T(8,128)(2,1)} %collective-permute-done.6.refs_1_, bf16[320,1024]{1,0:T(8,128)(2,1)} %bitcast.34, ...), custom_call_target="tpu_custom_call" | custom-call | flops 20000000000 | bytes 60000000 | tf_op jit(solution)/shard_map/pallas_call | solution.py:440
  95.0 0.0 collective-permute-done.8.rest_0_
  95.0 3.9 %all-to-all-done.4 = bf16[8,40,1024]{2,1,0:T(8,128)(2,1)S(1)} async-done(((bf16[8,40,1024]{2,1,0:T(8,128)(2,1)}), bf16[8,40,1024]{2,1,0:T(8,128)(2,1)S(1)}, u32[]{:S(2)}, u32[]{:S(2)}) %all-to-all-start.4) | async-done | bytes 655392 | tf_op jit(solution)/shard_map/all_to_all | solution.py:298
  98.9 1.3 %shard_map.131 = bf16[128,1024]{1,0:T(8,128)(2,1)} custom-call(s32[1]{0:T(128)} %bitcast.first_ref, f32[16,128]{1,0:T(8,128)S(1)} %shard_map.121.info_ref, bf16[320,1024]{1,0:T(8,128)(2,1)S(1)} %bitcast.24, bf16[128,1024]{1,0:T(8,128)(2,1)S(1)} %collective-permute-done.8.rest_0_), custom_call_target="tpu_custom_call" | custom-call | flops 1000000000 | bytes 3000000 | tf_op jit(solution)/shard_map/pallas_call | solution.py:320
Async XLA Ops:
  0.6 5.1 %copy-start = (s32[128,4]{0,1:T(4,128)S(1)}, s32[128,4]{0,1:T(4,128)}, u32[]{:S(2)}) copy-start(s32[128,4]{0,1:T(4,128)} %param.11) | copy-start | bytes 6148
  0.6 5.1 %copy-start.2 = (s32[2]{0:T(128)S(1)}, s32[2]{0:T(128)}, u32[]{:S(2)}) copy-start(s32[2]{0:T(128)} %lengths_ref.1) | copy-start | bytes 28
  0.7 5.1 %copy-start.3 = (s32[128]{0:T(128)S(1)}, s32[128]{0:T(128)}, u32[]{:S(2)}) copy-start(s32[128]{0:T(128)} %param.13) | copy-start | bytes 1540
  0.7 5.1 %copy-start.1 = (f32[128,4]{0,1:T(4,128)S(1)}, f32[128,4]{0,1:T(4,128)}, u32[]{:S(2)}) copy-start(f32[128,4]{0,1:T(4,128)} %param.12) | copy-start | bytes 6148
  1.7 16.4 %collective-permute-start.1 = (bf16[128,1024]{1,0:T(8,128)(2,1)S(1)}, bf16[128,1024]{1,0:T(8,128)(2,1)S(1)}, u32[]{:S(2)}, u32[]{:S(2)}) collective-permute-start(bf16[128,1024]{1,0:T(8,128)(2,1)S(1)} %shard_map.120.x_ref), channel_id=1, source_target_pairs={{0,16},{2,18},{4,20},{6,22},{8,24},{10,26},{12,28},{14,30},{16,0},... | collective-permute-start | bytes 786440 | tf_op jit(solution)/shard_map/ppermute | solution.py:294
  6.3 11.8 %collective-permute-start = (f32[16,128]{1,0:T(8,128)S(1)}, f32[16,128]{1,0:T(8,128)S(1)}, u32[]{:S(2)}, u32[]{:S(2)}) collective-permute-start(f32[16,128]{1,0:T(8,128)S(1)} %shard_map.121.info_ref), channel_id=1, source_target_pairs={{0,16},{2,18},{4,20},{6,22},{8,24},{10,26},{12,28},{14,30},{16,0},... | collective-permute-start | bytes 24584 | tf_op jit(solution)/shard_map/ppermute | solution.py:294
  7.7 20.8 %all-to-all-start = ((bf16[8,40,1024]{2,1,0:T(8,128)(2,1)}), bf16[8,40,1024]{2,1,0:T(8,128)(2,1)S(1)}, u32[]{:S(2)}, u32[]{:S(2)}) async-start(bf16[8,40,1024]{2,1,0:T(8,128)(2,1)} %bitcast.8), calls=%async_computation | async-start | bytes 1310720 | tf_op jit(solution)/shard_map/all_to_all | solution.py:298
  18.0 14.0 %collective-permute-start.2 = (bf16[128,1024]{1,0:T(8,128)(2,1)S(1)}, bf16[128,1024]{1,0:T(8,128)(2,1)S(1)}, u32[]{:S(2)}, u32[]{:S(2)}) collective-permute-start(bf16[128,1024]{1,0:T(8,128)(2,1)S(1)} %shard_map.122.x_ref), channel_id=1, source_target_pairs={{0,16},{2,18},{4,20},{6,22},{8,24},{10,26},{12,28},{14,30},{16,0},... | collective-permute-start | bytes 786440 | tf_op jit(solution)/shard_map/ppermute | solution.py:294
  28.5 5.5 %copy-start.6 = (bf16[8,40,1024]{2,1,0:T(8,128)(2,1)}, bf16[8,40,1024]{2,1,0:T(8,128)(2,1)S(1)}, u32[]{:S(2)}) copy-start(bf16[8,40,1024]{2,1,0:T(8,128)(2,1)S(1)} %all-to-all-done) | copy-start | bytes 1966084
  28.5 14.2 %all-to-all-start.1 = ((bf16[8,40,1024]{2,1,0:T(8,128)(2,1)}), bf16[8,40,1024]{2,1,0:T(8,128)(2,1)S(1)}, u32[]{:S(2)}, u32[]{:S(2)}) async-start(bf16[8,40,1024]{2,1,0:T(8,128)(2,1)} %bitcast.10), calls=%async_computation.1 | async-start | bytes 1310720 | tf_op jit(solution)/shard_map/all_to_all | solution.py:298
  34.0 12.3 %collective-permute-start.3 = (bf16[320,1024]{1,0:T(8,128)(2,1)S(1)}, bf16[320,1024]{1,0:T(8,128)(2,1)S(1)}, u32[]{:S(2)}, u32[]{:S(2)}) collective-permute-start(bf16[320,1024]{1,0:T(8,128)(2,1)S(1)} %bitcast.32), channel_id=1, source_target_pairs={{0,1},{1,0},{2,3},{3,2},{4,5},{5,4},{6,7},{7,6},{8,9},{9,8},{10,11... | collective-permute-start | bytes 1966088 | tf_op jit(solution)/shard_map/ppermute | solution.py:303
  42.7 5.9 %copy-start.7 = (bf16[8,40,1024]{2,1,0:T(8,128)(2,1)}, bf16[8,40,1024]{2,1,0:T(8,128)(2,1)S(1)}, u32[]{:S(2)}) copy-start(bf16[8,40,1024]{2,1,0:T(8,128)(2,1)S(1)} %all-to-all-done.1) | copy-start | bytes 1966084
  42.7 21.7 %all-to-all-start.2 = ((bf16[8,40,2176]{2,1,0:T(8,128)(2,1)}), bf16[8,40,2176]{2,1,0:T(8,128)(2,1)S(1)}, u32[]{:S(2)}, u32[]{:S(2)}) async-start(bf16[8,40,2176]{2,1,0:T(8,128)(2,1)} %bitcast.12), calls=%async_computation.2 | async-start | bytes 2785280 | tf_op jit(solution)/shard_map/all_to_all | solution.py:298
  46.3 2.3 %copy-start.8 = (bf16[320,1024]{1,0:T(8,128)(2,1)}, bf16[320,1024]{1,0:T(8,128)(2,1)S(1)}, u32[]{:S(2)}) copy-start(bf16[320,1024]{1,0:T(8,128)(2,1)S(1)} %collective-permute-done.3.refs_1_.refs_3_) | copy-start | bytes 1966084
  46.3 2.3 %collective-permute-start.4 = (bf16[320,1024]{1,0:T(8,128)(2,1)S(1)}, bf16[320,1024]{1,0:T(8,128)(2,1)}, u32[]{:S(2)}, u32[]{:S(2)}) collective-permute-start(bf16[320,1024]{1,0:T(8,128)(2,1)S(1)} %bitcast.35), channel_id=1, source_target_pairs={{0,1},{1,0},{2,3},{3,2},{4,5},{5,4},{6,7},{7,6},{8,9},{9,8},{10,11... | collective-permute-start | bytes 1966088 | tf_op jit(solution)/shard_map/ppermute | solution.py:303
  57.2 2.2 %collective-permute-start.5 = (bf16[320,1024]{1,0:T(8,128)(2,1)S(1)}, bf16[320,1024]{1,0:T(8,128)(2,1)S(1)}, u32[]{:S(2)}, u32[]{:S(2)}) collective-permute-start(bf16[320,1024]{1,0:T(8,128)(2,1)S(1)} %get-tuple-element.35), channel_id=1, source_target_pairs={{0,1},{1,0},{2,3},{3,2},{4,5},{5,4},{6,7},{7,6},{8,9},{9,8},{10,11... | collective-permute-start | bytes 1966088 | tf_op jit(solution)/shard_map/ppermute | solution.py:303
  59.3 8.6 %copy-start.9 = (bf16[320,1024]{1,0:T(8,128)(2,1)S(1)}, bf16[320,1024]{1,0:T(8,128)(2,1)}, u32[]{:S(2)}) copy-start(bf16[320,1024]{1,0:T(8,128)(2,1)} %get-tuple-element.44) | copy-start | bytes 1966084
  59.3 10.9 %copy-start.4 = (bf16[320,1024]{1,0:T(8,128)(2,1)S(1)}, bf16[320,1024]{1,0:T(8,128)(2,1)}, u32[]{:S(2)}) copy-start(bf16[320,1024]{1,0:T(8,128)(2,1)} %get-tuple-element.43.a_ref) | copy-start | bytes 1966084
  64.3 6.9 %copy-start.5 = (bf16[8,40,2176]{2,1,0:T(8,128)(2,1)}, bf16[8,40,2176]{2,1,0:T(8,128)(2,1)S(1)}, u32[]{:S(2)}) copy-start(bf16[8,40,2176]{2,1,0:T(8,128)(2,1)S(1)} %all-to-all-done.2) | copy-start | bytes 4177924
  64.3 19.7 %collective-permute-start.6 = (bf16[320,2176]{1,0:T(8,128)(2,1)S(1)}, bf16[320,2176]{1,0:T(8,128)(2,1)}, u32[]{:S(2)}, u32[]{:S(2)}) collective-permute-start(bf16[320,2176]{1,0:T(8,128)(2,1)S(1)} %bitcast.29), channel_id=1, source_target_pairs={{0,1},{1,0},{2,3},{3,2},{4,5},{5,4},{6,7},{7,6},{8,9},{9,8},{10,11... | collective-permute-start | bytes 4177928 | tf_op jit(solution)/shard_map/ppermute | solution.py:303
  64.3 14.7 %all-to-all-start.3 = ((bf16[8,40,1024]{2,1,0:T(8,128)(2,1)}), bf16[8,40,1024]{2,1,0:T(8,128)(2,1)S(1)}, u32[]{:S(2)}, u32[]{:S(2)}) async-start(bf16[8,40,1024]{2,1,0:T(8,128)(2,1)} %bitcast.17), calls=%async_computation.3 | async-start | bytes 1310720 | tf_op jit(solution)/shard_map/all_to_all | solution.py:298
  67.9 2.3 %collective-permute-start.7 = (bf16[320,1024]{1,0:T(8,128)(2,1)S(1)}, bf16[320,1024]{1,0:T(8,128)(2,1)S(1)}, u32[]{:S(2)}, u32[]{:S(2)}) collective-permute-start(bf16[320,1024]{1,0:T(8,128)(2,1)S(1)} %copy-done.9), channel_id=1, source_target_pairs={{0,1},{1,0},{2,3},{3,2},{4,5},{5,4},{6,7},{7,6},{8,9},{9,8},{10,11... | collective-permute-start | bytes 1966088 | tf_op jit(solution)/shard_map/ppermute | solution.py:303
  79.7 15.3 %collective-permute-start.8 = (bf16[128,1024]{1,0:T(8,128)(2,1)S(1)}, bf16[128,1024]{1,0:T(8,128)(2,1)S(1)}, u32[]{:S(2)}, u32[]{:S(2)}) collective-permute-start(bf16[128,1024]{1,0:T(8,128)(2,1)S(1)} %shard_map.128), channel_id=1, source_target_pairs={{0,16},{2,18},{4,20},{6,22},{8,24},{10,26},{12,28},{14,30},{16,0},... | collective-permute-start | bytes 786440 | tf_op jit(solution)/shard_map/ppermute | solution.py:294
  80.3 18.6 %all-to-all-start.4 = ((bf16[8,40,1024]{2,1,0:T(8,128)(2,1)}), bf16[8,40,1024]{2,1,0:T(8,128)(2,1)S(1)}, u32[]{:S(2)}, u32[]{:S(2)}) async-start(bf16[8,40,1024]{2,1,0:T(8,128)(2,1)} %bitcast.19), calls=%async_computation.4 | async-start | bytes 1310720 | tf_op jit(solution)/shard_map/all_to_all | solution.py:298

commit v5 on v4

--- a/solution.py
+++ b/solution.py
@@ -101,14 +101,20 @@
     out_ref[:, 2 * width :] = facts.astype(BF16)
 
 
-def mix_kernel(top, half, capacity, first_ref, info_ref, back_ref, *rest):
-    far_refs, (out_ref, pick_ref, weight_ref) = rest[:-3], rest[-3:]
-    slot_tables(top, half, capacity, first_ref[0], info_ref[...], pick_ref, weight_ref)
-    weight = weight_ref[...]
-    high = weight.astype(BF16)
-    low = (weight - high.astype(F32)).astype(BF16)
+def spread_kernel(top, half, capacity, first_ref, info_ref, info2_ref, *refs):
+    outs, (pick_ref, weight_ref) = refs[:-2], refs[-2:]
+    for i, info in enumerate((info_ref, info2_ref)):
+        slot_tables(top, half, capacity, first_ref[0], info[...], pick_ref, weight_ref)
+        weight = weight_ref[...]
+        high = weight.astype(BF16)
+        outs[2 * i][...] = high
+        outs[2 * i + 1][...] = (weight - high.astype(F32)).astype(BF16)
+
+
+def mix_kernel(high_ref, low_ref, back_ref, *rest):
+    far_refs, out_ref = rest[:-1], rest[-1]
     back = back_ref[...]
-    total = dot(high, back, ((0,), (0,))) + dot(low, back, ((0,), (0,)))
+    total = dot(high_ref[...], back, ((0,), (0,))) + dot(low_ref[...], back, ((0,), (0,)))
     for far in far_refs:
         total = total + far[...].astype(F32)
     out_ref[...] = total.astype(BF16)
@@ -316,16 +322,15 @@
     def after(value, *others):
         return lax.optimization_barrier((value, *others))[0]
 
-    def mixed_rows(info, back, *far):
+    def mixed_rows(spread, back, *far):
         return pl.pallas_call(
-            functools.partial(mix_kernel, top, half, capacity),
-            out_shape=jax.ShapeDtypeStruct((tok_rows, width), BF16),
-            in_specs=[SMEM, VMEM, VMEM] + [VMEM] * len(far),
+            mix_kernel,
+            out_shape=shape((tok_rows, width), BF16),
+            in_specs=[VMEM] * (3 + len(far)),
             out_specs=VMEM,
-            scratch_shapes=[table, table],
             compiler_params=limit,
             cost_estimate=cost(1),
-        )(first, info, back, *far)
+        )(*spread, back, *far)
 
     tok_mine = my_features(tokens, 1)
     tok_mate = to_mate(tok_mine)
@@ -354,6 +359,16 @@
     recv_own = exchange(gathered(about, tok_mine, 1)).reshape(slots, width)
     send_mate = gathered(about_mate, tok_mate, 20)
     recv_mate = exchange(after(send_mate, recv_own)).reshape(slots, width)
+
+    spreads = pl.pallas_call(
+        functools.partial(spread_kernel, top, half, capacity),
+        out_shape=[shape((slots, tok_rows), BF16)] * 4,
+        in_specs=[SMEM, VMEM, VMEM],
+        out_specs=[VMEM] * 4,
+        scratch_shapes=[table, table],
+        compiler_params=limit,
+        cost_estimate=cost(1),
+    )(first, about, about_mate)
 
     cot_mine = my_features(after(cotangent, about), 1)
     cot_mate = to_mate(after(cot_mine, tok_mate))
@@ -434,7 +449,7 @@
     else:
         both = [all_features(recv_cot[:, i * width : (i + 1) * width]) for i in range(2)]
         cots = [jnp.concatenate(both, axis=1)]
-    mix_mate = mixed_rows(about_mate, back_mate)
+    mix_mate = mixed_rows(spreads[2:], back_mate)
     mix_far = to_mate(mix_mate)
     keeps = [in_hbm(x) for x in (keep_gate, keep_up, after(hidden, mix_mate))]
     grad_gate, grad_up, grad_down = pl.pallas_call(
@@ -456,7 +471,7 @@
         cost_estimate=cost(20),
     )(at, *[in_hbm(x) for x in cots], *toks, in_hbm(recv_cot), weights[2], *keeps)
     back_own = exchange(after(out_own, mix_mate)).reshape(slots, width)
-    mixed = mixed_rows(after(about, grad_down), back_own, mix_far)
+    mixed = mixed_rows([after(spreads[0], grad_down), spreads[1]], back_own, mix_far)
     return (
         mixed,
         grad_gate[None],

time: 101 us -> 100 us (0.990)
  no operation moved by 1% of the time
where the time goes in v5:
time: 100 us; the launch traced here: 99.9 us
  waiting for transfers between devices  43.5 us (44%)
  Pallas kernels  30.4 us (30%)
  starting transfers between devices  25.1 us (25%)
    all_to_all x5, waiting for transfers between devices, exchange(): lax.all_to_all(value, 'dp', split_axis=0, concat_axis=0, axis_index_group...  33.4 us
    all_to_all x5, starting transfers between devices, exchange(): lax.all_to_all(value, 'dp', split_axis=0, concat_axis=0, axis_index_group...  19.4 us
    pallas_call x1, Pallas kernels, body(): pl.pallas_call(functools.partial(gradients_kernel, n, m, capacity, float(...  11 us
    pallas_call x1, Pallas kernels, body(): pl.pallas_call(functools.partial(forward_kernel, n, m, step), out_shape=[...  8.6 us
    ppermute x5, waiting for transfers between devices, swapped(): return lax.ppermute(value, 'tensor', [(0, 1), (1, 0)])  5.62 us
    ppermute x4, starting transfers between devices, to_mate(): return lax.ppermute(value, 'dp', mates)  4.83 us
    ppermute x4, waiting for transfers between devices, to_mate(): return lax.ppermute(value, 'dp', mates)  4.41 us
    pallas_call x2, Pallas kernels, gathered(): pl.pallas_call(functools.partial(gather_kernel, top, half, capacity), out...  2.56 us
  transfers between devices with their start and end apart: 14, of which 10 were waited for; matrix products, arithmetic and copies ran while one was open for 0% of the time, Pallas kernels for 28%

profile of v5, /device:TPU:0, one launch (start us, length us, event | category | flops | bytes accessed | tf_op | source)
XLA Modules:
  0.0 99.9 jit_solution(14632493424603578356)
XLA Ops:
  0.6 0.0 copy-start
  0.6 0.0 copy-start.2
  0.7 0.0 copy-start.3
  0.7 0.0 copy-start.1
  0.7 1.0 shard_map.120.x_ref
  1.7 4.1 %collective-permute-start.1 = (bf16[128,1024]{1,0:T(8,128)(2,1)S(1)}, bf16[128,1024]{1,0:T(8,128)(2,1)S(1)}, u32[]{:S(2)}, u32[]{:S(2)}) collective-permute-start(bf16[128,1024]{1,0:T(8,128)(2,1)S(1)} %shard_map.120.x_ref), channel_id=1, source_target_pairs={{0,16},{2,18},{4,20},{6,22},{8,24},{10,26},{12,28},{14,30},{16,0},... | collective-permute-start | bytes 786440 | tf_op jit(solution)/shard_map/ppermute | solution.py:300
  5.8 0.0 copy-done
  5.8 0.0 copy-done.2
  5.8 0.0 copy-done.3
  5.8 0.0 copy-done.1
  5.8 0.6 shard_map.121.info_ref
  6.3 0.1 collective-permute-start
  6.4 1.3 %shard_map.126 = bf16[320,1024]{1,0:T(8,128)(2,1)} custom-call(s32[1]{0:T(128)} %bitcast.first_ref, f32[16,128]{1,0:T(8,128)S(1)} %shard_map.121.info_ref, bf16[128,1024]{1,0:T(8,128)(2,1)S(1)} %shard_map.120.x_ref), custom_call_target="tpu_custom_call" | custom-call | flops 1000000000 | bytes 3000000 | tf_op jit(solution)/shard_map/pallas_call | solution.py:349
  7.7 5.0 %all-to-all-start = ((bf16[8,40,1024]{2,1,0:T(8,128)(2,1)}), bf16[8,40,1024]{2,1,0:T(8,128)(2,1)S(1)}, u32[]{:S(2)}, u32[]{:S(2)}) async-start(bf16[8,40,1024]{2,1,0:T(8,128)(2,1)} %bitcast.8), calls=%async_computation | async-start | bytes 1310720 | tf_op jit(solution)/shard_map/all_to_all | solution.py:304
  12.8 1.0 shard_map.123.x_ref
  13.7 4.3 %collective-permute-done.1.x_ref = bf16[128,1024]{1,0:T(8,128)(2,1)S(1)} collective-permute-done((bf16[128,1024]{1,0:T(8,128)(2,1)S(1)}, bf16[128,1024]{1,0:T(8,128)(2,1)S(1)}, u32[]{:S(2)}, u32[]{:S(2)}) %collective-permute-start.1) | collective-permute-done | bytes 262176 | tf_op jit(solution)/shard_map/ppermute | solution.py:300
  18.0 0.0 collective-permute-start.2
  18.1 0.1 collective-permute-done.info2_ref.info_ref
  18.1 1.3 %shard_map.125 = bf16[320,1024]{1,0:T(8,128)(2,1)} custom-call(s32[1]{0:T(128)} %bitcast.first_ref, f32[16,128]{1,0:T(8,128)S(1)} %collective-permute-done.info2_ref.info_ref, bf16[128,1024]{1,0:T(8,128)(2,1)S(1)} %collective-permute-done.1.x_ref), custom_call_target="tpu_custom_call" | custom-call | flops 20000000000 | bytes 60000000 | tf_op jit(solution)/shard_map/pallas_call | solution.py:349
  19.4 9.1 %all-to-all-done = bf16[8,40,1024]{2,1,0:T(8,128)(2,1)S(1)} async-done(((bf16[8,40,1024]{2,1,0:T(8,128)(2,1)}), bf16[8,40,1024]{2,1,0:T(8,128)(2,1)S(1)}, u32[]{:S(2)}, u32[]{:S(2)}) %all-to-all-start) | async-done | bytes 655392 | tf_op jit(solution)/shard_map/all_to_all | solution.py:304
  28.5 0.0 copy-start.6
  28.5 3.5 %all-to-all-start.1 = ((bf16[8,40,1024]{2,1,0:T(8,128)(2,1)}), bf16[8,40,1024]{2,1,0:T(8,128)(2,1)S(1)}, u32[]{:S(2)}, u32[]{:S(2)}) async-start(bf16[8,40,1024]{2,1,0:T(8,128)(2,1)} %bitcast.10), calls=%async_computation.1 | async-start | bytes 1310720 | tf_op jit(solution)/shard_map/all_to_all | solution.py:304
  32.1 0.0 collective-permute-done.2.x2_ref
  32.1 1.9 %shard_map.124 = bf16[320,2176]{1,0:T(8,128)(2,1)} custom-call(s32[1]{0:T(128)} %bitcast.first_ref, f32[16,128]{1,0:T(8,128)S(1)} %shard_map.121.info_ref, f32[16,128]{1,0:T(8,128)S(1)} %collective-permute-done.info2_ref.info_ref, bf16[128,1024]{1,0:T(8,128)(2,1)S(1)} %shard_map.123.x_ref, bf16[128,1024]{1,0:T(8,128)(2,1)S(1)} %collective-permute-done.2.x2_ref), custom_call_target="tpu_custom_call" | custom-call | flops 15000000512 | bytes 45000000 | tf_op jit(solution)/shard_map/pallas_call | solution.py:375
  34.0 0.0 copy-done.6
  34.0 0.0 collective-permute-start.3
  34.0 8.7 %all-to-all-done.1 = bf16[8,40,1024]{2,1,0:T(8,128)(2,1)S(1)} async-done(((bf16[8,40,1024]{2,1,0:T(8,128)(2,1)}), bf16[8,40,1024]{2,1,0:T(8,128)(2,1)S(1)}, u32[]{:S(2)}, u32[]{:S(2)}) %all-to-all-start.1) | async-done | bytes 655392 | tf_op jit(solution)/shard_map/all_to_all | solution.py:304
  42.7 0.0 copy-start.7
  42.7 3.6 %all-to-all-start.2 = ((bf16[8,40,2176]{2,1,0:T(8,128)(2,1)}), bf16[8,40,2176]{2,1,0:T(8,128)(2,1)S(1)}, u32[]{:S(2)}, u32[]{:S(2)}) async-start(bf16[8,40,2176]{2,1,0:T(8,128)(2,1)} %bitcast.12), calls=%async_computation.2 | async-start | bytes 2785280 | tf_op jit(solution)/shard_map/all_to_all | solution.py:304
  46.3 0.0 collective-permute-done.3.refs_1_.refs_3_
  46.3 0.0 copy-start.8
  46.3 0.1 collective-permute-start.4
  46.4 0.1 pad_add_fusion.at_ref
  46.4 2.1 %collective-permute-done.4.refs_3_.refs_5_ = bf16[320,1024]{1,0:T(8,128)(2,1)} collective-permute-done((bf16[320,1024]{1,0:T(8,128)(2,1)S(1)}, bf16[320,1024]{1,0:T(8,128)(2,1)}, u32[]{:S(2)}, u32[]{:S(2)}) %collective-permute-start.4) | collective-permute-done | bytes 655392 | tf_op jit(solution)/shard_map/ppermute | solution.py:309
  48.6 0.0 copy-done.7
  48.6 0.0 copy-done.8
  48.6 8.6 %shard_map.127 = (bf16[640,512]{1,0:T(8,128)(2,1)}, bf16[640,512]{1,0:T(8,128)(2,1)}, bf16[640,512]{1,0:T(8,128)(2,1)}, bf16[320,1024]{1,0:T(8,128)(2,1)S(1)}, b...) custom-call(s32[4]{0:T(128)S(1)} %pad_add_fusion.at_ref, ...), custom_call_target="tpu_custom_call" | custom-call | flops 8000000000 | bytes 24000000 | tf_op jit(solution)/shard_map/pallas_call | solution.py:427
  57.2 0.2 collective-permute-start.5
  57.4 2.0 %collective-permute-done.5.b_ref = bf16[320,1024]{1,0:T(8,128)(2,1)S(1)} collective-permute-done((bf16[320,1024]{1,0:T(8,128)(2,1)S(1)}, bf16[320,1024]{1,0:T(8,128)(2,1)S(1)}, u32[]{:S(2)}, u32[]{:S(2)}) %collective-permute-start.5) | collective-permute-done | bytes 655392 | tf_op jit(solution)/shard_map/ppermute | solution.py:309
  59.3 0.0 copy-start.9
  59.3 1.0 %shard_map.128 = bf16[320,1024]{1,0:T(8,128)(2,1)} custom-call(bf16[320,1024]{1,0:T(8,128)(2,1)S(1)} %get-tuple-element.39.a_ref, bf16[320,1024]{1,0:T(8,128)(2,1)S(1)} %collective-permute-done.5.b_ref), custom_call_target="tpu_custom_call" | custom-call | flops 1000000000 | bytes 3000000 | tf_op jit(solution)/shard_map/pallas_call | solution.py:417
  60.4 4.0 %all-to-all-done.2 = bf16[8,40,2176]{2,1,0:T(8,128)(2,1)S(1)} async-done(((bf16[8,40,2176]{2,1,0:T(8,128)(2,1)}), bf16[8,40,2176]{2,1,0:T(8,128)(2,1)S(1)}, u32[]{:S(2)}, u32[]{:S(2)}) %all-to-all-start.2) | async-done | bytes 1392672 | tf_op jit(solution)/shard_map/all_to_all | solution.py:304
  64.3 0.0 copy-start.5
  64.3 0.0 collective-permute-start.6
  64.3 3.5 %all-to-all-start.3 = ((bf16[8,40,1024]{2,1,0:T(8,128)(2,1)}), bf16[8,40,1024]{2,1,0:T(8,128)(2,1)S(1)}, u32[]{:S(2)}, u32[]{:S(2)}) async-start(bf16[8,40,1024]{2,1,0:T(8,128)(2,1)} %bitcast.17), calls=%async_computation.3 | async-start | bytes 1310720 | tf_op jit(solution)/shard_map/all_to_all | solution.py:304
  67.9 0.0 copy-start.4
  67.9 0.0 copy-done.9
  67.9 0.6 collective-permute-start.7
  68.5 0.2 shard_map.122
  68.7 0.0 copy-done.5
  68.7 1.5 %collective-permute-done.7.b_ref = bf16[320,1024]{1,0:T(8,128)(2,1)S(1)} collective-permute-done((bf16[320,1024]{1,0:T(8,128)(2,1)S(1)}, bf16[320,1024]{1,0:T(8,128)(2,1)S(1)}, u32[]{:S(2)}, u32[]{:S(2)}) %collective-permute-start.7) | collective-permute-done | bytes 655392 | tf_op jit(solution)/shard_map/ppermute | solution.py:309
  70.2 0.0 copy-done.4
  70.2 1.0 %shard_map.131 = bf16[320,1024]{1,0:T(8,128)(2,1)} custom-call(bf16[320,1024]{1,0:T(8,128)(2,1)S(1)} %copy-done.4, bf16[320,1024]{1,0:T(8,128)(2,1)S(1)} %collective-permute-done.7.b_ref), custom_call_target="tpu_custom_call" | custom-call | flops 1000000000 | bytes 3000000 | tf_op jit(solution)/shard_map/pallas_call | solution.py:417
  71.3 7.8 %all-to-all-done.3 = bf16[8,40,1024]{2,1,0:T(8,128)(2,1)S(1)} async-done(((bf16[8,40,1024]{2,1,0:T(8,128)(2,1)}), bf16[8,40,1024]{2,1,0:T(8,128)(2,1)S(1)}, u32[]{:S(2)}, u32[]{:S(2)}) %all-to-all-start.3) | async-done | bytes 655392 | tf_op jit(solution)/shard_map/all_to_all | solution.py:304
  79.1 0.5 shard_map.129
  79.6 0.6 collective-permute-start.8
  80.2 3.7 %all-to-all-start.4 = ((bf16[8,40,1024]{2,1,0:T(8,128)(2,1)}), bf16[8,40,1024]{2,1,0:T(8,128)(2,1)S(1)}, u32[]{:S(2)}, u32[]{:S(2)}) async-start(bf16[8,40,1024]{2,1,0:T(8,128)(2,1)} %bitcast.19), calls=%async_computation.4 | async-start | bytes 1310720 | tf_op jit(solution)/shard_map/all_to_all | solution.py:304
  83.9 0.0 collective-permute-done.6.refs_1_
  83.9 11.0 %shard_map.130 = (bf16[512,2048]{1,0:T(8,128)(2,1)}, bf16[512,2048]{1,0:T(8,128)(2,1)}, bf16[512,2048]{1,0:T(8,128)(2,1)}) custom-call(s32[4]{0:T(128)S(1)} %pad_add_fusion.at_ref, bf16[320,2176]{1,0:T(8,128)(2,1)} %bitcast.30, bf16[320,2176]{1,0:T(8,128)(2,1)} %collective-permute-done.6.refs_1_, bf16[320,1024]{1,0:T(8,128)(2,1)} %bitcast.34, ...), custom_call_target="tpu_custom_call" | custom-call | flops 20000000000 | bytes 60000000 | tf_op jit(solution)/shard_map/pallas_call | solution.py:455
  94.9 0.0 collective-permute-done.8.rest_0_
  94.9 3.9 %all-to-all-done.4 = bf16[8,40,1024]{2,1,0:T(8,128)(2,1)S(1)} async-done(((bf16[8,40,1024]{2,1,0:T(8,128)(2,1)}), bf16[8,40,1024]{2,1,0:T(8,128)(2,1)S(1)}, u32[]{:S(2)}, u32[]{:S(2)}) %all-to-all-start.4) | async-done | bytes 655392 | tf_op jit(solution)/shard_map/all_to_all | solution.py:304
  98.8 1.2 %shard_map.132 = bf16[128,1024]{1,0:T(8,128)(2,1)} custom-call(bf16[320,128]{1,0:T(8,128)(2,1)S(1)} %get-tuple-element.49.high_ref, bf16[320,128]{1,0:T(8,128)(2,1)S(1)} %get-tuple-element.50.low_ref, bf16[320,1024]{1,0:T(8,128)(2,1)S(1)} %bitcast.24, bf16[128,1024]{1,0:T(8,128)(2,1)S(1)} %collective-permute-done.8.rest_0_), custom_call_target="tpu_custom_call" | custom-call | flops 1000000000 | bytes 3000000 | tf_op jit(solution)/shard_map/pallas_call | solution.py:326
Async XLA Ops:
  0.6 5.1 %copy-start = (s32[128,4]{0,1:T(4,128)S(1)}, s32[128,4]{0,1:T(4,128)}, u32[]{:S(2)}) copy-start(s32[128,4]{0,1:T(4,128)} %param.11) | copy-start | bytes 6148
  0.6 5.1 %copy-start.2 = (s32[2]{0:T(128)S(1)}, s32[2]{0:T(128)}, u32[]{:S(2)}) copy-start(s32[2]{0:T(128)} %lengths_ref.1) | copy-start | bytes 28
  0.7 5.1 %copy-start.3 = (s32[128]{0:T(128)S(1)}, s32[128]{0:T(128)}, u32[]{:S(2)}) copy-start(s32[128]{0:T(128)} %param.13) | copy-start | bytes 1540
  0.7 5.1 %copy-start.1 = (f32[128,4]{0,1:T(4,128)S(1)}, f32[128,4]{0,1:T(4,128)}, u32[]{:S(2)}) copy-start(f32[128,4]{0,1:T(4,128)} %param.12) | copy-start | bytes 6148
  1.7 16.4 %collective-permute-start.1 = (bf16[128,1024]{1,0:T(8,128)(2,1)S(1)}, bf16[128,1024]{1,0:T(8,128)(2,1)S(1)}, u32[]{:S(2)}, u32[]{:S(2)}) collective-permute-start(bf16[128,1024]{1,0:T(8,128)(2,1)S(1)} %shard_map.120.x_ref), channel_id=1, source_target_pairs={{0,16},{2,18},{4,20},{6,22},{8,24},{10,26},{12,28},{14,30},{16,0},... | collective-permute-start | bytes 786440 | tf_op jit(solution)/shard_map/ppermute | solution.py:300
  6.3 11.8 %collective-permute-start = (f32[16,128]{1,0:T(8,128)S(1)}, f32[16,128]{1,0:T(8,128)S(1)}, u32[]{:S(2)}, u32[]{:S(2)}) collective-permute-start(f32[16,128]{1,0:T(8,128)S(1)} %shard_map.121.info_ref), channel_id=1, source_target_pairs={{0,16},{2,18},{4,20},{6,22},{8,24},{10,26},{12,28},{14,30},{16,0},... | collective-permute-start | bytes 24584 | tf_op jit(solution)/shard_map/ppermute | solution.py:300
  7.7 20.8 %all-to-all-start = ((bf16[8,40,1024]{2,1,0:T(8,128)(2,1)}), bf16[8,40,1024]{2,1,0:T(8,128)(2,1)S(1)}, u32[]{:S(2)}, u32[]{:S(2)}) async-start(bf16[8,40,1024]{2,1,0:T(8,128)(2,1)} %bitcast.8), calls=%async_computation | async-start | bytes 1310720 | tf_op jit(solution)/shard_map/all_to_all | solution.py:304
  18.0 14.0 %collective-permute-start.2 = (bf16[128,1024]{1,0:T(8,128)(2,1)S(1)}, bf16[128,1024]{1,0:T(8,128)(2,1)S(1)}, u32[]{:S(2)}, u32[]{:S(2)}) collective-permute-start(bf16[128,1024]{1,0:T(8,128)(2,1)S(1)} %shard_map.123.x_ref), channel_id=1, source_target_pairs={{0,16},{2,18},{4,20},{6,22},{8,24},{10,26},{12,28},{14,30},{16,0},... | collective-permute-start | bytes 786440 | tf_op jit(solution)/shard_map/ppermute | solution.py:300
  28.5 5.5 %copy-start.6 = (bf16[8,40,1024]{2,1,0:T(8,128)(2,1)}, bf16[8,40,1024]{2,1,0:T(8,128)(2,1)S(1)}, u32[]{:S(2)}) copy-start(bf16[8,40,1024]{2,1,0:T(8,128)(2,1)S(1)} %all-to-all-done) | copy-start | bytes 1966084
  28.5 14.2 %all-to-all-start.1 = ((bf16[8,40,1024]{2,1,0:T(8,128)(2,1)}), bf16[8,40,1024]{2,1,0:T(8,128)(2,1)S(1)}, u32[]{:S(2)}, u32[]{:S(2)}) async-start(bf16[8,40,1024]{2,1,0:T(8,128)(2,1)} %bitcast.10), calls=%async_computation.1 | async-start | bytes 1310720 | tf_op jit(solution)/shard_map/all_to_all | solution.py:304
  34.0 12.3 %collective-permute-start.3 = (bf16[320,1024]{1,0:T(8,128)(2,1)S(1)}, bf16[320,1024]{1,0:T(8,128)(2,1)S(1)}, u32[]{:S(2)}, u32[]{:S(2)}) collective-permute-start(bf16[320,1024]{1,0:T(8,128)(2,1)S(1)} %bitcast.32), channel_id=1, source_target_pairs={{0,1},{1,0},{2,3},{3,2},{4,5},{5,4},{6,7},{7,6},{8,9},{9,8},{10,11... | collective-permute-start | bytes 1966088 | tf_op jit(solution)/shard_map/ppermute | solution.py:309
  42.7 5.9 %copy-start.7 = (bf16[8,40,1024]{2,1,0:T(8,128)(2,1)}, bf16[8,40,1024]{2,1,0:T(8,128)(2,1)S(1)}, u32[]{:S(2)}) copy-start(bf16[8,40,1024]{2,1,0:T(8,128)(2,1)S(1)} %all-to-all-done.1) | copy-start | bytes 1966084
  42.7 21.7 %all-to-all-start.2 = ((bf16[8,40,2176]{2,1,0:T(8,128)(2,1)}), bf16[8,40,2176]{2,1,0:T(8,128)(2,1)S(1)}, u32[]{:S(2)}, u32[]{:S(2)}) async-start(bf16[8,40,2176]{2,1,0:T(8,128)(2,1)} %bitcast.12), calls=%async_computation.2 | async-start | bytes 2785280 | tf_op jit(solution)/shard_map/all_to_all | solution.py:304
  46.3 2.3 %copy-start.8 = (bf16[320,1024]{1,0:T(8,128)(2,1)}, bf16[320,1024]{1,0:T(8,128)(2,1)S(1)}, u32[]{:S(2)}) copy-start(bf16[320,1024]{1,0:T(8,128)(2,1)S(1)} %collective-permute-done.3.refs_1_.refs_3_) | copy-start | bytes 1966084
  46.3 2.3 %collective-permute-start.4 = (bf16[320,1024]{1,0:T(8,128)(2,1)S(1)}, bf16[320,1024]{1,0:T(8,128)(2,1)}, u32[]{:S(2)}, u32[]{:S(2)}) collective-permute-start(bf16[320,1024]{1,0:T(8,128)(2,1)S(1)} %bitcast.35), channel_id=1, source_target_pairs={{0,1},{1,0},{2,3},{3,2},{4,5},{5,4},{6,7},{7,6},{8,9},{9,8},{10,11... | collective-permute-start | bytes 1966088 | tf_op jit(solution)/shard_map/ppermute | solution.py:309
  57.2 2.2 %collective-permute-start.5 = (bf16[320,1024]{1,0:T(8,128)(2,1)S(1)}, bf16[320,1024]{1,0:T(8,128)(2,1)S(1)}, u32[]{:S(2)}, u32[]{:S(2)}) collective-permute-start(bf16[320,1024]{1,0:T(8,128)(2,1)S(1)} %get-tuple-element.40), channel_id=1, source_target_pairs={{0,1},{1,0},{2,3},{3,2},{4,5},{5,4},{6,7},{7,6},{8,9},{9,8},{10,11... | collective-permute-start | bytes 1966088 | tf_op jit(solution)/shard_map/ppermute | solution.py:309
  59.3 8.6 %copy-start.9 = (bf16[320,1024]{1,0:T(8,128)(2,1)S(1)}, bf16[320,1024]{1,0:T(8,128)(2,1)}, u32[]{:S(2)}) copy-start(bf16[320,1024]{1,0:T(8,128)(2,1)} %get-tuple-element.52) | copy-start | bytes 1966084
  64.3 4.3 %copy-start.5 = (bf16[8,40,2176]{2,1,0:T(8,128)(2,1)}, bf16[8,40,2176]{2,1,0:T(8,128)(2,1)S(1)}, u32[]{:S(2)}) copy-start(bf16[8,40,2176]{2,1,0:T(8,128)(2,1)S(1)} %all-to-all-done.2) | copy-start | bytes 4177924
  64.3 19.6 %collective-permute-start.6 = (bf16[320,2176]{1,0:T(8,128)(2,1)S(1)}, bf16[320,2176]{1,0:T(8,128)(2,1)}, u32[]{:S(2)}, u32[]{:S(2)}) collective-permute-start(bf16[320,2176]{1,0:T(8,128)(2,1)S(1)} %bitcast.29), channel_id=1, source_target_pairs={{0,1},{1,0},{2,3},{3,2},{4,5},{5,4},{6,7},{7,6},{8,9},{9,8},{10,11... | collective-permute-start | bytes 4177928 | tf_op jit(solution)/shard_map/ppermute | solution.py:309
  64.3 14.7 %all-to-all-start.3 = ((bf16[8,40,1024]{2,1,0:T(8,128)(2,1)}), bf16[8,40,1024]{2,1,0:T(8,128)(2,1)S(1)}, u32[]{:S(2)}, u32[]{:S(2)}) async-start(bf16[8,40,1024]{2,1,0:T(8,128)(2,1)} %bitcast.17), calls=%async_computation.3 | async-start | bytes 1310720 | tf_op jit(solution)/shard_map/all_to_all | solution.py:304
  67.9 2.3 %copy-start.4 = (bf16[320,1024]{1,0:T(8,128)(2,1)S(1)}, bf16[320,1024]{1,0:T(8,128)(2,1)}, u32[]{:S(2)}) copy-start(bf16[320,1024]{1,0:T(8,128)(2,1)} %get-tuple-element.51.a_ref) | copy-start | bytes 1966084
  67.9 2.3 %collective-permute-start.7 = (bf16[320,1024]{1,0:T(8,128)(2,1)S(1)}, bf16[320,1024]{1,0:T(8,128)(2,1)S(1)}, u32[]{:S(2)}, u32[]{:S(2)}) collective-permute-start(bf16[320,1024]{1,0:T(8,128)(2,1)S(1)} %copy-done.9), channel_id=1, source_target_pairs={{0,1},{1,0},{2,3},{3,2},{4,5},{5,4},{6,7},{7,6},{8,9},{9,8},{10,11... | collective-permute-start | bytes 1966088 | tf_op jit(solution)/shard_map/ppermute | solution.py:309
  79.6 15.3 %collective-permute-start.8 = (bf16[128,1024]{1,0:T(8,128)(2,1)S(1)}, bf16[128,1024]{1,0:T(8,128)(2,1)S(1)}, u32[]{:S(2)}, u32[]{:S(2)}) collective-permute-start(bf16[128,1024]{1,0:T(8,128)(2,1)S(1)} %shard_map.129), channel_id=1, source_target_pairs={{0,16},{2,18},{4,20},{6,22},{8,24},{10,26},{12,28},{14,30},{16,0},... | collective-permute-start | bytes 786440 | tf_op jit(solution)/shard_map/ppermute | solution.py:300
  80.2 18.6 %all-to-all-start.4 = ((bf16[8,40,1024]{2,1,0:T(8,128)(2,1)}), bf16[8,40,1024]{2,1,0:T(8,128)(2,1)S(1)}, u32[]{:S(2)}, u32[]{:S(2)}) async-start(bf16[8,40,1024]{2,1,0:T(8,128)(2,1)} %bitcast.19), calls=%async_computation.4 | async-start | bytes 1310720 | tf_op jit(solution)/shard_map/all_to_all | solution.py:304

commit v6 on v5

--- a/solution.py
+++ b/solution.py
@@ -371,7 +371,7 @@
     )(first, about, about_mate)
 
     cot_mine = my_features(after(cotangent, about), 1)
-    cot_mate = to_mate(after(cot_mine, tok_mate))
+    cot_mate = to_mate(after(cot_mine, send_mate))
     send_cot = pl.pallas_call(
         functools.partial(cot_kernel, top, half, capacity),
         out_shape=shape((slots, 2 * width + LANES), BF16),

time: 100 us -> 100 us (level)
  waiting for transfers between devices: 43.5 us -> 42.2 us
    all_to_all x5, waiting for transfers between devices: 33.4 us -> 29.6 us  [exchange(): lax.all_to_all(value, 'dp', split_axis=0, concat_axis=0, axis_index_group...]
    ppermute x4, waiting for transfers between devices: 4.41 us -> 7.02 us  [to_mate(): return lax.ppermute(value, 'dp', mates)]
where the time goes in v6:
time: 100 us; the launch traced here: 99.5 us
  waiting for transfers between devices  42.2 us (42%)
  Pallas kernels  30.4 us (30%)
  starting transfers between devices  25.9 us (26%)
    all_to_all x5, waiting for transfers between devices, exchange(): lax.all_to_all(value, 'dp', split_axis=0, concat_axis=0, axis_index_group...  29.6 us
    all_to_all x5, starting transfers between devices, exchange(): lax.all_to_all(value, 'dp', split_axis=0, concat_axis=0, axis_index_group...  19.4 us
    pallas_call x1, Pallas kernels, body(): pl.pallas_call(functools.partial(gradients_kernel, n, m, capacity, float(...  11 us
    pallas_call x1, Pallas kernels, body(): pl.pallas_call(functools.partial(forward_kernel, n, m, step), out_shape=[...  8.59 us
    ppermute x4, waiting for transfers between devices, to_mate(): return lax.ppermute(value, 'dp', mates)  7.02 us
    ppermute x5, waiting for transfers between devices, swapped(): return lax.ppermute(value, 'tensor', [(0, 1), (1, 0)])  5.61 us
    ppermute x4, starting transfers between devices, to_mate(): return lax.ppermute(value, 'dp', mates)  5.6 us
    pallas_call x2, Pallas kernels, gathered(): pl.pallas_call(functools.partial(gather_kernel, top, half, capacity), out...  2.56 us
  transfers between devices with their start and end apart: 14, of which 10 were waited for; matrix products, arithmetic and copies ran while one was open for 0% of the time, Pallas kernels for 28%

profile of v6, /device:TPU:0, one launch (start us, length us, event | category | flops | bytes accessed | tf_op | source)
XLA Modules:
  0.0 99.5 jit_solution(16584798699461457907)
XLA Ops:
  0.6 0.0 copy-start
  0.6 0.0 copy-start.2
  0.7 0.0 copy-start.3
  0.7 0.0 copy-start.1
  0.7 1.0 shard_map.120.x_ref
  1.7 4.1 %collective-permute-start.1 = (bf16[128,1024]{1,0:T(8,128)(2,1)S(1)}, bf16[128,1024]{1,0:T(8,128)(2,1)S(1)}, u32[]{:S(2)}, u32[]{:S(2)}) collective-permute-start(bf16[128,1024]{1,0:T(8,128)(2,1)S(1)} %shard_map.120.x_ref), channel_id=1, source_target_pairs={{0,16},{2,18},{4,20},{6,22},{8,24},{10,26},{12,28},{14,30},{16,0},... | collective-permute-start | bytes 786440 | tf_op jit(solution)/shard_map/ppermute | solution.py:300
  5.8 0.0 copy-done
  5.8 0.0 copy-done.2
  5.8 0.0 copy-done.3
  5.8 0.0 copy-done.1
  5.8 0.6 shard_map.121.info_ref
  6.3 0.1 collective-permute-start
  6.4 1.3 %shard_map.126 = bf16[320,1024]{1,0:T(8,128)(2,1)} custom-call(s32[1]{0:T(128)} %bitcast.first_ref, f32[16,128]{1,0:T(8,128)S(1)} %shard_map.121.info_ref, bf16[128,1024]{1,0:T(8,128)(2,1)S(1)} %shard_map.120.x_ref), custom_call_target="tpu_custom_call" | custom-call | flops 1000000000 | bytes 3000000 | tf_op jit(solution)/shard_map/pallas_call | solution.py:349
  7.7 5.0 %all-to-all-start = ((bf16[8,40,1024]{2,1,0:T(8,128)(2,1)}), bf16[8,40,1024]{2,1,0:T(8,128)(2,1)S(1)}, u32[]{:S(2)}, u32[]{:S(2)}) async-start(bf16[8,40,1024]{2,1,0:T(8,128)(2,1)} %bitcast.8), calls=%async_computation | async-start | bytes 1310720 | tf_op jit(solution)/shard_map/all_to_all | solution.py:304
  12.8 1.0 shard_map.123.x_ref
  13.7 4.4 %collective-permute-done.info2_ref.info_ref = f32[16,128]{1,0:T(8,128)S(1)} collective-permute-done((f32[16,128]{1,0:T(8,128)S(1)}, f32[16,128]{1,0:T(8,128)S(1)}, u32[]{:S(2)}, u32[]{:S(2)}) %collective-permute-start) | collective-permute-done | bytes 8224 | tf_op jit(solution)/shard_map/ppermute | solution.py:300
  18.1 0.0 collective-permute-done.1.x_ref
  18.1 1.3 %shard_map.124 = bf16[320,1024]{1,0:T(8,128)(2,1)} custom-call(s32[1]{0:T(128)} %bitcast.first_ref, f32[16,128]{1,0:T(8,128)S(1)} %collective-permute-done.info2_ref.info_ref, bf16[128,1024]{1,0:T(8,128)(2,1)S(1)} %collective-permute-done.1.x_ref), custom_call_target="tpu_custom_call" | custom-call | flops 20000000000 | bytes 60000000 | tf_op jit(solution)/shard_map/pallas_call | solution.py:349
  19.4 0.0 collective-permute-start.2
  19.4 7.8 %all-to-all-done = bf16[8,40,1024]{2,1,0:T(8,128)(2,1)S(1)} async-done(((bf16[8,40,1024]{2,1,0:T(8,128)(2,1)}), bf16[8,40,1024]{2,1,0:T(8,128)(2,1)S(1)}, u32[]{:S(2)}, u32[]{:S(2)}) %all-to-all-start) | async-done | bytes 655392 | tf_op jit(solution)/shard_map/all_to_all | solution.py:304
  27.3 0.0 copy-start.6
  27.3 3.5 %all-to-all-start.1 = ((bf16[8,40,1024]{2,1,0:T(8,128)(2,1)}), bf16[8,40,1024]{2,1,0:T(8,128)(2,1)S(1)}, u32[]{:S(2)}, u32[]{:S(2)}) async-start(bf16[8,40,1024]{2,1,0:T(8,128)(2,1)} %bitcast.10), calls=%async_computation.1 | async-start | bytes 1310720 | tf_op jit(solution)/shard_map/all_to_all | solution.py:304
  30.8 2.6 %collective-permute-done.2.x2_ref = bf16[128,1024]{1,0:T(8,128)(2,1)S(1)} collective-permute-done((bf16[128,1024]{1,0:T(8,128)(2,1)S(1)}, bf16[128,1024]{1,0:T(8,128)(2,1)S(1)}, u32[]{:S(2)}, u32[]{:S(2)}) %collective-permute-start.2) | collective-permute-done | bytes 262176 | tf_op jit(solution)/shard_map/ppermute | solution.py:300
  33.4 1.9 %shard_map.125 = bf16[320,2176]{1,0:T(8,128)(2,1)} custom-call(s32[1]{0:T(128)} %bitcast.first_ref, f32[16,128]{1,0:T(8,128)S(1)} %shard_map.121.info_ref, f32[16,128]{1,0:T(8,128)S(1)} %collective-permute-done.info2_ref.info_ref, bf16[128,1024]{1,0:T(8,128)(2,1)S(1)} %shard_map.123.x_ref, bf16[128,1024]{1,0:T(8,128)(2,1)S(1)} %collective-permute-done.2.x2_ref), custom_call_target="tpu_custom_call" | custom-call | flops 15000000512 | bytes 45000000 | tf_op jit(solution)/shard_map/pallas_call | solution.py:375
  35.3 0.0 copy-done.6
  35.3 0.0 collective-permute-start.3
  35.3 6.1 %all-to-all-done.1 = bf16[8,40,1024]{2,1,0:T(8,128)(2,1)S(1)} async-done(((bf16[8,40,1024]{2,1,0:T(8,128)(2,1)}), bf16[8,40,1024]{2,1,0:T(8,128)(2,1)S(1)}, u32[]{:S(2)}, u32[]{:S(2)}) %all-to-all-start.1) | async-done | bytes 655392 | tf_op jit(solution)/shard_map/all_to_all | solution.py:304
  41.4 0.0 copy-start.7
  41.4 3.6 %all-to-all-start.2 = ((bf16[8,40,2176]{2,1,0:T(8,128)(2,1)}), bf16[8,40,2176]{2,1,0:T(8,128)(2,1)S(1)}, u32[]{:S(2)}, u32[]{:S(2)}) async-start(bf16[8,40,2176]{2,1,0:T(8,128)(2,1)} %bitcast.12), calls=%async_computation.2 | async-start | bytes 2785280 | tf_op jit(solution)/shard_map/all_to_all | solution.py:304
  45.0 0.0 collective-permute-done.3.refs_1_.refs_3_
  45.0 0.0 copy-start.8
  45.0 0.1 collective-permute-start.4
  45.1 0.1 pad_add_fusion.at_ref
  45.2 2.1 %collective-permute-done.4.refs_3_.refs_5_ = bf16[320,1024]{1,0:T(8,128)(2,1)} collective-permute-done((bf16[320,1024]{1,0:T(8,128)(2,1)S(1)}, bf16[320,1024]{1,0:T(8,128)(2,1)}, u32[]{:S(2)}, u32[]{:S(2)}) %collective-permute-start.4) | collective-permute-done | bytes 655392 | tf_op jit(solution)/shard_map/ppermute | solution.py:309
  47.3 0.0 copy-done.7
  47.3 0.0 copy-done.8
  47.3 8.6 %shard_map.127 = (bf16[640,512]{1,0:T(8,128)(2,1)}, bf16[640,512]{1,0:T(8,128)(2,1)}, bf16[640,512]{1,0:T(8,128)(2,1)}, bf16[320,1024]{1,0:T(8,128)(2,1)S(1)}, b...) custom-call(s32[4]{0:T(128)S(1)} %pad_add_fusion.at_ref, ...), custom_call_target="tpu_custom_call" | custom-call | flops 8000000000 | bytes 24000000 | tf_op jit(solution)/shard_map/pallas_call | solution.py:427
  55.9 0.2 collective-permute-start.5
  56.1 2.0 %collective-permute-done.5.b_ref = bf16[320,1024]{1,0:T(8,128)(2,1)S(1)} collective-permute-done((bf16[320,1024]{1,0:T(8,128)(2,1)S(1)}, bf16[320,1024]{1,0:T(8,128)(2,1)S(1)}, u32[]{:S(2)}, u32[]{:S(2)}) %collective-permute-start.5) | collective-permute-done | bytes 655392 | tf_op jit(solution)/shard_map/ppermute | solution.py:309
  58.1 0.0 copy-start.9
  58.1 1.0 %shard_map.128 = bf16[320,1024]{1,0:T(8,128)(2,1)} custom-call(bf16[320,1024]{1,0:T(8,128)(2,1)S(1)} %get-tuple-element.39.a_ref, bf16[320,1024]{1,0:T(8,128)(2,1)S(1)} %collective-permute-done.5.b_ref), custom_call_target="tpu_custom_call" | custom-call | flops 1000000000 | bytes 3000000 | tf_op jit(solution)/shard_map/pallas_call | solution.py:417
  59.1 4.0 %all-to-all-done.2 = bf16[8,40,2176]{2,1,0:T(8,128)(2,1)S(1)} async-done(((bf16[8,40,2176]{2,1,0:T(8,128)(2,1)}), bf16[8,40,2176]{2,1,0:T(8,128)(2,1)S(1)}, u32[]{:S(2)}, u32[]{:S(2)}) %all-to-all-start.2) | async-done | bytes 1392672 | tf_op jit(solution)/shard_map/all_to_all | solution.py:304
  63.1 0.0 copy-start.5
  63.1 0.0 collective-permute-start.6
  63.1 3.5 %all-to-all-start.3 = ((bf16[8,40,1024]{2,1,0:T(8,128)(2,1)}), bf16[8,40,1024]{2,1,0:T(8,128)(2,1)S(1)}, u32[]{:S(2)}, u32[]{:S(2)}) async-start(bf16[8,40,1024]{2,1,0:T(8,128)(2,1)} %bitcast.17), calls=%async_computation.3 | async-start | bytes 1310720 | tf_op jit(solution)/shard_map/all_to_all | solution.py:304
  66.6 0.0 copy-start.4
  66.7 0.0 copy-done.9
  66.7 0.6 collective-permute-start.7
  67.2 0.2 shard_map.122
  67.4 0.0 copy-done.5
  67.4 1.5 %collective-permute-done.7.b_ref = bf16[320,1024]{1,0:T(8,128)(2,1)S(1)} collective-permute-done((bf16[320,1024]{1,0:T(8,128)(2,1)S(1)}, bf16[320,1024]{1,0:T(8,128)(2,1)S(1)}, u32[]{:S(2)}, u32[]{:S(2)}) %collective-permute-start.7) | collective-permute-done | bytes 655392 | tf_op jit(solution)/shard_map/ppermute | solution.py:309
  69.0 0.0 copy-done.4
  69.0 1.0 %shard_map.131 = bf16[320,1024]{1,0:T(8,128)(2,1)} custom-call(bf16[320,1024]{1,0:T(8,128)(2,1)S(1)} %copy-done.4, bf16[320,1024]{1,0:T(8,128)(2,1)S(1)} %collective-permute-done.7.b_ref), custom_call_target="tpu_custom_call" | custom-call | flops 1000000000 | bytes 3000000 | tf_op jit(solution)/shard_map/pallas_call | solution.py:417
  70.0 7.8 %all-to-all-done.3 = bf16[8,40,1024]{2,1,0:T(8,128)(2,1)S(1)} async-done(((bf16[8,40,1024]{2,1,0:T(8,128)(2,1)}), bf16[8,40,1024]{2,1,0:T(8,128)(2,1)S(1)}, u32[]{:S(2)}, u32[]{:S(2)}) %all-to-all-start.3) | async-done | bytes 655392 | tf_op jit(solution)/shard_map/all_to_all | solution.py:304
  77.8 0.5 shard_map.129
  78.3 1.4 %collective-permute-start.8 = (bf16[128,1024]{1,0:T(8,128)(2,1)S(1)}, bf16[128,1024]{1,0:T(8,128)(2,1)S(1)}, u32[]{:S(2)}, u32[]{:S(2)}) collective-permute-start(bf16[128,1024]{1,0:T(8,128)(2,1)S(1)} %shard_map.129), channel_id=1, source_target_pairs={{0,16},{2,18},{4,20},{6,22},{8,24},{10,26},{12,28},{14,30},{16,0},... | collective-permute-start | bytes 786440 | tf_op jit(solution)/shard_map/ppermute | solution.py:300
  79.7 3.7 %all-to-all-start.4 = ((bf16[8,40,1024]{2,1,0:T(8,128)(2,1)}), bf16[8,40,1024]{2,1,0:T(8,128)(2,1)S(1)}, u32[]{:S(2)}, u32[]{:S(2)}) async-start(bf16[8,40,1024]{2,1,0:T(8,128)(2,1)} %bitcast.19), calls=%async_computation.4 | async-start | bytes 1310720 | tf_op jit(solution)/shard_map/all_to_all | solution.py:304
  83.4 0.0 collective-permute-done.6.refs_1_
  83.4 11.0 %shard_map.130 = (bf16[512,2048]{1,0:T(8,128)(2,1)}, bf16[512,2048]{1,0:T(8,128)(2,1)}, bf16[512,2048]{1,0:T(8,128)(2,1)}) custom-call(s32[4]{0:T(128)S(1)} %pad_add_fusion.at_ref, bf16[320,2176]{1,0:T(8,128)(2,1)} %bitcast.30, bf16[320,2176]{1,0:T(8,128)(2,1)} %collective-permute-done.6.refs_1_, bf16[320,1024]{1,0:T(8,128)(2,1)} %bitcast.34, ...), custom_call_target="tpu_custom_call" | custom-call | flops 20000000000 | bytes 60000000 | tf_op jit(solution)/shard_map/pallas_call | solution.py:455
  94.4 0.0 collective-permute-done.8.rest_0_
  94.4 3.9 %all-to-all-done.4 = bf16[8,40,1024]{2,1,0:T(8,128)(2,1)S(1)} async-done(((bf16[8,40,1024]{2,1,0:T(8,128)(2,1)}), bf16[8,40,1024]{2,1,0:T(8,128)(2,1)S(1)}, u32[]{:S(2)}, u32[]{:S(2)}) %all-to-all-start.4) | async-done | bytes 655392 | tf_op jit(solution)/shard_map/all_to_all | solution.py:304
  98.3 1.2 %shard_map.132 = bf16[128,1024]{1,0:T(8,128)(2,1)} custom-call(bf16[320,128]{1,0:T(8,128)(2,1)S(1)} %get-tuple-element.49.high_ref, bf16[320,128]{1,0:T(8,128)(2,1)S(1)} %get-tuple-element.50.low_ref, bf16[320,1024]{1,0:T(8,128)(2,1)S(1)} %bitcast.24, bf16[128,1024]{1,0:T(8,128)(2,1)S(1)} %collective-permute-done.8.rest_0_), custom_call_target="tpu_custom_call" | custom-call | flops 1000000000 | bytes 3000000 | tf_op jit(solution)/shard_map/pallas_call | solution.py:326
Async XLA Ops:
  0.6 5.1 %copy-start = (s32[128,4]{0,1:T(4,128)S(1)}, s32[128,4]{0,1:T(4,128)}, u32[]{:S(2)}) copy-start(s32[128,4]{0,1:T(4,128)} %param.11) | copy-start | bytes 6148
  0.6 5.1 %copy-start.2 = (s32[2]{0:T(128)S(1)}, s32[2]{0:T(128)}, u32[]{:S(2)}) copy-start(s32[2]{0:T(128)} %lengths_ref.1) | copy-start | bytes 28
  0.7 5.1 %copy-start.3 = (s32[128]{0:T(128)S(1)}, s32[128]{0:T(128)}, u32[]{:S(2)}) copy-start(s32[128]{0:T(128)} %param.13) | copy-start | bytes 1540
  0.7 5.1 %copy-start.1 = (f32[128,4]{0,1:T(4,128)S(1)}, f32[128,4]{0,1:T(4,128)}, u32[]{:S(2)}) copy-start(f32[128,4]{0,1:T(4,128)} %param.12) | copy-start | bytes 6148
  1.7 16.5 %collective-permute-start.1 = (bf16[128,1024]{1,0:T(8,128)(2,1)S(1)}, bf16[128,1024]{1,0:T(8,128)(2,1)S(1)}, u32[]{:S(2)}, u32[]{:S(2)}) collective-permute-start(bf16[128,1024]{1,0:T(8,128)(2,1)S(1)} %shard_map.120.x_ref), channel_id=1, source_target_pairs={{0,16},{2,18},{4,20},{6,22},{8,24},{10,26},{12,28},{14,30},{16,0},... | collective-permute-start | bytes 786440 | tf_op jit(solution)/shard_map/ppermute | solution.py:300
  6.3 11.8 %collective-permute-start = (f32[16,128]{1,0:T(8,128)S(1)}, f32[16,128]{1,0:T(8,128)S(1)}, u32[]{:S(2)}, u32[]{:S(2)}) collective-permute-start(f32[16,128]{1,0:T(8,128)S(1)} %shard_map.121.info_ref), channel_id=1, source_target_pairs={{0,16},{2,18},{4,20},{6,22},{8,24},{10,26},{12,28},{14,30},{16,0},... | collective-permute-start | bytes 24584 | tf_op jit(solution)/shard_map/ppermute | solution.py:300
  7.7 19.5 %all-to-all-start = ((bf16[8,40,1024]{2,1,0:T(8,128)(2,1)}), bf16[8,40,1024]{2,1,0:T(8,128)(2,1)S(1)}, u32[]{:S(2)}, u32[]{:S(2)}) async-start(bf16[8,40,1024]{2,1,0:T(8,128)(2,1)} %bitcast.8), calls=%async_computation | async-start | bytes 1310720 | tf_op jit(solution)/shard_map/all_to_all | solution.py:304
  19.4 14.0 %collective-permute-start.2 = (bf16[128,1024]{1,0:T(8,128)(2,1)S(1)}, bf16[128,1024]{1,0:T(8,128)(2,1)S(1)}, u32[]{:S(2)}, u32[]{:S(2)}) collective-permute-start(bf16[128,1024]{1,0:T(8,128)(2,1)S(1)} %shard_map.123.x_ref), channel_id=1, source_target_pairs={{0,16},{2,18},{4,20},{6,22},{8,24},{10,26},{12,28},{14,30},{16,0},... | collective-permute-start | bytes 786440 | tf_op jit(solution)/shard_map/ppermute | solution.py:300
  27.3 8.1 %copy-start.6 = (bf16[8,40,1024]{2,1,0:T(8,128)(2,1)}, bf16[8,40,1024]{2,1,0:T(8,128)(2,1)S(1)}, u32[]{:S(2)}) copy-start(bf16[8,40,1024]{2,1,0:T(8,128)(2,1)S(1)} %all-to-all-done) | copy-start | bytes 1966084
  27.3 14.2 %all-to-all-start.1 = ((bf16[8,40,1024]{2,1,0:T(8,128)(2,1)}), bf16[8,40,1024]{2,1,0:T(8,128)(2,1)S(1)}, u32[]{:S(2)}, u32[]{:S(2)}) async-start(bf16[8,40,1024]{2,1,0:T(8,128)(2,1)} %bitcast.10), calls=%async_computation.1 | async-start | bytes 1310720 | tf_op jit(solution)/shard_map/all_to_all | solution.py:304
  35.3 9.7 %collective-permute-start.3 = (bf16[320,1024]{1,0:T(8,128)(2,1)S(1)}, bf16[320,1024]{1,0:T(8,128)(2,1)S(1)}, u32[]{:S(2)}, u32[]{:S(2)}) collective-permute-start(bf16[320,1024]{1,0:T(8,128)(2,1)S(1)} %bitcast.32), channel_id=1, source_target_pairs={{0,1},{1,0},{2,3},{3,2},{4,5},{5,4},{6,7},{7,6},{8,9},{9,8},{10,11... | collective-permute-start | bytes 1966088 | tf_op jit(solution)/shard_map/ppermute | solution.py:309
  41.4 5.9 %copy-start.7 = (bf16[8,40,1024]{2,1,0:T(8,128)(2,1)}, bf16[8,40,1024]{2,1,0:T(8,128)(2,1)S(1)}, u32[]{:S(2)}) copy-start(bf16[8,40,1024]{2,1,0:T(8,128)(2,1)S(1)} %all-to-all-done.1) | copy-start | bytes 1966084
  41.4 21.7 %all-to-all-start.2 = ((bf16[8,40,2176]{2,1,0:T(8,128)(2,1)}), bf16[8,40,2176]{2,1,0:T(8,128)(2,1)S(1)}, u32[]{:S(2)}, u32[]{:S(2)}) async-start(bf16[8,40,2176]{2,1,0:T(8,128)(2,1)} %bitcast.12), calls=%async_computation.2 | async-start | bytes 2785280 | tf_op jit(solution)/shard_map/all_to_all | solution.py:304
  45.0 2.3 %copy-start.8 = (bf16[320,1024]{1,0:T(8,128)(2,1)}, bf16[320,1024]{1,0:T(8,128)(2,1)S(1)}, u32[]{:S(2)}) copy-start(bf16[320,1024]{1,0:T(8,128)(2,1)S(1)} %collective-permute-done.3.refs_1_.refs_3_) | copy-start | bytes 1966084
  45.0 2.3 %collective-permute-start.4 = (bf16[320,1024]{1,0:T(8,128)(2,1)S(1)}, bf16[320,1024]{1,0:T(8,128)(2,1)}, u32[]{:S(2)}, u32[]{:S(2)}) collective-permute-start(bf16[320,1024]{1,0:T(8,128)(2,1)S(1)} %bitcast.35), channel_id=1, source_target_pairs={{0,1},{1,0},{2,3},{3,2},{4,5},{5,4},{6,7},{7,6},{8,9},{9,8},{10,11... | collective-permute-start | bytes 1966088 | tf_op jit(solution)/shard_map/ppermute | solution.py:309
  55.9 2.2 %collective-permute-start.5 = (bf16[320,1024]{1,0:T(8,128)(2,1)S(1)}, bf16[320,1024]{1,0:T(8,128)(2,1)S(1)}, u32[]{:S(2)}, u32[]{:S(2)}) collective-permute-start(bf16[320,1024]{1,0:T(8,128)(2,1)S(1)} %get-tuple-element.40), channel_id=1, source_target_pairs={{0,1},{1,0},{2,3},{3,2},{4,5},{5,4},{6,7},{7,6},{8,9},{9,8},{10,11... | collective-permute-start | bytes 1966088 | tf_op jit(solution)/shard_map/ppermute | solution.py:309
  58.1 8.6 %copy-start.9 = (bf16[320,1024]{1,0:T(8,128)(2,1)S(1)}, bf16[320,1024]{1,0:T(8,128)(2,1)}, u32[]{:S(2)}) copy-start(bf16[320,1024]{1,0:T(8,128)(2,1)} %get-tuple-element.52) | copy-start | bytes 1966084
  63.1 4.3 %copy-start.5 = (bf16[8,40,2176]{2,1,0:T(8,128)(2,1)}, bf16[8,40,2176]{2,1,0:T(8,128)(2,1)S(1)}, u32[]{:S(2)}) copy-start(bf16[8,40,2176]{2,1,0:T(8,128)(2,1)S(1)} %all-to-all-done.2) | copy-start | bytes 4177924
  63.1 20.3 %collective-permute-start.6 = (bf16[320,2176]{1,0:T(8,128)(2,1)S(1)}, bf16[320,2176]{1,0:T(8,128)(2,1)}, u32[]{:S(2)}, u32[]{:S(2)}) collective-permute-start(bf16[320,2176]{1,0:T(8,128)(2,1)S(1)} %bitcast.29), channel_id=1, source_target_pairs={{0,1},{1,0},{2,3},{3,2},{4,5},{5,4},{6,7},{7,6},{8,9},{9,8},{10,11... | collective-permute-start | bytes 4177928 | tf_op jit(solution)/shard_map/ppermute | solution.py:309
  63.1 14.7 %all-to-all-start.3 = ((bf16[8,40,1024]{2,1,0:T(8,128)(2,1)}), bf16[8,40,1024]{2,1,0:T(8,128)(2,1)S(1)}, u32[]{:S(2)}, u32[]{:S(2)}) async-start(bf16[8,40,1024]{2,1,0:T(8,128)(2,1)} %bitcast.17), calls=%async_computation.3 | async-start | bytes 1310720 | tf_op jit(solution)/shard_map/all_to_all | solution.py:304
  66.6 2.3 %copy-start.4 = (bf16[320,1024]{1,0:T(8,128)(2,1)S(1)}, bf16[320,1024]{1,0:T(8,128)(2,1)}, u32[]{:S(2)}) copy-start(bf16[320,1024]{1,0:T(8,128)(2,1)} %get-tuple-element.51.a_ref) | copy-start | bytes 1966084
  66.7 2.3 %collective-permute-start.7 = (bf16[320,1024]{1,0:T(8,128)(2,1)S(1)}, bf16[320,1024]{1,0:T(8,128)(2,1)S(1)}, u32[]{:S(2)}, u32[]{:S(2)}) collective-permute-start(bf16[320,1024]{1,0:T(8,128)(2,1)S(1)} %copy-done.9), channel_id=1, source_target_pairs={{0,1},{1,0},{2,3},{3,2},{4,5},{5,4},{6,7},{7,6},{8,9},{9,8},{10,11... | collective-permute-start | bytes 1966088 | tf_op jit(solution)/shard_map/ppermute | solution.py:309
  78.3 16.1 %collective-permute-start.8 = (bf16[128,1024]{1,0:T(8,128)(2,1)S(1)}, bf16[128,1024]{1,0:T(8,128)(2,1)S(1)}, u32[]{:S(2)}, u32[]{:S(2)}) collective-permute-start(bf16[128,1024]{1,0:T(8,128)(2,1)S(1)} %shard_map.129), channel_id=1, source_target_pairs={{0,16},{2,18},{4,20},{6,22},{8,24},{10,26},{12,28},{14,30},{16,0},... | collective-permute-start | bytes 786440 | tf_op jit(solution)/shard_map/ppermute | solution.py:300
  79.7 18.6 %all-to-all-start.4 = ((bf16[8,40,1024]{2,1,0:T(8,128)(2,1)}), bf16[8,40,1024]{2,1,0:T(8,128)(2,1)S(1)}, u32[]{:S(2)}, u32[]{:S(2)}) async-start(bf16[8,40,1024]{2,1,0:T(8,128)(2,1)} %bitcast.19), calls=%async_computation.4 | async-start | bytes 1310720 | tf_op jit(solution)/shard_map/all_to_all | solution.py:304

commit v7 on v6

--- a/solution.py
+++ b/solution.py
@@ -468,9 +468,9 @@
             pltpu.SemaphoreType.DMA((4 * n + 3 * m + 5,)),
         ],
         compiler_params=roomy,
-        cost_estimate=cost(20),
+        cost_estimate=cost(12),
     )(at, *[in_hbm(x) for x in cots], *toks, in_hbm(recv_cot), weights[2], *keeps)
-    back_own = exchange(after(out_own, mix_mate)).reshape(slots, width)
+    back_own = exchange(after(out_own, back_mate)).reshape(slots, width)
     mixed = mixed_rows([after(spreads[0], grad_down), spreads[1]], back_own, mix_far)
     return (
         mixed,

time: 100 us -> 98.8 us (0.988)
  waiting for transfers between devices: 42.2 us -> 40.2 us
    all_to_all x5, waiting for transfers between devices: 29.6 us -> 27.6 us  [exchange(): lax.all_to_all(value, 'dp', split_axis=0, concat_axis=0, axis_index_group...]
  transfers between devices with their start and end apart: 14 -> 14, of which waited for: 10 -> 10; matrix products, arithmetic and copies ran while one was open for 0% -> 0% of each run, Pallas kernels for 28% -> 29%
where the time goes in v7:
time: 98.8 us; the launch traced here: 98.3 us
  waiting for transfers between devices  40.2 us (41%)
  Pallas kernels  30.4 us (31%)
  starting transfers between devices  25.9 us (26%)
    all_to_all x5, waiting for transfers between devices, exchange(): lax.all_to_all(value, 'dp', split_axis=0, concat_axis=0, axis_index_group...  27.6 us
    all_to_all x5, starting transfers between devices, exchange(): lax.all_to_all(value, 'dp', split_axis=0, concat_axis=0, axis_index_group...  19.4 us
    pallas_call x1, Pallas kernels, body(): pl.pallas_call(functools.partial(gradients_kernel, n, m, capacity, float(...  11 us
    pallas_call x1, Pallas kernels, body(): pl.pallas_call(functools.partial(forward_kernel, n, m, step), out_shape=[...  8.59 us
    ppermute x4, waiting for transfers between devices, to_mate(): return lax.ppermute(value, 'dp', mates)  6.91 us
    ppermute x5, waiting for transfers between devices, swapped(): return lax.ppermute(value, 'tensor', [(0, 1), (1, 0)])  5.69 us
    ppermute x4, starting transfers between devices, to_mate(): return lax.ppermute(value, 'dp', mates)  5.61 us
    pallas_call x2, Pallas kernels, gathered(): pl.pallas_call(functools.partial(gather_kernel, top, half, capacity), out...  2.56 us
  transfers between devices with their start and end apart: 14, of which 10 were waited for; matrix products, arithmetic and copies ran while one was open for 0% of the time, Pallas kernels for 29%

profile of v7, /device:TPU:0, one launch (start us, length us, event | category | flops | bytes accessed | tf_op | source)
XLA Modules:
  0.0 98.3 jit_solution(10654626788181058850)
XLA Ops:
  0.6 0.0 copy-start
  0.6 0.0 copy-start.2
  0.7 0.0 copy-start.3
  0.7 0.0 copy-start.1
  0.7 1.0 shard_map.120.x_ref
  1.7 4.1 %collective-permute-start.1 = (bf16[128,1024]{1,0:T(8,128)(2,1)S(1)}, bf16[128,1024]{1,0:T(8,128)(2,1)S(1)}, u32[]{:S(2)}, u32[]{:S(2)}) collective-permute-start(bf16[128,1024]{1,0:T(8,128)(2,1)S(1)} %shard_map.120.x_ref), channel_id=1, source_target_pairs={{0,16},{2,18},{4,20},{6,22},{8,24},{10,26},{12,28},{14,30},{16,0},... | collective-permute-start | bytes 786440 | tf_op jit(solution)/shard_map/ppermute | solution.py:300
  5.8 0.0 copy-done
  5.8 0.0 copy-done.2
  5.8 0.0 copy-done.3
  5.8 0.0 copy-done.1
  5.8 0.6 shard_map.121.info_ref
  6.3 0.1 collective-permute-start
  6.4 1.3 %shard_map.126 = bf16[320,1024]{1,0:T(8,128)(2,1)} custom-call(s32[1]{0:T(128)} %bitcast.first_ref, f32[16,128]{1,0:T(8,128)S(1)} %shard_map.121.info_ref, bf16[128,1024]{1,0:T(8,128)(2,1)S(1)} %shard_map.120.x_ref), custom_call_target="tpu_custom_call" | custom-call | flops 1000000000 | bytes 3000000 | tf_op jit(solution)/shard_map/pallas_call | solution.py:349
  7.7 5.0 %all-to-all-start = ((bf16[8,40,1024]{2,1,0:T(8,128)(2,1)}), bf16[8,40,1024]{2,1,0:T(8,128)(2,1)}, u32[]{:S(2)}, u32[]{:S(2)}) async-start(bf16[8,40,1024]{2,1,0:T(8,128)(2,1)} %bitcast.8), calls=%async_computation | async-start | bytes 1310720 | tf_op jit(solution)/shard_map/all_to_all | solution.py:304
  12.8 1.0 shard_map.123.x_ref
  13.7 4.4 %collective-permute-done.info2_ref.info_ref = f32[16,128]{1,0:T(8,128)S(1)} collective-permute-done((f32[16,128]{1,0:T(8,128)S(1)}, f32[16,128]{1,0:T(8,128)S(1)}, u32[]{:S(2)}, u32[]{:S(2)}) %collective-permute-start) | collective-permute-done | bytes 8224 | tf_op jit(solution)/shard_map/ppermute | solution.py:300
  18.1 0.0 collective-permute-done.1.x_ref
  18.1 1.3 %shard_map.124 = bf16[320,1024]{1,0:T(8,128)(2,1)} custom-call(s32[1]{0:T(128)} %bitcast.first_ref, f32[16,128]{1,0:T(8,128)S(1)} %collective-permute-done.info2_ref.info_ref, bf16[128,1024]{1,0:T(8,128)(2,1)S(1)} %collective-permute-done.1.x_ref), custom_call_target="tpu_custom_call" | custom-call | flops 20000000000 | bytes 60000000 | tf_op jit(solution)/shard_map/pallas_call | solution.py:349
  19.4 0.0 collective-permute-start.2
  19.4 8.0 %all-to-all-done = bf16[8,40,1024]{2,1,0:T(8,128)(2,1)} async-done(((bf16[8,40,1024]{2,1,0:T(8,128)(2,1)}), bf16[8,40,1024]{2,1,0:T(8,128)(2,1)}, u32[]{:S(2)}, u32[]{:S(2)}) %all-to-all-start) | async-done | bytes 655392 | tf_op jit(solution)/shard_map/all_to_all | solution.py:304
  27.4 3.5 %all-to-all-start.1 = ((bf16[8,40,1024]{2,1,0:T(8,128)(2,1)}), bf16[8,40,1024]{2,1,0:T(8,128)(2,1)S(1)}, u32[]{:S(2)}, u32[]{:S(2)}) async-start(bf16[8,40,1024]{2,1,0:T(8,128)(2,1)} %bitcast.10), calls=%async_computation.1 | async-start | bytes 1310720 | tf_op jit(solution)/shard_map/all_to_all | solution.py:304
  30.9 2.5 %collective-permute-done.2.x2_ref = bf16[128,1024]{1,0:T(8,128)(2,1)S(1)} collective-permute-done((bf16[128,1024]{1,0:T(8,128)(2,1)S(1)}, bf16[128,1024]{1,0:T(8,128)(2,1)S(1)}, u32[]{:S(2)}, u32[]{:S(2)}) %collective-permute-start.2) | collective-permute-done | bytes 262176 | tf_op jit(solution)/shard_map/ppermute | solution.py:300
  33.4 1.9 %shard_map.125 = bf16[320,2176]{1,0:T(8,128)(2,1)} custom-call(s32[1]{0:T(128)} %bitcast.first_ref, f32[16,128]{1,0:T(8,128)S(1)} %shard_map.121.info_ref, f32[16,128]{1,0:T(8,128)S(1)} %collective-permute-done.info2_ref.info_ref, bf16[128,1024]{1,0:T(8,128)(2,1)S(1)} %shard_map.123.x_ref, bf16[128,1024]{1,0:T(8,128)(2,1)S(1)} %collective-permute-done.2.x2_ref), custom_call_target="tpu_custom_call" | custom-call | flops 15000000512 | bytes 45000000 | tf_op jit(solution)/shard_map/pallas_call | solution.py:375
  35.3 0.0 collective-permute-start.3
  35.3 6.2 %all-to-all-done.1 = bf16[8,40,1024]{2,1,0:T(8,128)(2,1)S(1)} async-done(((bf16[8,40,1024]{2,1,0:T(8,128)(2,1)}), bf16[8,40,1024]{2,1,0:T(8,128)(2,1)S(1)}, u32[]{:S(2)}, u32[]{:S(2)}) %all-to-all-start.1) | async-done | bytes 655392 | tf_op jit(solution)/shard_map/all_to_all | solution.py:304
  41.5 0.0 copy-start.6
  41.5 3.6 %all-to-all-start.2 = ((bf16[8,40,2176]{2,1,0:T(8,128)(2,1)}), bf16[8,40,2176]{2,1,0:T(8,128)(2,1)S(1)}, u32[]{:S(2)}, u32[]{:S(2)}) async-start(bf16[8,40,2176]{2,1,0:T(8,128)(2,1)} %bitcast.12), calls=%async_computation.2 | async-start | bytes 2785280 | tf_op jit(solution)/shard_map/all_to_all | solution.py:304
  45.1 0.0 collective-permute-done.3.refs_1_.refs_3_
  45.1 0.0 copy-start.7
  45.1 0.1 collective-permute-start.4
  45.2 0.1 pad_add_fusion.at_ref
  45.3 2.0 %collective-permute-done.4.refs_3_.refs_5_ = bf16[320,1024]{1,0:T(8,128)(2,1)S(1)} collective-permute-done((bf16[320,1024]{1,0:T(8,128)(2,1)S(1)}, bf16[320,1024]{1,0:T(8,128)(2,1)S(1)}, u32[]{:S(2)}, u32[]{:S(2)}) %collective-permute-start.4) | collective-permute-done | bytes 655392 | tf_op jit(solution)/shard_map/ppermute | solution.py:309
  47.3 0.0 copy-start.8
  47.3 0.0 copy-done.6
  47.3 0.0 copy-done.7
  47.3 0.9 copy-done.8
  48.2 8.6 %shard_map.127 = (bf16[640,512]{1,0:T(8,128)(2,1)}, bf16[640,512]{1,0:T(8,128)(2,1)}, bf16[640,512]{1,0:T(8,128)(2,1)}, bf16[320,1024]{1,0:T(8,128)(2,1)S(1)}, b...) custom-call(s32[4]{0:T(128)S(1)} %pad_add_fusion.at_ref, ...), custom_call_target="tpu_custom_call" | custom-call | flops 8000000000 | bytes 24000000 | tf_op jit(solution)/shard_map/pallas_call | solution.py:427
  56.8 0.2 collective-permute-start.5
  57.0 2.0 %collective-permute-done.5.b_ref = bf16[320,1024]{1,0:T(8,128)(2,1)S(1)} collective-permute-done((bf16[320,1024]{1,0:T(8,128)(2,1)S(1)}, bf16[320,1024]{1,0:T(8,128)(2,1)S(1)}, u32[]{:S(2)}, u32[]{:S(2)}) %collective-permute-start.5) | collective-permute-done | bytes 655392 | tf_op jit(solution)/shard_map/ppermute | solution.py:309
  58.9 1.0 %shard_map.128 = bf16[320,1024]{1,0:T(8,128)(2,1)} custom-call(bf16[320,1024]{1,0:T(8,128)(2,1)S(1)} %get-tuple-element.39.a_ref, bf16[320,1024]{1,0:T(8,128)(2,1)S(1)} %collective-permute-done.5.b_ref), custom_call_target="tpu_custom_call" | custom-call | flops 1000000000 | bytes 3000000 | tf_op jit(solution)/shard_map/pallas_call | solution.py:417
  59.9 3.2 %all-to-all-done.2 = bf16[8,40,2176]{2,1,0:T(8,128)(2,1)S(1)} async-done(((bf16[8,40,2176]{2,1,0:T(8,128)(2,1)}), bf16[8,40,2176]{2,1,0:T(8,128)(2,1)S(1)}, u32[]{:S(2)}, u32[]{:S(2)}) %all-to-all-start.2) | async-done | bytes 1392672 | tf_op jit(solution)/shard_map/all_to_all | solution.py:304
  63.2 0.0 copy-start.5
  63.2 0.0 collective-permute-start.6
  63.2 3.5 %all-to-all-start.3 = ((bf16[8,40,1024]{2,1,0:T(8,128)(2,1)}), bf16[8,40,1024]{2,1,0:T(8,128)(2,1)S(1)}, u32[]{:S(2)}, u32[]{:S(2)}) async-start(bf16[8,40,1024]{2,1,0:T(8,128)(2,1)} %bitcast.17), calls=%async_computation.3 | async-start | bytes 1310720 | tf_op jit(solution)/shard_map/all_to_all | solution.py:304
  66.7 0.0 copy-start.4
  66.8 0.6 collective-permute-start.7
  67.3 0.2 shard_map.122
  67.5 0.0 copy-done.5
  67.5 1.7 %collective-permute-done.7.b_ref = bf16[320,1024]{1,0:T(8,128)(2,1)S(1)} collective-permute-done((bf16[320,1024]{1,0:T(8,128)(2,1)}, bf16[320,1024]{1,0:T(8,128)(2,1)S(1)}, u32[]{:S(2)}, u32[]{:S(2)}) %collective-permute-start.7) | collective-permute-done | bytes 655392 | tf_op jit(solution)/shard_map/ppermute | solution.py:309
  69.3 0.0 copy-done.4
  69.3 1.0 %shard_map.131 = bf16[320,1024]{1,0:T(8,128)(2,1)} custom-call(bf16[320,1024]{1,0:T(8,128)(2,1)S(1)} %copy-done.4, bf16[320,1024]{1,0:T(8,128)(2,1)S(1)} %collective-permute-done.7.b_ref), custom_call_target="tpu_custom_call" | custom-call | flops 1000000000 | bytes 3000000 | tf_op jit(solution)/shard_map/pallas_call | solution.py:417
  70.3 7.6 %all-to-all-done.3 = bf16[8,40,1024]{2,1,0:T(8,128)(2,1)S(1)} async-done(((bf16[8,40,1024]{2,1,0:T(8,128)(2,1)}), bf16[8,40,1024]{2,1,0:T(8,128)(2,1)S(1)}, u32[]{:S(2)}, u32[]{:S(2)}) %all-to-all-start.3) | async-done | bytes 655392 | tf_op jit(solution)/shard_map/all_to_all | solution.py:304
  78.0 3.7 %all-to-all-start.4 = ((bf16[8,40,1024]{2,1,0:T(8,128)(2,1)}), bf16[8,40,1024]{2,1,0:T(8,128)(2,1)S(1)}, u32[]{:S(2)}, u32[]{:S(2)}) async-start(bf16[8,40,1024]{2,1,0:T(8,128)(2,1)} %bitcast.19), calls=%async_computation.4 | async-start | bytes 1310720 | tf_op jit(solution)/shard_map/all_to_all | solution.py:304
  81.7 0.5 shard_map.129
  82.1 1.4 %collective-permute-start.8 = (bf16[128,1024]{1,0:T(8,128)(2,1)S(1)}, bf16[128,1024]{1,0:T(8,128)(2,1)S(1)}, u32[]{:S(2)}, u32[]{:S(2)}) collective-permute-start(bf16[128,1024]{1,0:T(8,128)(2,1)S(1)} %shard_map.129), channel_id=1, source_target_pairs={{0,16},{2,18},{4,20},{6,22},{8,24},{10,26},{12,28},{14,30},{16,0},... | collective-permute-start | bytes 786440 | tf_op jit(solution)/shard_map/ppermute | solution.py:300
  83.5 0.0 collective-permute-done.6.refs_1_
  83.5 11.0 %shard_map.130 = (bf16[512,2048]{1,0:T(8,128)(2,1)}, bf16[512,2048]{1,0:T(8,128)(2,1)}, bf16[512,2048]{1,0:T(8,128)(2,1)}) custom-call(s32[4]{0:T(128)S(1)} %pad_add_fusion.at_ref, bf16[320,2176]{1,0:T(8,128)(2,1)} %bitcast.30, bf16[320,2176]{1,0:T(8,128)(2,1)} %collective-permute-done.6.refs_1_, bf16[320,1024]{1,0:T(8,128)(2,1)} %bitcast.9.refs_0_.refs_2_, ...), custom_call_target="tpu_custom_call" | custom-call | flops 12000000000 | bytes 36000000 | tf_op jit(solution)/shard_map/pallas_call | solution.py:455
  94.5 0.0 collective-permute-done.8.rest_0_
  94.5 2.6 %all-to-all-done.4 = bf16[8,40,1024]{2,1,0:T(8,128)(2,1)S(1)} async-done(((bf16[8,40,1024]{2,1,0:T(8,128)(2,1)}), bf16[8,40,1024]{2,1,0:T(8,128)(2,1)S(1)}, u32[]{:S(2)}, u32[]{:S(2)}) %all-to-all-start.4) | async-done | bytes 655392 | tf_op jit(solution)/shard_map/all_to_all | solution.py:304
  97.1 1.2 %shard_map.132 = bf16[128,1024]{1,0:T(8,128)(2,1)} custom-call(bf16[320,128]{1,0:T(8,128)(2,1)S(1)} %get-tuple-element.49.high_ref, bf16[320,128]{1,0:T(8,128)(2,1)S(1)} %get-tuple-element.50.low_ref, bf16[320,1024]{1,0:T(8,128)(2,1)S(1)} %bitcast.24, bf16[128,1024]{1,0:T(8,128)(2,1)S(1)} %collective-permute-done.8.rest_0_), custom_call_target="tpu_custom_call" | custom-call | flops 1000000000 | bytes 3000000 | tf_op jit(solution)/shard_map/pallas_call | solution.py:326
Async XLA Ops:
  0.6 5.1 %copy-start = (s32[128,4]{0,1:T(4,128)S(1)}, s32[128,4]{0,1:T(4,128)}, u32[]{:S(2)}) copy-start(s32[128,4]{0,1:T(4,128)} %param.11) | copy-start | bytes 6148
  0.6 5.1 %copy-start.2 = (s32[2]{0:T(128)S(1)}, s32[2]{0:T(128)}, u32[]{:S(2)}) copy-start(s32[2]{0:T(128)} %lengths_ref.1) | copy-start | bytes 28
  0.7 5.1 %copy-start.3 = (s32[128]{0:T(128)S(1)}, s32[128]{0:T(128)}, u32[]{:S(2)}) copy-start(s32[128]{0:T(128)} %param.13) | copy-start | bytes 1540
  0.7 5.1 %copy-start.1 = (f32[128,4]{0,1:T(4,128)S(1)}, f32[128,4]{0,1:T(4,128)}, u32[]{:S(2)}) copy-start(f32[128,4]{0,1:T(4,128)} %param.12) | copy-start | bytes 6148
  1.7 16.5 %collective-permute-start.1 = (bf16[128,1024]{1,0:T(8,128)(2,1)S(1)}, bf16[128,1024]{1,0:T(8,128)(2,1)S(1)}, u32[]{:S(2)}, u32[]{:S(2)}) collective-permute-start(bf16[128,1024]{1,0:T(8,128)(2,1)S(1)} %shard_map.120.x_ref), channel_id=1, source_target_pairs={{0,16},{2,18},{4,20},{6,22},{8,24},{10,26},{12,28},{14,30},{16,0},... | collective-permute-start | bytes 786440 | tf_op jit(solution)/shard_map/ppermute | solution.py:300
  6.3 11.8 %collective-permute-start = (f32[16,128]{1,0:T(8,128)S(1)}, f32[16,128]{1,0:T(8,128)S(1)}, u32[]{:S(2)}, u32[]{:S(2)}) collective-permute-start(f32[16,128]{1,0:T(8,128)S(1)} %shard_map.121.info_ref), channel_id=1, source_target_pairs={{0,16},{2,18},{4,20},{6,22},{8,24},{10,26},{12,28},{14,30},{16,0},... | collective-permute-start | bytes 24584 | tf_op jit(solution)/shard_map/ppermute | solution.py:300
  7.7 19.6 %all-to-all-start = ((bf16[8,40,1024]{2,1,0:T(8,128)(2,1)}), bf16[8,40,1024]{2,1,0:T(8,128)(2,1)}, u32[]{:S(2)}, u32[]{:S(2)}) async-start(bf16[8,40,1024]{2,1,0:T(8,128)(2,1)} %bitcast.8), calls=%async_computation | async-start | bytes 1310720 | tf_op jit(solution)/shard_map/all_to_all | solution.py:304
  19.4 14.0 %collective-permute-start.2 = (bf16[128,1024]{1,0:T(8,128)(2,1)S(1)}, bf16[128,1024]{1,0:T(8,128)(2,1)S(1)}, u32[]{:S(2)}, u32[]{:S(2)}) collective-permute-start(bf16[128,1024]{1,0:T(8,128)(2,1)S(1)} %shard_map.123.x_ref), channel_id=1, source_target_pairs={{0,16},{2,18},{4,20},{6,22},{8,24},{10,26},{12,28},{14,30},{16,0},... | collective-permute-start | bytes 786440 | tf_op jit(solution)/shard_map/ppermute | solution.py:300
  27.4 14.2 %all-to-all-start.1 = ((bf16[8,40,1024]{2,1,0:T(8,128)(2,1)}), bf16[8,40,1024]{2,1,0:T(8,128)(2,1)S(1)}, u32[]{:S(2)}, u32[]{:S(2)}) async-start(bf16[8,40,1024]{2,1,0:T(8,128)(2,1)} %bitcast.10), calls=%async_computation.1 | async-start | bytes 1310720 | tf_op jit(solution)/shard_map/all_to_all | solution.py:304
  35.3 9.8 %collective-permute-start.3 = (bf16[320,1024]{1,0:T(8,128)(2,1)}, bf16[320,1024]{1,0:T(8,128)(2,1)S(1)}, u32[]{:S(2)}, u32[]{:S(2)}) collective-permute-start(bf16[320,1024]{1,0:T(8,128)(2,1)} %bitcast.9.refs_0_.refs_2_), channel_id=1, source_target_pairs={{0,1},{1,0},{2,3},{3,2},{4,5},{5,4},{6,7},{7,6},{8,9},{9,8},{10,11... | collective-permute-start | bytes 1966088 | tf_op jit(solution)/shard_map/ppermute | solution.py:309
  41.5 5.8 %copy-start.6 = (bf16[8,40,1024]{2,1,0:T(8,128)(2,1)}, bf16[8,40,1024]{2,1,0:T(8,128)(2,1)S(1)}, u32[]{:S(2)}) copy-start(bf16[8,40,1024]{2,1,0:T(8,128)(2,1)S(1)} %all-to-all-done.1) | copy-start | bytes 1966084
  41.5 21.7 %all-to-all-start.2 = ((bf16[8,40,2176]{2,1,0:T(8,128)(2,1)}), bf16[8,40,2176]{2,1,0:T(8,128)(2,1)S(1)}, u32[]{:S(2)}, u32[]{:S(2)}) async-start(bf16[8,40,2176]{2,1,0:T(8,128)(2,1)} %bitcast.12), calls=%async_computation.2 | async-start | bytes 2785280 | tf_op jit(solution)/shard_map/all_to_all | solution.py:304
  45.1 2.2 %copy-start.7 = (bf16[320,1024]{1,0:T(8,128)(2,1)}, bf16[320,1024]{1,0:T(8,128)(2,1)S(1)}, u32[]{:S(2)}) copy-start(bf16[320,1024]{1,0:T(8,128)(2,1)S(1)} %collective-permute-done.3.refs_1_.refs_3_) | copy-start | bytes 1966084
  45.1 2.2 %collective-permute-start.4 = (bf16[320,1024]{1,0:T(8,128)(2,1)S(1)}, bf16[320,1024]{1,0:T(8,128)(2,1)S(1)}, u32[]{:S(2)}, u32[]{:S(2)}) collective-permute-start(bf16[320,1024]{1,0:T(8,128)(2,1)S(1)} %bitcast.32), channel_id=1, source_target_pairs={{0,1},{1,0},{2,3},{3,2},{4,5},{5,4},{6,7},{7,6},{8,9},{9,8},{10,11... | collective-permute-start | bytes 1966088 | tf_op jit(solution)/shard_map/ppermute | solution.py:309
  47.3 0.9 copy-start.8
  56.8 2.2 %collective-permute-start.5 = (bf16[320,1024]{1,0:T(8,128)(2,1)S(1)}, bf16[320,1024]{1,0:T(8,128)(2,1)S(1)}, u32[]{:S(2)}, u32[]{:S(2)}) collective-permute-start(bf16[320,1024]{1,0:T(8,128)(2,1)S(1)} %get-tuple-element.40), channel_id=1, source_target_pairs={{0,1},{1,0},{2,3},{3,2},{4,5},{5,4},{6,7},{7,6},{8,9},{9,8},{10,11... | collective-permute-start | bytes 1966088 | tf_op jit(solution)/shard_map/ppermute | solution.py:309
  63.2 4.3 %copy-start.5 = (bf16[8,40,2176]{2,1,0:T(8,128)(2,1)}, bf16[8,40,2176]{2,1,0:T(8,128)(2,1)S(1)}, u32[]{:S(2)}) copy-start(bf16[8,40,2176]{2,1,0:T(8,128)(2,1)S(1)} %all-to-all-done.2) | copy-start | bytes 4177924
  63.2 20.3 %collective-permute-start.6 = (bf16[320,2176]{1,0:T(8,128)(2,1)S(1)}, bf16[320,2176]{1,0:T(8,128)(2,1)}, u32[]{:S(2)}, u32[]{:S(2)}) collective-permute-start(bf16[320,2176]{1,0:T(8,128)(2,1)S(1)} %bitcast.29), channel_id=1, source_target_pairs={{0,1},{1,0},{2,3},{3,2},{4,5},{5,4},{6,7},{7,6},{8,9},{9,8},{10,11... | collective-permute-start | bytes 4177928 | tf_op jit(solution)/shard_map/ppermute | solution.py:309
  63.2 14.7 %all-to-all-start.3 = ((bf16[8,40,1024]{2,1,0:T(8,128)(2,1)}), bf16[8,40,1024]{2,1,0:T(8,128)(2,1)S(1)}, u32[]{:S(2)}, u32[]{:S(2)}) async-start(bf16[8,40,1024]{2,1,0:T(8,128)(2,1)} %bitcast.17), calls=%async_computation.3 | async-start | bytes 1310720 | tf_op jit(solution)/shard_map/all_to_all | solution.py:304
  66.7 2.5 %copy-start.4 = (bf16[320,1024]{1,0:T(8,128)(2,1)S(1)}, bf16[320,1024]{1,0:T(8,128)(2,1)}, u32[]{:S(2)}) copy-start(bf16[320,1024]{1,0:T(8,128)(2,1)} %get-tuple-element.51.a_ref) | copy-start | bytes 1966084
  66.8 2.5 %collective-permute-start.7 = (bf16[320,1024]{1,0:T(8,128)(2,1)}, bf16[320,1024]{1,0:T(8,128)(2,1)S(1)}, u32[]{:S(2)}, u32[]{:S(2)}) collective-permute-start(bf16[320,1024]{1,0:T(8,128)(2,1)} %get-tuple-element.52), channel_id=1, source_target_pairs={{0,1},{1,0},{2,3},{3,2},{4,5},{5,4},{6,7},{7,6},{8,9},{9,8},{10,11... | collective-permute-start | bytes 1966088 | tf_op jit(solution)/shard_map/ppermute | solution.py:309
  78.0 19.1 %all-to-all-start.4 = ((bf16[8,40,1024]{2,1,0:T(8,128)(2,1)}), bf16[8,40,1024]{2,1,0:T(8,128)(2,1)S(1)}, u32[]{:S(2)}, u32[]{:S(2)}) async-start(bf16[8,40,1024]{2,1,0:T(8,128)(2,1)} %bitcast.19), calls=%async_computation.4 | async-start | bytes 1310720 | tf_op jit(solution)/shard_map/all_to_all | solution.py:304
  82.1 12.4 %collective-permute-start.8 = (bf16[128,1024]{1,0:T(8,128)(2,1)S(1)}, bf16[128,1024]{1,0:T(8,128)(2,1)S(1)}, u32[]{:S(2)}, u32[]{:S(2)}) collective-permute-start(bf16[128,1024]{1,0:T(8,128)(2,1)S(1)} %shard_map.129), channel_id=1, source_target_pairs={{0,16},{2,18},{4,20},{6,22},{8,24},{10,26},{12,28},{14,30},{16,0},... | collective-permute-start | bytes 786440 | tf_op jit(solution)/shard_map/ppermute | solution.py:300
